TPU v7x, 32 devices: a whole 2x2x4 slice. The times are simulated.
32 devices in a mesh: genome: 8 (over y, x, core), offset: 4 (over z).
Axes of the slice: x: 2, y: 2, z: 4, core: 2. Of those that a mesh axis runs over, the one named last changes fastest.
Arguments:
- contacts: bfloat16 [5120, 5120], P('offset', 'genome'), as said below
- masked_bins: int32 [128], replicated, may hold values from 0 to 5119
- chrom_bounds: int32 [2], replicated, may hold values from 1 to 5119
Outputs:
- peak_score: float32 [5120, 5120], P('offset', 'genome')
- bias: float32 [5120], P('genome')
Inputs may be any that keep to these rules, and one draw needn't show every extreme that they name: `contacts`: every entry is positive.
All inputs are finite; a program needn't handle non-finite values.
Results may differ from a plain program's by a relative error of at most 0.0003.
Values sent between devices are 32-bit elements; how exact they have to be, the bound alone decides.
No kernel may reach another device: no remote copies, remote signals or barrier semaphores. Data moves between devices by JAX's collectives and lax.ppermute only.
A program may use at most 128 MiB of HBM per device.

v0:
```python
import jax
import jax.numpy as jnp
from jax import lax
from jax.sharding import PartitionSpec as P

P1 = 2
P2 = 5
SWEEPS = 2


def extended(value, sides, width):
    for axis, dim in sides:
        size, length = (lax.axis_size(axis), value.shape[dim])
        up = [(i, (i + 1) % size) for i in range(size - 1)]
        down = [(j, i) for i, j in up]
        last = lax.slice_in_dim(value, length - width, length, axis=dim)
        leading = lax.slice_in_dim(value, 0, width, axis=dim)
        before = lax.ppermute(last, axis, up)
        after = lax.ppermute(leading, axis, down)
        value = jnp.concatenate([before, value, after], axis=dim)
    return value


def skew_window(window, row_count, col_count):
    length = window.shape[0]
    tiled_window = jnp.tile(window, row_count + 1)
    sheared = tiled_window[: row_count * (length + 1)].reshape(row_count, length + 1)
    return sheared[:, :col_count]


def antidiagonal_sums(matrix):
    row_count, col_count = matrix.shape
    length = row_count + col_count
    padded = jnp.pad(matrix, ((0, 0), (0, length + 1 - col_count)))
    sheared = padded.reshape(-1)[: row_count * length].reshape(row_count, length)
    return jnp.sum(sheared, axis=0)


def filter_sums(padded, halo_width, inner_width, outer_width, row_count, col_count):
    running = jnp.cumsum(padded, axis=0)
    prefix = jnp.concatenate([jnp.zeros((1, padded.shape[1]), jnp.float32), running], axis=0)
    cache = {}

    def range_sum(row_shift, low, high):
        name_key = (row_shift, low, high)
        if name_key not in cache:
            columns = prefix[:, halo_width + row_shift : halo_width + row_shift + col_count]
            upper = halo_width + high - row_shift + 1
            lower = halo_width + low - row_shift
            cache[name_key] = (
                columns[upper : upper + row_count] - columns[lower : lower + row_count]
            )
        return cache[name_key]

    far_low, far_high = (inner_width + 1, outer_width)
    donut_total = None
    lower_total = None
    horizontal_total = None
    vertical_total = None
    for row_shift in range(-outer_width, outer_width + 1):
        if abs(row_shift) > inner_width:
            term = range_sum(row_shift, -outer_width, -1) + range_sum(row_shift, 1, outer_width)
            column_term = range_sum(row_shift, -1, 1)
            vertical_total = column_term if vertical_total is None else vertical_total + column_term
        elif row_shift != 0:
            term = range_sum(row_shift, -far_high, -far_low) + range_sum(
                row_shift, far_low, far_high
            )
        else:
            term = None
        if term is not None:
            donut_total = term if donut_total is None else donut_total + term
        if row_shift >= 1:
            if row_shift > inner_width:
                lower_term = range_sum(row_shift, -outer_width, -1)
            else:
                lower_term = range_sum(row_shift, -far_high, -far_low)
            lower_total = lower_term if lower_total is None else lower_total + lower_term
        if abs(row_shift) <= 1:
            side_term = range_sum(row_shift, -far_high, -far_low) + range_sum(
                row_shift, far_low, far_high
            )
            horizontal_total = (
                side_term if horizontal_total is None else horizontal_total + side_term
            )
    return [donut_total, lower_total, horizontal_total, vertical_total]


def on_device(contacts, masked_bins, chrom_bounds):
    diag_dev, bin_dev = contacts.shape
    genome_count = lax.axis_size("genome")
    offset_count = lax.axis_size("offset")
    total_bins = bin_dev * genome_count
    band_width = diag_dev * offset_count
    halo_width = 2 * P2
    left_pad = 2 * halo_width
    right_pad = band_width + bin_dev + 2 * halo_width
    bin_start = lax.axis_index("genome") * bin_dev
    diag_start = lax.axis_index("offset") * diag_dev
    keep_full = jnp.ones((total_bins,), jnp.float32).at[masked_bins].set(0.0)
    bin_line = jnp.arange(total_bins, dtype=jnp.int32)
    chrom_full = jnp.sum((bin_line[:, None] >= chrom_bounds[None, :]).astype(jnp.int32), axis=1)
    keep_pad = jnp.concatenate(
        [jnp.zeros((left_pad,), jnp.float32), keep_full, jnp.zeros((right_pad,), jnp.float32)]
    )
    chrom_pad = jnp.concatenate(
        [jnp.full((left_pad,), -1, jnp.int32), chrom_full, jnp.full((right_pad,), -1, jnp.int32)]
    )
    keep_rows = lax.dynamic_slice_in_dim(keep_pad, bin_start + left_pad, bin_dev)
    chrom_rows = lax.dynamic_slice_in_dim(chrom_pad, bin_start + left_pad, bin_dev)
    partner_start = bin_start + diag_start + left_pad
    keep_partner = skew_window(
        lax.dynamic_slice_in_dim(keep_pad, partner_start, diag_dev + bin_dev), diag_dev, bin_dev
    )
    chrom_partner = skew_window(
        lax.dynamic_slice_in_dim(chrom_pad, partner_start, diag_dev + bin_dev), diag_dev, bin_dev
    )
    diag_index = diag_start + jnp.arange(diag_dev, dtype=jnp.int32)
    in_band = ((diag_index >= 0) & (diag_index < band_width)).astype(jnp.float32)
    same_chrom = (chrom_rows[None, :] == chrom_partner).astype(jnp.float32)
    valid_mask = keep_rows[None, :] * keep_partner * same_chrom * in_band[:, None]
    weighted = contacts.astype(jnp.float32) * valid_mask
    diag_index = diag_start + jnp.arange(diag_dev, dtype=jnp.int32)
    off_main = (diag_index >= 1).astype(jnp.float32)
    keep_rows = lax.dynamic_slice_in_dim(keep_full, bin_start, bin_dev)
    kept_count = jnp.sum(keep_full)

    def balance(bias_full):
        bias_pad = jnp.concatenate(
            [jnp.zeros((left_pad,), jnp.float32), bias_full, jnp.zeros((right_pad,), jnp.float32)]
        )
        bias_rows = lax.dynamic_slice_in_dim(bias_full, bin_start, bin_dev)
        partner_window = lax.dynamic_slice_in_dim(
            bias_pad, bin_start + diag_start + left_pad, diag_dev + bin_dev
        )
        bias_partner = skew_window(partner_window, diag_dev, bin_dev)
        return weighted * bias_rows[None, :] * bias_partner

    bias_full = keep_full
    for sweep_index in range(SWEEPS):
        balanced = balance(bias_full)
        own_sums = jnp.sum(balanced, axis=0)
        partner_sums = antidiagonal_sums(balanced * off_main[:, None])
        placed = jnp.zeros((total_bins + band_width + bin_dev,), jnp.float32)
        placed = lax.dynamic_update_slice_in_dim(placed, partner_sums, bin_start + diag_start, 0)
        placed = placed + lax.dynamic_update_slice_in_dim(
            jnp.zeros_like(placed), own_sums, bin_start, 0
        )
        contrib = placed[:total_bins]
        row_sums = lax.psum(contrib, ("genome", "offset"))
        level = jnp.sum(row_sums * keep_full) / kept_count
        safe_sums = jnp.where(keep_full > 0, row_sums, 1.0)
        bias_full = jnp.where(keep_full > 0, bias_full * level / safe_sums, 0.0)
    balanced = balance(bias_full)
    diag_sums = jnp.sum(balanced, axis=1)
    diag_counts = jnp.sum(valid_mask, axis=1)
    diag_sums, diag_counts = lax.psum((diag_sums, diag_counts), "genome")
    expected = diag_sums / jnp.maximum(diag_counts, 1.0)
    local_expected = expected[:, None] * valid_mask
    stacked = jnp.stack([balanced, local_expected])
    padded = extended(stacked, (("genome", 2), ("offset", 1)), halo_width)
    observed_pad = padded[0]
    expected_pad = padded[1]
    center_expected = jnp.where(valid_mask > 0, expected[:, None], 1.0)
    observed_sets = filter_sums(observed_pad, halo_width, P1, P2, diag_dev, bin_dev)
    expected_sets = filter_sums(expected_pad, halo_width, P1, P2, diag_dev, bin_dev)
    score = None
    for observed_sum, expected_sum in zip(observed_sets, expected_sets):
        ratio = (
            balanced
            * (expected_sum + center_expected)
            / (center_expected * (observed_sum + center_expected))
        )
        score = ratio if score is None else jnp.minimum(score, ratio)
    peak_score = jnp.where(valid_mask > 0, score, 0.0)
    bias_rows = lax.dynamic_slice_in_dim(bias_full, bin_start, bin_dev)
    return (peak_score, bias_rows)


def solution(mesh):
    placed = (P("offset", "genome"), P(), P())
    return jax.shard_map(
        on_device,
        mesh=mesh,
        in_specs=placed,
        out_specs=(P("offset", "genome"), P("genome")),
        check_vma=False,
    )
```

profile of v0, /device:TPU:0, one launch (start us, length us, event | category | flops | bytes accessed | tf_op | source)
XLA Modules:
  0.0 744.5 jit_solution(4616025293160920762)
XLA Ops:
  3.6 4.4 tile.18
  8.1 11.0 %tile.19 = f32[2459520]{0:T(1024)} reshape(f32[1281,1920]{1,0:T(8,128)} %tile.18) | data formatting | bytes 19676160 | tf_op jit(solution)/shard_map/tile | solution.py:26
  19.1 17.4 %reshape.73 = f32[1280,1921]{1,0:T(8,128)} reshape(f32[2458880]{0:T(1024)} %bitcast.35) | data formatting | bytes 19671040 | tf_op jit(solution)/shard_map/reshape | solution.py:27
  36.5 4.4 tile.16
  40.9 11.1 %tile.17 = s32[2459520]{0:T(1024)} reshape(s32[1281,1920]{1,0:T(8,128)} %tile.16) | data formatting | bytes 19676160 | tf_op jit(solution)/shard_map/tile | solution.py:26
  51.9 17.7 %reshape.72 = s32[1280,1921]{1,0:T(8,128)} reshape(s32[2458880]{0:T(1024)} %bitcast.36) | data formatting | bytes 19671040 | tf_op jit(solution)/shard_map/reshape | solution.py:27
  69.7 4.2 fusion.72
  73.9 2.6 broadcast_multiply_fusion.1
  76.6 5.4 pad.15
  81.9 16.9 %reshape.74 = f32[2458880]{0:T(1024)} reshape(f32[1280,1921]{1,0:T(8,128)} %pad.15) | data formatting | bytes 19671040 | tf_op jit(solution)/shard_map/reshape | solution.py:35
  98.8 8.5 %slice.938 = f32[2457600]{0:T(1024)} slice(f32[2458880]{0:T(1024)} %reshape.74), slice={[0:2457600]} | slice | bytes 19660800 | tf_op jit(solution)/shard_map/slice | solution.py:35
  107.3 11.4 %reshape.75 = f32[1280,1920]{1,0:T(8,128)} reshape(f32[2457600]{0:T(1024)} %slice.938) | data formatting | bytes 19660800 | tf_op jit(solution)/shard_map/reshape | solution.py:35
  118.8 4.3 reduce_sum.91
  123.6 42.3 %psum.28 = f32[5120]{0:T(1024)S(1)} all-reduce(f32[5120]{0:T(1024)S(1)} %slice.939), channel_id=1, replica_groups=mesh['genome'=8,'offset'=4] {'genome','offset'}, use_global_device_ids=true, to_apply=%region_4.5 | all-reduce | flops 5120 | bytes 40960 | tf_op jit(solution)/shard_map/psum | solution.py:150
  168.2 4.4 tile.20
  172.6 11.0 %tile.21 = f32[2459520]{0:T(1024)} reshape(f32[1281,1920]{1,0:T(8,128)} %tile.20) | data formatting | bytes 19676160 | tf_op jit(solution)/shard_map/tile | solution.py:26
  183.6 17.4 %reshape.76 = f32[1280,1921]{1,0:T(8,128)} reshape(f32[2458880]{0:T(1024)} %bitcast.37) | data formatting | bytes 19671040 | tf_op jit(solution)/shard_map/reshape | solution.py:27
  201.0 3.3 fusion.83
  204.3 5.4 pad.16
  209.7 16.6 %reshape.77 = f32[2458880]{0:T(1024)} reshape(f32[1280,1921]{1,0:T(8,128)} %pad.16) | data formatting | bytes 19671040 | tf_op jit(solution)/shard_map/reshape | solution.py:35
  226.2 8.5 %slice.942 = f32[2457600]{0:T(1024)} slice(f32[2458880]{0:T(1024)} %reshape.77), slice={[0:2457600]} | slice | bytes 19660800 | tf_op jit(solution)/shard_map/slice | solution.py:35
  234.8 11.4 %reshape.78 = f32[1280,1920]{1,0:T(8,128)} reshape(f32[2457600]{0:T(1024)} %slice.942) | data formatting | bytes 19660800 | tf_op jit(solution)/shard_map/reshape | solution.py:35
  246.2 4.3 reduce_sum.95
  251.1 40.7 %psum.29 = f32[5120]{0:T(1024)S(1)} all-reduce(f32[5120]{0:T(1024)S(1)} %slice.943), channel_id=1, replica_groups=mesh['genome'=8,'offset'=4] {'genome','offset'}, use_global_device_ids=true, to_apply=%region_9.10 | all-reduce | flops 5120 | bytes 40960 | tf_op jit(solution)/shard_map/psum | solution.py:150
  294.0 4.4 tile.22
  298.4 11.0 %tile.23 = f32[2459520]{0:T(1024)} reshape(f32[1281,1920]{1,0:T(8,128)} %tile.22) | data formatting | bytes 19676160 | tf_op jit(solution)/shard_map/tile | solution.py:26
  309.5 17.4 %reshape.79 = f32[1280,1921]{1,0:T(8,128)} reshape(f32[2458880]{0:T(1024)} %bitcast.38) | data formatting | bytes 19671040 | tf_op jit(solution)/shard_map/reshape | solution.py:27
  326.9 4.7 fusion.85
  331.5 23.1 %all-reduce.6 = (f32[1280]{0:T(1024)S(1)}, f32[1280]{0:T(1024)S(1)}) all-reduce(f32[1280]{0:T(1024)S(1)} %get-tuple-element.8, f32[1280]{0:T(1024)S(1)} %get-tuple-element.2), channel_id=1, replica_groups=mesh['genome'=8,'offset'=4] {'genome'}, use_global_device_ids=true, to_apply=%region_12.13 | all-reduce | flops 2560 | bytes 20480 | tf_op jit(solution)/shard_map/psum | solution.py:157
  355.0 2.8 copy-done.2
  362.7 2.4 copy.20
  368.6 2.4 copy.22
  371.0 6.1 pad_maximum_fusion
  377.2 3.1 copy-done.3
  380.4 2.4 collective-permute-start.2
  385.0 4.3 collective-permute-done.3
  389.3 23.8 %concatenate.30 = f32[2,1300,660]{2,1,0:T(8,128)} concatenate(f32[2,10,660]{2,1,0:T(8,128)S(1)} %collective-permute-done.2, f32[2,1280,660]{2,1,0:T(8,128)} %copy-done.3, f32[2,10,660]{2,1,0:T(8,128)S(1)} %collective-permute-done.3), dimensions={1} | concatenate | bytes 13728000 | tf_op jit(solution)/shard_map/concatenate | solution.py:20
  413.1 5.8 slice_bitcast_fusion.1
  419.2 3.8 fusion.2
  423.0 2.7 copy-done.7
  425.7 3.4 broadcast_add_fusion.1
  429.1 2.5 copy.24
  431.6 2.3 slice.988
  437.0 3.8 fusion
  440.7 2.7 copy-done.6
  443.4 3.4 broadcast_add_fusion
  446.9 2.5 copy.26
  453.5 290.7 %fusion.11 = f32[1280,640]{1,0:T(8,128)} fusion(f32[1280,640]{1,0:T(8,128)} %get-tuple-element.9, f32[1408,660]{1,0:T(8,128)} %bitcast.32, f32[1408,660]{1,0:T(8,128)} %bitcast.30, f32[1300,660]{1,0:T(8,128)} %slice.1031, f32[1300,660]{1,0:T(8,128)} %slice.988, f32[1280,640]{1,0:T(8,128)S(1)} %get-tuple-element.11, f32[1280]{0:T(1024)S(1)} %maximum_divide_fusion), kind=kLoop, calls=%fused_computation.29 | loop fusion | flops 117964800 | bytes 377147520 | tf_op jit(solution)/shard_map/jit(_where)/select_n | solution.py:175
  (69 shorter events, 24.3 us)
Async XLA Ops:
  69.7 4.2 copy-start.5
  293.9 32.9 %copy-start.9 = (f32[640]{0:T(1024)}, f32[640]{0:T(1024)S(1)}, u32[]{:S(2)}) copy-start(f32[640]{0:T(1024)S(1)} %dynamic_slice.36) | copy-start | bytes 7684
  354.7 3.1 copy-start.2
  355.0 4.8 copy-start.4
  361.4 5.1 collective-permute-start
  365.1 3.5 collective-permute-start.1
  377.2 3.2 copy-start.3
  380.4 4.6 collective-permute-start.2
  382.8 6.5 collective-permute-start.3
  423.0 2.7 copy-start.7
  431.6 4.1 copy-start
  431.6 5.0 copy-start.8
  440.7 2.7 copy-start.6
  449.4 2.0 copy-start.1
where the time goes:
time: 758 us; the launch traced here: 744 us
  other arithmetic  340 us (45%)
  local copies, waits for them, and re-layouts  282 us (37%)
  blocking collectives  106 us (14%)
    select_n x1, other arithmetic, on_device(): peak_score = jnp.where(valid_mask > 0, score, 0.0)  291 us
    psum x2, blocking collectives, on_device(): row_sums = lax.psum(contrib, ('genome', 'offset'))  83.1 us
    reshape x4, local copies, waits for them, and re-layouts, skew_window(): tiled_window[:row_count * (length + 1)].reshape(row_count, length + 1)  69.9 us
    another operation x8, local copies, waits for them, and re-layouts, skew_window(): tiled_window = jnp.tile(window, row_count + 1)  61.8 us
    reshape x4, local copies, waits for them, and re-layouts, antidiagonal_sums(): sheared = padded.reshape(-1)[:row_count * length].reshape(row_count, length)  56.3 us
    concatenate x1, local copies, waits for them, and re-layouts, extended(): value = jnp.concatenate([before, value, after], axis=dim)  23.8 us
    psum x1, blocking collectives, on_device(): diag_sums, diag_counts = lax.psum((diag_sums, diag_counts), 'genome')  23.1 us
    slice x2, local copies, waits for them, and re-layouts, antidiagonal_sums(): sheared = padded.reshape(-1)[:row_count * length].reshape(row_count, length)  17.1 us
  transfers between devices with their start and end apart: 4, of which 3 were waited for; matrix products, arithmetic and copies ran while one was open for 1% of the time, Pallas kernels for 0%

commit v1 on v0

v1 whole, which is shorter than its diff:
```python
import functools

import jax
import jax.numpy as jnp
from jax import lax
from jax.experimental import pallas as pl
from jax.experimental.pallas import tpu as pltpu
from jax.sharding import PartitionSpec as P

RIM = 16
SIDE = 8
LANES = 128
F32 = jnp.float32
BF16 = jnp.bfloat16
TINY = 2.0**-126
VMEM = pl.BlockSpec(memory_space=pltpu.VMEM)
SMEM = pl.BlockSpec(memory_space=pltpu.SMEM)
NT = (((1,), (1,)), ((), ()))


def params(mib=48):
    return pltpu.CompilerParams(vmem_limit_bytes=mib << 20)


def iota(shape, dim):
    return lax.broadcasted_iota(jnp.int32, shape, dim)


def split3(x):
    hi = x.astype(BF16)
    rest = x - hi.astype(F32)
    mid = rest.astype(BF16)
    low = (rest - mid.astype(F32)).astype(BF16)
    return hi, mid, low


def place(nd, nb):
    first = lax.axis_index("genome") * nb
    partner = first + lax.axis_index("offset") * nd
    return first // LANES, partner // LANES, partner % LANES


def roll(x, shift):
    length = x.shape[1]
    if isinstance(shift, int):
        shift = shift % length
        if shift == 0:
            return x
    return pltpu.roll(x, shift, 1)


def hankel(rows_ref, row0, lane0, tiles, out_ref):
    extra = 1 if lane0 is None else 2
    base = jnp.concatenate(
        [jnp.broadcast_to(rows_ref[pl.ds(row0 + t, 1), :], (8, LANES)) for t in range(tiles + extra)],
        axis=1,
    )
    length = base.shape[1]
    if lane0 is not None:
        base = roll(base, length - lane0)
    sub = iota(base.shape, 0)
    for bit in (1, 2, 4):
        base = jnp.where((sub & bit) > 0, roll(base, length - bit), base)
    for r in range(16):
        out_ref[8 * r : 8 * r + 8, : tiles * LANES] = roll(base, length - 8 * r)[:, : tiles * LANES]


def antidiagonal(acc_ref, tiles, lane0):
    extra = 1 if lane0 is None else 2
    pad = jnp.zeros((8, extra * LANES), F32)
    total = None
    for r in range(15, -1, -1):
        part = jnp.concatenate([acc_ref[8 * r : 8 * r + 8, : tiles * LANES], pad], axis=1)
        total = part if total is None else roll(total, 8) + part
    sub = iota(total.shape, 0)
    for bit in (4, 2, 1):
        total = jnp.where((sub & bit) > 0, roll(total, bit), total)
    total = jnp.sum(total, axis=0, keepdims=True)
    if lane0 is not None:
        total = roll(total, lane0)
    return total


def spread(own, partner, row_own, row_partner, placed_ref, out_ref):
    placed_ref[...] = jnp.zeros_like(placed_ref)
    for t in range(partner.shape[1] // LANES):
        placed_ref[pl.ds(row_partner + t, 1), :] = partner[:, t * LANES : (t + 1) * LANES]
    for c in range(own.shape[1] // LANES):
        placed_ref[pl.ds(row_own + c, 1), :] += own[:, c * LANES : (c + 1) * LANES]
    out_ref[...] = placed_ref[: out_ref.shape[0], :]


def sweep(nd, nb, entry, weigh_own, weigh_partner, acc_ref):
    cols = nb // LANES
    full, rest = nd // LANES, nd % LANES
    first_diag = lax.axis_index("offset") * nd
    sub = iota((16, LANES), 0)

    def body(ms, fresh, r, own):
        own = list(own)
        q0 = pl.multiple_of(16 * r, 16)
        sums = {}
        for m in ms:
            for c in range(cols):
                w = entry(m, c, q0)
                own[c] = own[c] + weigh_own(w, m, c, q0)
                g = weigh_partner(w, c)
                if m == 0:
                    g = jnp.where(sub + q0 + first_diag > 0, g, 0.0)
                sums[m + c] = sums[m + c] + g if m + c in sums else g
        for t, value in sums.items():
            tile = (pl.ds(q0, 16), slice(t * LANES, (t + 1) * LANES))
            acc_ref[tile] = value if fresh else acc_ref[tile] + value
        return tuple(own)

    own = tuple(jnp.zeros((16, LANES), F32) for _ in range(cols))
    if rest:
        acc_ref[...] = jnp.zeros_like(acc_ref)
    own = lax.fori_loop(0, 8, functools.partial(body, range(full), not rest), own)
    if rest:
        own = lax.fori_loop(0, rest // 16, functools.partial(body, [full], False), own)
    return jnp.concatenate([jnp.sum(o, axis=0, keepdims=True) for o in own], axis=1)


def keep_of(masked, rows):
    count = masked.shape[1]
    in_row = (jnp.broadcast_to(masked >> 7, (rows, count)) == iota((rows, count), 0))
    in_lane = (jnp.broadcast_to(masked & 127, (LANES, count)) == iota((LANES, count), 0))
    hits = lax.dot_general(
        in_row.astype(F32).astype(BF16), in_lane.astype(F32).astype(BF16), NT, preferred_element_type=F32
    )
    return jnp.where(hits > 0.0, 0.0, 1.0)


def first_kernel(nd, nb, bounds_ref, x_ref, masked_ref, w_ref, part_ref, keep_ref, top_ref, bottom_ref,
                 codes_ref, hank_ref, acc_ref, placed_ref):
    rows = keep_ref.shape[0]
    cols = nb // LANES
    span = -(-nd // LANES) + cols - 1
    row_own, row_partner, lane0 = place(nd, nb)
    lane0 = lane0 if nd % LANES else None
    keep = keep_of(masked_ref[...], rows)
    keep_ref[...] = keep
    bins = iota((rows, LANES), 0) * LANES + iota((rows, LANES), 1)
    chrom = jnp.zeros((rows, LANES), F32)
    for k in range(bounds_ref.shape[0]):
        chrom = chrom + jnp.where(bins >= bounds_ref[k], 1.0, 0.0)
    codes_ref[...] = jnp.full_like(codes_ref, -2.0)
    codes_ref[:rows, :] = jnp.where(keep > 0.0, chrom, -2.0)
    hankel(codes_ref, row_partner, lane0, span, hank_ref)
    code_own = []
    for c in range(cols):
        code = codes_ref[pl.ds(row_own + c, 1), :]
        code = jnp.where(code < 0.0, -1.0, code)
        code_own.append(jnp.broadcast_to(code, (16, LANES)))

    def entry(m, c, q0):
        here = (pl.ds(q0 + m * LANES, 16), slice(c * LANES, (c + 1) * LANES))
        code = hank_ref[pl.ds(q0, 16), (m + c) * LANES : (m + c + 1) * LANES]
        value = jnp.maximum(x_ref[here].astype(F32), TINY)
        w = jnp.where(code == code_own[c], value, 0.0)
        w_ref[here] = w.astype(BF16)
        return w

    own = sweep(nd, nb, entry, lambda w, m, c, q0: w, lambda w, c: w, acc_ref)
    spread(own, antidiagonal(acc_ref, span, lane0), row_own, row_partner, placed_ref, part_ref)
    top_ref[...] = w_ref[:RIM, :].astype(F32)
    bottom_ref[...] = w_ref[nd - RIM :, :].astype(F32)


def next_bias(keep, bias, sums):
    level = jnp.sum(sums * keep, keepdims=True) / jnp.sum(keep, keepdims=True)
    safe = jnp.where(keep > 0.0, sums, 1.0)
    return jnp.where(keep > 0.0, bias * level / safe, 0.0)


def second_kernel(nd, nb, w_ref, sums_ref, keep_ref, part_ref, bias_ref, window_ref, hank_ref, acc_ref, placed_ref):
    rows = keep_ref.shape[0]
    cols = nb // LANES
    span = -(-nd // LANES) + cols - 1
    row_own, row_partner, lane0 = place(nd, nb)
    lane0 = lane0 if nd % LANES else None
    bias = next_bias(keep_ref[...], keep_ref[...], sums_ref[...])
    bias_ref[...] = bias
    window_ref[...] = jnp.zeros_like(window_ref)
    window_ref[:rows, :] = bias
    hankel(window_ref, row_partner, lane0, span, hank_ref)
    rows_own = [window_ref[pl.ds(row_own + c, 1), :] for c in range(cols)]
    own_bias = [jnp.broadcast_to(b, (16, LANES)) for b in rows_own]

    def entry(m, c, q0):
        return w_ref[pl.ds(q0 + m * LANES, 16), c * LANES : (c + 1) * LANES].astype(F32)

    def weigh_own(w, m, c, q0):
        return w * hank_ref[pl.ds(q0, 16), (m + c) * LANES : (m + c + 1) * LANES]

    own = sweep(nd, nb, entry, weigh_own, lambda w, c: w * own_bias[c], acc_ref)
    own = own * jnp.concatenate(rows_own, axis=1)
    partner = antidiagonal(acc_ref, span, lane0)
    tiles = partner.shape[1] // LANES
    partner = partner * jnp.concatenate(
        [window_ref[pl.ds(row_partner + t, 1), :] for t in range(tiles)], axis=1
    )
    spread(own, partner, row_own, row_partner, placed_ref, part_ref)


def side_kernel(nd, nb, w_ref, top_ref, bottom_ref, left_ref, right_ref):
    row, lane = iota((SIDE, LANES), 0), iota((SIDE, LANES), 1)
    for out_ref, pick, first in (
        (left_ref, row == lane, 0),
        (right_ref, row + LANES - SIDE == lane, nb - LANES),
    ):
        pick = pick.astype(F32).astype(BF16)
        cols = slice(first, first + LANES)
        block = jnp.concatenate(
            [w_ref[:, cols], bottom_ref[:, cols].astype(BF16), top_ref[:, cols].astype(BF16)], axis=0
        )
        out_ref[...] = lax.dot_general(pick, block, NT, preferred_element_type=F32)


def strip_kernel(nd, nb, first, count, w_ref, top_ref, bottom_ref, left_ref, right_ref, out_ref, perm_ref, side_ref):
    stride = nb // LANES
    width = count * LANES
    lane = iota((nb, LANES), 1)
    row = iota((nb, LANES), 0)
    for k in range(count):
        hit = row == lane * stride + (first + k)
        perm_ref[:, k * LANES : (k + 1) * LANES] = hit.astype(F32).astype(BF16)
    perm = perm_ref[...]
    rims = []
    row, lane = iota((2 * SIDE, LANES), 0), iota((2 * SIDE, LANES), 1)
    bin_of = jnp.where(row < SIDE, row - SIDE, row - SIDE + nb)
    for k in range(count):
        rims.append((bin_of == lane * stride + (first + k)).astype(F32).astype(BF16))
    rims = jnp.concatenate(rims, axis=1)
    sides = jnp.concatenate([left_ref[...], right_ref[...]], axis=0).astype(BF16)
    outer = first < 0 or first + count > stride
    if outer:
        side_ref[...] = lax.dot_general(
            sides, rims, (((0,), (0,)), ((), ())), preferred_element_type=F32
        )

    def emit(block, at, side_at, rows):
        value = jnp.dot(block, perm, preferred_element_type=F32)
        if outer:
            value = value + side_ref[pl.ds(side_at, rows), :]
        for k in range(count):
            out_ref[k, pl.ds(at, rows), :] = value[:, k * LANES : (k + 1) * LANES].astype(BF16)

    emit(top_ref[...].astype(BF16), 0, nd + RIM, RIM)
    emit(bottom_ref[...].astype(BF16), nd + RIM, nd, RIM)
    step = 64

    def body(i, _):
        r0 = pl.multiple_of(i * step, step)
        emit(w_ref[pl.ds(r0, step), :], r0 + RIM, r0, step)
        return 0

    lax.fori_loop(0, nd // step, body, 0)


def column(row, out_ref, at):
    eye = iota((LANES, LANES), 0) == iota((LANES, LANES), 1)
    diag = jnp.where(eye, jnp.broadcast_to(row, (LANES, LANES)), 0.0)
    value = jnp.dot(
        jnp.concatenate(split3(diag), axis=1), jnp.ones((3 * LANES, LANES), BF16), preferred_element_type=F32
    )
    out_ref[at : at + LANES, :] = value


def fan(col_ref, other_ref, start, rows, stride, out_ref):
    lane = {}
    source, offset = col_ref, start
    target = other_ref
    for bit in (64, 32, 16, 8, 4, 2, 1):
        need = rows + stride * (bit - 1)
        need = -(-need // 8) * 8
        if bit == 1:
            target = out_ref
        step = 32 if need >= 32 else 8

        def move(at, size, source=source, target=target, offset=offset, bit=bit):
            low = source[pl.ds(offset + at, size), :]
            high = source[pl.ds(offset + at + stride * bit, size), :]
            odd = (iota((size, LANES), 1) & bit) > 0
            target[pl.ds(at, size), :] = jnp.where(odd, high, low)

        def body(i, _, move=move):
            move(pl.multiple_of(i * 32, 32), 32)
            return 0

        lax.fori_loop(0, need // 32, body, 0)
        for at in range(need // 32 * 32, need, 8):
            move(at, 8)
        source, target, offset = target, source, 0


def fan_rows(nd):
    return nd + 2 * RIM + 32


def third_kernel(nd, nb, mid_ref, sums_ref, keep_ref, bias_ref, own_ref, fan_ref, near_ref, diag_ref,
                 window_ref, col_ref, other_ref, ncol_ref, nother_ref, total_ref):
    rows = keep_ref.shape[0]
    cols = nb // LANES
    stride = cols
    row_own, row_partner, lane0 = place(nd, nb)
    bias = next_bias(keep_ref[...], bias_ref[...], sums_ref[...])
    window_ref[...] = jnp.zeros_like(window_ref)
    window_ref[8 : 8 + rows, :] = bias
    for c in range(cols):
        own_ref[c : c + 1, :] = window_ref[pl.ds(8 + row_own + c, 1), :]
    tiles = col_ref.shape[0] // LANES
    for t in range(tiles):
        column(window_ref[pl.ds(7 + row_partner + t, 1), :], col_ref, t * LANES)
    start = LANES - RIM - 8
    if nd % LANES:
        start = start + lane0
    fan(col_ref, other_ref, start, fan_rows(nd), stride, fan_ref)
    for t in range(ncol_ref.shape[0] // LANES):
        column(window_ref[pl.ds(7 + row_own + t, 1), :], ncol_ref, t * LANES)
    fan(ncol_ref, nother_ref, LANES - 8, near_ref.shape[0], stride, near_ref)
    total_rows = nd + 2 * RIM
    step = 32

    def body(i, _):
        r0 = pl.multiple_of(i * step, step)
        total, count = None, None
        for s in range(stride):
            w = mid_ref[s, pl.ds(r0, step), :].astype(F32)
            b = w * jnp.broadcast_to(near_ref[8 + s : 9 + s, :], (step, LANES)) * fan_ref[pl.ds(r0 + 8 + s, step), :]
            v = jnp.where(w > 0.0, 1.0, 0.0)
            total = b if total is None else total + b
            count = v if count is None else count + v
        hi, mid, low = split3(total)
        for k, part in enumerate((hi, mid, low, count.astype(BF16))):
            total_ref[pl.ds(r0, step), k * LANES : (k + 1) * LANES] = part
        return 0

    lax.fori_loop(0, total_rows // step, body, 0)
    ones = jnp.ones((8, 3 * LANES), BF16)
    padded = diag_ref.shape[1]
    if padded > total_rows:
        total_ref[total_rows:, :] = jnp.zeros((padded - total_rows, 4 * LANES), BF16)
    sums = lax.dot_general(ones, total_ref[:, : 3 * LANES], NT, preferred_element_type=F32)
    counts = lax.dot_general(ones[:, :LANES], total_ref[:, 3 * LANES :], NT, preferred_element_type=F32)
    diag_ref[...] = jnp.where(iota((8, padded), 0) == 0, sums, counts)


def windows(nd, stride, x_ref, tri_ref, u_ref, wd_ref, lp_ref):
    step = 32
    total_rows = nd + 2 * RIM

    def tri(i, _):
        r0 = pl.multiple_of(i * step + 8, 8)
        for s in range(-4, stride + 4):
            tri_ref[s + 4, pl.ds(r0, step), :] = (
                x_ref[s + 4, pl.ds(r0 + 1, step), :]
                + x_ref[s + 5, pl.ds(r0, step), :]
                + x_ref[s + 6, pl.ds(r0 - 1, step), :]
            )
        return 0

    lax.fori_loop(0, (total_rows - 32) // step, tri, 0)
    for r0, size in ((1, 7), (total_rows - 24, 23)):
        for s in range(-4, stride + 4):
            tri_ref[s + 4, r0 : r0 + size, :] = (
                x_ref[s + 4, r0 + 1 : r0 + 1 + size, :]
                + x_ref[s + 5, r0 : r0 + size, :]
                + x_ref[s + 6, r0 - 1 : r0 - 1 + size, :]
            )

    def mixed(r0, size):
        for s in range(stride):
            hp = tri_ref[s + 8, pl.ds(r0 - 4, size), :]
            hm = tri_ref[s, pl.ds(r0 + 4, size), :]
            ep = x_ref[s + 6, pl.ds(r0 - 1, size), :] + x_ref[s + 7, pl.ds(r0 - 2, size), :]
            em = x_ref[s + 4, pl.ds(r0 + 1, size), :] + x_ref[s + 3, pl.ds(r0 + 2, size), :]
            lp = hp + ep
            u_ref[s, pl.ds(r0, size), :] = hp + hm
            lp_ref[s, pl.ds(r0, size), :] = lp
            wd_ref[s, pl.ds(r0, size), :] = lp + (hm + em)

    def mixed_body(i, _):
        mixed(pl.multiple_of(i * step + RIM, 16), step)
        return 0

    lax.fori_loop(0, nd // step, mixed_body, 0)
    mixed(RIM - 8, 8)
    mixed(RIM + nd, 8)

    def runs(r0, size):
        for s in range(stride):
            wd_ref[s, pl.ds(r0, size), :] = (
                wd_ref[s, pl.ds(r0, size), :] + wd_ref[s, pl.ds(r0 + 1, size), :] + wd_ref[s, pl.ds(r0 + 2, size), :]
            )
            tri_ref[s, pl.ds(r0, size), :] = (
                tri_ref[s + 4, pl.ds(r0, size), :]
                + tri_ref[s + 4, pl.ds(r0 + 1, size), :]
                + tri_ref[s + 4, pl.ds(r0 + 2, size), :]
            )

    def runs_body(i, _):
        runs(pl.multiple_of(i * step + RIM, 16) - 5, step)
        return 0

    lax.fori_loop(0, nd // step, runs_body, 0)
    runs(RIM + nd - 5, 8)


def sums_at(s, r0, size, tri_ref, u_ref, wd_ref, lp_ref):
    at = lambda ref, k, shift: ref[k, pl.ds(r0 + shift, size), :]
    u = [at(u_ref, s, shift) for shift in (-2, -1, 0, 1, 2)]
    donut = at(wd_ref, s, -5) + at(wd_ref, s, 3) + (u[0] + u[1]) + (u[3] + u[4])
    vertical = u[1] + u[2] + u[3]
    horizontal = at(tri_ref, s, -5) + at(tri_ref, s, 3)
    lower = (at(lp_ref, s, -5) + at(lp_ref, s, -4) + at(lp_ref, s, -3)) + (
        at(tri_ref, s + 8, -6) + at(tri_ref, s + 8, -5)
    )
    return donut, lower, horizontal, vertical


def scaled(nd, strips, near_ref, fan_ref, x_ref):
    step = 32

    def body(i, _):
        r0 = pl.multiple_of(i * step, step)
        for s, (ref, k) in strips.items():
            w = ref[k, pl.ds(r0, step), :].astype(F32)
            near = jnp.broadcast_to(near_ref[8 + s : 9 + s, :], (step, LANES))
            x_ref[s + 5, pl.ds(r0, step), :] = w * near * fan_ref[pl.ds(r0 + 8 + s, step), :]
        return 0

    lax.fori_loop(0, (nd + 2 * RIM) // step, body, 0)


def strips_of(stride, low_ref, mid_ref, high_ref):
    strips = {}
    for s in range(-5, 0):
        strips[s] = (low_ref, s + 5)
    for s in range(stride):
        strips[s] = (mid_ref, s)
    for s in range(stride, stride + 5):
        strips[s] = (high_ref, s - stride)
    return strips


def observed_kernel(nd, nb, low_ref, mid_ref, high_ref, near_ref, fan_ref, center_ref,
                    donut_ref, lower_ref, horizontal_ref, vertical_ref,
                    x_ref, tri_ref, u_ref, wd_ref, lp_ref):
    stride = nb // LANES
    scaled(nd, strips_of(stride, low_ref, mid_ref, high_ref), near_ref, fan_ref, x_ref)
    windows(nd, stride, x_ref, tri_ref, u_ref, wd_ref, lp_ref)
    step = 32

    def body(i, _):
        o0 = pl.multiple_of(i * step, step)
        r0 = o0 + RIM
        for s in range(stride):
            center_ref[s, pl.ds(o0, step), :] = x_ref[s + 5, pl.ds(r0, step), :]
            sums = sums_at(s, r0, step, tri_ref, u_ref, wd_ref, lp_ref)
            for ref, value in zip((donut_ref, lower_ref, horizontal_ref, vertical_ref), sums):
                ref[s, pl.ds(o0, step), :] = value
        return 0

    lax.fori_loop(0, nd // step, body, 0)


def score_kernel(nd, nb, low_ref, mid_ref, high_ref, diag_ref, center_ref,
                 donut_ref, lower_ref, horizontal_ref, vertical_ref, out_ref,
                 col_ref, x_ref, tri_ref, u_ref, wd_ref, lp_ref, perm_ref):
    stride = nb // LANES
    total_rows = nd + 2 * RIM
    expected = diag_ref[0:1, :] / jnp.maximum(diag_ref[1:2, :], 1.0)
    for t in range(diag_ref.shape[1] // LANES):
        column(expected[:, t * LANES : (t + 1) * LANES], col_ref, t * LANES)
    strips = strips_of(stride, low_ref, mid_ref, high_ref)
    step = 32

    def fill(i, _):
        r0 = pl.multiple_of(i * step, step)
        e = col_ref[pl.ds(r0, step), :]
        for s, (ref, k) in strips.items():
            w = ref[k, pl.ds(r0, step), :].astype(F32)
            x_ref[s + 5, pl.ds(r0, step), :] = jnp.where(w > 0.0, e, 0.0)
        return 0

    lax.fori_loop(0, total_rows // step, fill, 0)
    windows(nd, stride, x_ref, tri_ref, u_ref, wd_ref, lp_ref)
    row, lane = iota((LANES, nb), 0), iota((LANES, nb), 1)
    for s in range(stride):
        perm_ref[s * LANES : (s + 1) * LANES, :] = (lane == row * stride + s).astype(F32).astype(BF16)
    perm = perm_ref[...]

    def body(i, _):
        o0 = pl.multiple_of(i * step, step)
        r0 = o0 + RIM
        e = col_ref[pl.ds(r0, step), :]
        inverse = 1.0 / e
        scores = []
        for s in range(stride):
            sums = sums_at(s, r0, step, tri_ref, u_ref, wd_ref, lp_ref)
            score = None
            for ref, value in zip((donut_ref, lower_ref, horizontal_ref, vertical_ref), sums):
                ratio = (value + e) / (ref[s, pl.ds(o0, step), :] + e)
                score = ratio if score is None else jnp.minimum(score, ratio)
            w = mid_ref[s, pl.ds(r0, step), :].astype(F32)
            score = score * (center_ref[s, pl.ds(o0, step), :] * inverse)
            scores.append(jnp.where(w > 0.0, score, 0.0))
        scores = jnp.concatenate(scores, axis=1)
        hi, mid, _ = split3(scores)
        out_ref[pl.ds(o0, step), :] = jnp.dot(hi, perm, preferred_element_type=F32) + jnp.dot(
            mid, perm, preferred_element_type=F32
        )
        return 0

    lax.fori_loop(0, nd // step, body, 0)


def exchange(x, axis, masks):
    size = lax.axis_size(axis)
    parts = [lax.ppermute(x, axis, [(i, i ^ mask) for i in range(size)]) for mask in masks]
    for part in parts:
        x = x + part
    return x


def total(x, axis):
    size = lax.axis_size(axis)
    bit = 1
    while bit < size:
        x = exchange(x, axis, [bit])
        bit *= 2
    return x


def to_neighbours(before, after, axis):
    size = lax.axis_size(axis)
    up = [(i, i + 1) for i in range(size - 1)]
    down = [(j, i) for i, j in up]
    return lax.ppermute(before, axis, down), lax.ppermute(after, axis, up)


def on_device(contacts, masked_bins, chrom_bounds):
    nd, nb = contacts.shape
    cols = nb // LANES
    bins = nb * lax.axis_size("genome")
    band = nd * lax.axis_size("offset")
    rows = bins // LANES
    span = -(-nd // LANES) + cols - 1
    tall = rows + -(-band // LANES) + 24
    total_rows = nd + 2 * RIM
    shape = jax.ShapeDtypeStruct
    f = lambda *dims: shape(dims, F32)

    w, part, keep, top, bottom = pl.pallas_call(
        functools.partial(first_kernel, nd, nb),
        out_shape=(shape((nd, nb), BF16), f(rows, LANES), f(rows, LANES), f(RIM, nb), f(RIM, nb)),
        in_specs=[SMEM, VMEM, VMEM],
        out_specs=(VMEM,) * 5,
        scratch_shapes=[
            pltpu.VMEM((tall, LANES), F32),
            pltpu.VMEM((LANES, span * LANES), F32),
            pltpu.VMEM((LANES, span * LANES), F32),
            pltpu.VMEM((tall, LANES), F32),
        ],
        compiler_params=params(),
        name="first_sums",
    )(chrom_bounds, contacts, masked_bins.reshape(1, -1))

    bottom_rim, top_rim = to_neighbours(top, bottom, "offset")
    sums = total(total(part, "genome"), "offset")

    part, bias = pl.pallas_call(
        functools.partial(second_kernel, nd, nb),
        out_shape=(f(rows, LANES), f(rows, LANES)),
        in_specs=[VMEM] * 3,
        out_specs=(VMEM,) * 2,
        scratch_shapes=[
            pltpu.VMEM((tall, LANES), F32),
            pltpu.VMEM((LANES, span * LANES), F32),
            pltpu.VMEM((LANES, span * LANES), F32),
            pltpu.VMEM((tall, LANES), F32),
        ],
        compiler_params=params(),
        name="second_sums",
    )(w, sums, keep)

    left, right = pl.pallas_call(
        functools.partial(side_kernel, nd, nb),
        out_shape=(f(SIDE, total_rows), f(SIDE, total_rows)),
        in_specs=[VMEM] * 3,
        out_specs=(VMEM,) * 2,
        compiler_params=params(),
        name="sides",
    )(w, top_rim, bottom_rim)
    right_rim, left_rim = to_neighbours(left, right, "genome")
    strips = []
    for first, count in ((-5, 5), (0, cols), (cols, 5)):
        strips.append(
            pl.pallas_call(
                functools.partial(strip_kernel, nd, nb, first, count),
                out_shape=shape((count, total_rows, LANES), BF16),
                in_specs=[VMEM] * 5,
                out_specs=VMEM,
                scratch_shapes=[
                    pltpu.VMEM((nb, count * LANES), BF16),
                    pltpu.VMEM((total_rows, count * LANES), F32),
                ],
                compiler_params=params(),
                name="strips",
            )(w, top_rim, bottom_rim, left_rim, right_rim)
        )
    low, mid, high = strips
    sums = total(total(part, "genome"), "offset")

    padded = -(-total_rows // LANES) * LANES
    fan_len = fan_rows(nd)
    reach = -(-(fan_len + cols * (LANES - 1) + 2 * LANES) // LANES) * LANES
    near = 24
    near_reach = -(-(near + cols * (LANES - 1) + LANES) // LANES) * LANES
    own, fans, nears, diag = pl.pallas_call(
        functools.partial(third_kernel, nd, nb),
        out_shape=(f(cols, LANES), f(fan_len, LANES), f(near, LANES), f(8, padded)),
        in_specs=[VMEM] * 4,
        out_specs=(VMEM,) * 4,
        scratch_shapes=[
            pltpu.VMEM((tall + 8, LANES), F32),
            pltpu.VMEM((reach, LANES), F32),
            pltpu.VMEM((reach, LANES), F32),
            pltpu.VMEM((near_reach, LANES), F32),
            pltpu.VMEM((near_reach, LANES), F32),
            pltpu.VMEM((padded, 4 * LANES), BF16),
        ],
        compiler_params=params(),
        name="diagonal_sums",
    )(mid, sums, keep, bias)
    diag = total(diag, "genome")

    scratch = [
        pltpu.VMEM((cols + 10, total_rows, LANES), F32),
        pltpu.VMEM((cols + 8, total_rows, LANES), F32),
    ] + [pltpu.VMEM((cols, total_rows, LANES), F32)] * 3
    observed = pl.pallas_call(
        functools.partial(observed_kernel, nd, nb),
        out_shape=(f(cols, nd, LANES),) * 5,
        in_specs=[VMEM] * 5,
        out_specs=(VMEM,) * 5,
        scratch_shapes=scratch,
        compiler_params=params(60),
        name="observed",
    )(low, mid, high, nears, fans)

    score = pl.pallas_call(
        functools.partial(score_kernel, nd, nb),
        out_shape=f(nd, nb),
        in_specs=[VMEM] * 9,
        out_specs=VMEM,
        scratch_shapes=[pltpu.VMEM((padded, LANES), F32)] + scratch + [pltpu.VMEM((nb, nb), BF16)],
        compiler_params=params(60),
        name="score",
    )(low, mid, high, diag, *observed)
    return score, own.reshape(nb)


def solution(mesh):
    return jax.shard_map(
        on_device,
        mesh=mesh,
        in_specs=(P("offset", "genome"), P(), P()),
        out_specs=(P("offset", "genome"), P("genome")),
        check_vma=False,
    )
```

time: 758 us -> 135 us (0.18); the launches traced: 744 us -> 135 us
  other arithmetic: 340 us -> 0.68 us
  local copies, waits for them, and re-layouts: 282 us -> 5.95 us
  blocking collectives: 106 us -> 0 us
  Pallas kernels: 0 us -> 78.6 us
  starting transfers between devices: 6.43 us -> 34 us
  waiting for transfers between devices: 5.78 us -> 14.9 us
    select_n x4 -> x0, other arithmetic: 291 us -> none  [the longest x1 291 us: on_device(): peak_score = jnp.where(valid_mask > 0, score, 0.0)]
    reshape x8 -> x0, local copies, waits for them, and re-layouts: 126 us -> none  [the longest x4 69.9 us: skew_window(): tiled_window[:row_count * (length + 1)].reshape(row_count, length + 1)]
    psum x3 -> x0, blocking collectives: 106 us -> none  [the longest x2 83.1 us: on_device(): row_sums = lax.psum(contrib, ('genome', 'offset'))]
    pallas_call x0 -> x9, Pallas kernels: none -> 78.6 us  [the longest x1 33 us: on_device(): pl.pallas_call(functools.partial(score_kernel, nd, nb), out_shape=f(nd, n...]
    another operation x21 -> x0, local copies, waits for them, and re-layouts: 71.9 us -> none  [the longest x8 61.8 us: skew_window(): tiled_window = jnp.tile(window, row_count + 1)]
    ppermute x4 -> x17, starting transfers between devices: 6.43 us -> 34 us  [the longest x13 26.3 us: exchange(): lax.ppermute(x, axis, [(i, i ^ mask) for i in range(size)])]
    concatenate x5 -> x0, local copies, waits for them, and re-layouts: 24.2 us -> none  [the longest x1 23.8 us: extended(): value = jnp.concatenate([before, value, after], axis=dim)]
    reduce_sum x8 -> x0, other arithmetic: 22.8 us -> none  [the longest x2 8.6 us: antidiagonal_sums(): return jnp.sum(sheared, axis=0)]
  transfers between devices with their start and end apart: 4 -> 17, of which waited for: 3 -> 9; matrix products, arithmetic and copies ran while one was open for 1% -> 0% of each run, Pallas kernels for 0% -> 25%
where the time goes in v1:
time: 135 us
  Pallas kernels  78.6 us (58%)
  starting transfers between devices  34 us (25%)
  waiting for transfers between devices  14.9 us (11%)
  local copies, waits for them, and re-layouts  5.95 us (4%)
    pallas_call x1, Pallas kernels, on_device(): pl.pallas_call(functools.partial(score_kernel, nd, nb), out_shape=f(nd, n...  33 us
    ppermute x13, starting transfers between devices, exchange(): lax.ppermute(x, axis, [(i, i ^ mask) for i in range(size)])  26.3 us
    pallas_call x3, Pallas kernels, on_device(): pl.pallas_call(functools.partial(strip_kernel, nd, nb, first, count), out...  18.3 us
    pallas_call x1, Pallas kernels, on_device(): pl.pallas_call(functools.partial(observed_kernel, nd, nb), out_shape=(f(c...  15.6 us
    ppermute x13, waiting for transfers between devices, exchange(): lax.ppermute(x, axis, [(i, i ^ mask) for i in range(size)])  14.8 us
    ppermute x4, starting transfers between devices, to_neighbours(): return (lax.ppermute(before, axis, down), lax.ppermute(after, axis, up))  7.7 us
    unnamed x16, local copies, waits for them, and re-layouts  5.95 us
    pallas_call x1, Pallas kernels, on_device(): pl.pallas_call(functools.partial(third_kernel, nd, nb), out_shape=(f(cols...  5.05 us
  transfers between devices with their start and end apart: 17, of which 9 were waited for; matrix products, arithmetic and copies ran while one was open for 0% of the time, Pallas kernels for 25%

profile of v1, /device:TPU:0, one launch (start us, length us, event | category | flops | bytes accessed | tf_op | source)
XLA Modules:
  0.0 134.9 jit_solution(7270722166325768402)
XLA Ops:
  0.6 1.4 %copy-done.3 = bf16[1280,640]{1,0:T(8,128)(2,1)S(1)} copy-done((bf16[1280,640]{1,0:T(8,128)(2,1)S(1)}, bf16[1280,640]{1,0:T(8,128)(2,1)}, u32[]{:S(2)}) %copy-start.3) | copy-done | bytes 1638424
  2.1 0.7 copy-done.6
  2.7 0.7 copy-done.7
  3.4 3.6 %first_sums.1 = (bf16[1280,640]{1,0:T(8,128)(2,1)S(1)}, f32[40,128]{1,0:T(8,128)S(1)}, f32[40,128]{1,0:T(8,128)S(1)}, f32[16,640]{1,0:T(8,128)S(1)}, f32[16,640]{1,0:T(8,128)S(1)}) custom-call(s32[2]{0:T(128)S(1)} %copy-done.6, bf16[1280,640]{1,0:T(8,128)(2,1)S(1)} %copy-done.3, s32[1,128]{1,0:T(1,128)S(1)} %bitcast.2), custom_call_target="tpu_custom_call" | custom-call | tf_op jit(solution)/shard_map/first_sums/pallas_call | solution.py:556
  7.0 0.5 collective-permute-start.4
  7.5 0.8 collective-permute-done.4
  8.4 2.8 %collective-permute-start.5 = (f32[40,128]{1,0:T(8,128)S(1)}, f32[40,128]{1,0:T(8,128)S(1)}, u32[]{:S(2)}, u32[]{:S(2)}) collective-permute-start(f32[40,128]{1,0:T(8,128)S(1)} %add.39), channel_id=1, source_target_pairs={{0,8},{4,12},{8,0},{12,4},{16,24},{20,28},{24,16},{28,20},{1,9},{5... | collective-permute-start | bytes 61448 | tf_op jit(solution)/shard_map/ppermute | solution.py:522
  11.2 1.8 %collective-permute-done.5 = f32[40,128]{1,0:T(8,128)S(1)} collective-permute-done((f32[40,128]{1,0:T(8,128)S(1)}, f32[40,128]{1,0:T(8,128)S(1)}, u32[]{:S(2)}, u32[]{:S(2)}) %collective-permute-start.5) | collective-permute-done | bytes 20512 | tf_op jit(solution)/shard_map/ppermute | solution.py:522
  13.0 2.0 %collective-permute-start.6 = (f32[40,128]{1,0:T(8,128)S(1)}, f32[40,128]{1,0:T(8,128)S(1)}, u32[]{:S(2)}, u32[]{:S(2)}) collective-permute-start(f32[40,128]{1,0:T(8,128)S(1)} %add.40), channel_id=1, source_target_pairs={{0,16},{4,20},{8,24},{12,28},{16,0},{20,4},{24,8},{28,12},{1,17},{... | collective-permute-start | bytes 61448 | tf_op jit(solution)/shard_map/ppermute | solution.py:522
  15.0 1.8 %collective-permute-done.6 = f32[40,128]{1,0:T(8,128)S(1)} collective-permute-done((f32[40,128]{1,0:T(8,128)S(1)}, f32[40,128]{1,0:T(8,128)S(1)}, u32[]{:S(2)}, u32[]{:S(2)}) %collective-permute-start.6) | collective-permute-done | bytes 20512 | tf_op jit(solution)/shard_map/ppermute | solution.py:522
  16.8 2.1 %collective-permute-start.7 = (f32[40,128]{1,0:T(8,128)S(1)}, f32[40,128]{1,0:T(8,128)S(1)}, u32[]{:S(2)}, u32[]{:S(2)}) collective-permute-start(f32[40,128]{1,0:T(8,128)S(1)} %add.41), channel_id=1, source_target_pairs={{0,1},{1,0},{2,3},{3,2},{4,5},{5,4},{6,7},{7,6},{8,9},{9,8},{10,11... | collective-permute-start | bytes 61448 | tf_op jit(solution)/shard_map/ppermute | solution.py:522
  18.9 1.8 %collective-permute-done.7 = f32[40,128]{1,0:T(8,128)S(1)} collective-permute-done((f32[40,128]{1,0:T(8,128)S(1)}, f32[40,128]{1,0:T(8,128)S(1)}, u32[]{:S(2)}, u32[]{:S(2)}) %collective-permute-start.7) | collective-permute-done | bytes 20512 | tf_op jit(solution)/shard_map/ppermute | solution.py:522
  20.6 3.0 %collective-permute-start.8 = (f32[40,128]{1,0:T(8,128)S(1)}, f32[40,128]{1,0:T(8,128)S(1)}, u32[]{:S(2)}, u32[]{:S(2)}) collective-permute-start(f32[40,128]{1,0:T(8,128)S(1)} %add.42), channel_id=1, source_target_pairs={{0,2},{1,3},{2,0},{3,1},{4,6},{5,7},{6,4},{7,5},{8,10},{9,11},{10,... | collective-permute-start | bytes 61448 | tf_op jit(solution)/shard_map/ppermute | solution.py:522
  23.7 1.8 %collective-permute-done.8 = f32[40,128]{1,0:T(8,128)S(1)} collective-permute-done((f32[40,128]{1,0:T(8,128)S(1)}, f32[40,128]{1,0:T(8,128)S(1)}, u32[]{:S(2)}, u32[]{:S(2)}) %collective-permute-start.8) | collective-permute-done | bytes 20512 | tf_op jit(solution)/shard_map/ppermute | solution.py:522
  25.4 2.8 %second_sums.1 = (f32[40,128]{1,0:T(8,128)S(1)}, f32[40,128]{1,0:T(8,128)S(1)}) custom-call(bf16[1280,640]{1,0:T(8,128)(2,1)S(1)} %get-tuple-element.20.w_ref, f32[40,128]{1,0:T(8,128)S(1)} %add.43.sums_ref, f32[40,128]{1,0:T(8,128)S(1)} %get-tuple-element.26.keep_ref), custom_call_target="tpu_custom_call" | custom-call | tf_op jit(solution)/shard_map/second_sums/pallas_call | solution.py:574
  28.2 0.1 collective-permute-start.9
  28.3 3.8 %collective-permute-start = (f32[16,640]{1,0:T(8,128)S(1)}, f32[16,640]{1,0:T(8,128)S(1)}, u32[]{:S(2)}, u32[]{:S(2)}) collective-permute-start(f32[16,640]{1,0:T(8,128)S(1)} %get-tuple-element.21), channel_id=1, source_target_pairs={{0,1},{1,2},{2,3},{4,5},{5,6},{6,7},{8,9},{9,10},{10,11},{12,13},{... | collective-permute-start | bytes 122888 | tf_op jit(solution)/shard_map/ppermute | solution.py:541
  32.1 1.3 collective-permute-start.1
  33.4 0.0 collective-permute-done.9
  33.4 1.6 %collective-permute-start.10 = (f32[40,128]{1,0:T(8,128)S(1)}, f32[40,128]{1,0:T(8,128)S(1)}, u32[]{:S(2)}, u32[]{:S(2)}) collective-permute-start(f32[40,128]{1,0:T(8,128)S(1)} %add.44), channel_id=1, source_target_pairs={{0,8},{4,12},{8,0},{12,4},{16,24},{20,28},{24,16},{28,20},{1,9},{5... | collective-permute-start | bytes 61448 | tf_op jit(solution)/shard_map/ppermute | solution.py:522
  35.0 2.3 %collective-permute-done.10 = f32[40,128]{1,0:T(8,128)S(1)} collective-permute-done((f32[40,128]{1,0:T(8,128)S(1)}, f32[40,128]{1,0:T(8,128)S(1)}, u32[]{:S(2)}, u32[]{:S(2)}) %collective-permute-start.10) | collective-permute-done | bytes 20512 | tf_op jit(solution)/shard_map/ppermute | solution.py:522
  37.3 1.5 %collective-permute-start.11 = (f32[40,128]{1,0:T(8,128)S(1)}, f32[40,128]{1,0:T(8,128)S(1)}, u32[]{:S(2)}, u32[]{:S(2)}) collective-permute-start(f32[40,128]{1,0:T(8,128)S(1)} %add.45), channel_id=1, source_target_pairs={{0,16},{4,20},{8,24},{12,28},{16,0},{20,4},{24,8},{28,12},{1,17},{... | collective-permute-start | bytes 61448 | tf_op jit(solution)/shard_map/ppermute | solution.py:522
  38.8 0.0 collective-permute-done.top_ref
  38.8 0.0 collective-permute-done.1.bottom_ref
  38.8 0.3 sides.1
  39.1 1.3 collective-permute-start.2
  40.4 1.3 collective-permute-start.3
  41.7 0.0 collective-permute-done.11
  41.7 2.7 %collective-permute-start.12 = (f32[40,128]{1,0:T(8,128)S(1)}, f32[40,128]{1,0:T(8,128)S(1)}, u32[]{:S(2)}, u32[]{:S(2)}) collective-permute-start(f32[40,128]{1,0:T(8,128)S(1)} %add.46), channel_id=1, source_target_pairs={{0,1},{1,0},{2,3},{3,2},{4,5},{5,4},{6,7},{7,6},{8,9},{9,8},{10,11... | collective-permute-start | bytes 61448 | tf_op jit(solution)/shard_map/ppermute | solution.py:522
  44.4 1.8 %collective-permute-done.12 = f32[40,128]{1,0:T(8,128)S(1)} collective-permute-done((f32[40,128]{1,0:T(8,128)S(1)}, f32[40,128]{1,0:T(8,128)S(1)}, u32[]{:S(2)}, u32[]{:S(2)}) %collective-permute-start.12) | collective-permute-done | bytes 20512 | tf_op jit(solution)/shard_map/ppermute | solution.py:522
  46.2 3.0 %collective-permute-start.13 = (f32[40,128]{1,0:T(8,128)S(1)}, f32[40,128]{1,0:T(8,128)S(1)}, u32[]{:S(2)}, u32[]{:S(2)}) collective-permute-start(f32[40,128]{1,0:T(8,128)S(1)} %add.47), channel_id=1, source_target_pairs={{0,2},{1,3},{2,0},{3,1},{4,6},{5,7},{6,4},{7,5},{8,10},{9,11},{10,... | collective-permute-start | bytes 61448 | tf_op jit(solution)/shard_map/ppermute | solution.py:522
  49.2 0.0 collective-permute-done.2.left_ref
  49.2 0.0 collective-permute-done.3.right_ref
  49.2 5.8 %strips.4.mid_ref = bf16[5,1312,128]{2,1,0:T(8,128)(2,1)S(1)} custom-call(bf16[1280,640]{1,0:T(8,128)(2,1)S(1)} %get-tuple-element.20.w_ref, f32[16,640]{1,0:T(8,128)S(1)} %collective-permute-done.top_ref, f32[16,640]{1,0:T(8,128)S(1)} %collective-permute-done.1.bottom_ref, f32[8,1312]{1,0:T(8,128)S(1)} %collective-permute-done.2.left_ref, ...), custom_call_target="tpu_custom_call" | custom-call | tf_op jit(solution)/shard_map/strips/pallas_call | solution.py:601
  55.1 5.1 %diagonal_sums.1 = (f32[5,128]{1,0:T(8,128)}, f32[1344,128]{1,0:T(8,128)S(1)}, f32[24,128]{1,0:T(8,128)S(1)}, f32[8,1408]{1,0:T(8,128)S(1)}) custom-call(bf16[5,1312,128]{2,1,0:T(8,128)(2,1)S(1)} %strips.4.mid_ref, f32[40,128]{1,0:T(8,128)S(1)} %add.48.sums_ref, f32[40,128]{1,0:T(8,128)S(1)} %get-tuple-element.26.keep_ref, ...), custom_call_target="tpu_custom_call" | custom-call | tf_op jit(solution)/shard_map/diagonal_sums/pallas_call | solution.py:622
  60.2 0.8 copy-done.4
  61.0 1.4 %collective-permute-start.14 = (f32[8,1408]{1,0:T(8,128)S(1)}, f32[8,1408]{1,0:T(8,128)S(1)}, u32[]{:S(2)}, u32[]{:S(2)}) collective-permute-start(f32[8,1408]{1,0:T(8,128)S(1)} %get-tuple-element.29), channel_id=1, source_target_pairs={{0,4},{4,0},{8,12},{12,8},{16,20},{20,16},{24,28},{28,24},{1,5},{5... | collective-permute-start | bytes 135176 | tf_op jit(solution)/shard_map/ppermute | solution.py:522
  62.5 0.9 collective-permute-done.14
  63.3 3.5 %collective-permute-start.15 = (f32[8,1408]{1,0:T(8,128)S(1)}, f32[8,1408]{1,0:T(8,128)S(1)}, u32[]{:S(2)}, u32[]{:S(2)}) collective-permute-start(f32[8,1408]{1,0:T(8,128)S(1)} %add.49), channel_id=1, source_target_pairs={{0,8},{4,12},{8,0},{12,4},{16,24},{20,28},{24,16},{28,20},{1,9},{5... | collective-permute-start | bytes 135176 | tf_op jit(solution)/shard_map/ppermute | solution.py:522
  66.8 2.0 %collective-permute-done.15 = f32[8,1408]{1,0:T(8,128)S(1)} collective-permute-done((f32[8,1408]{1,0:T(8,128)S(1)}, f32[8,1408]{1,0:T(8,128)S(1)}, u32[]{:S(2)}, u32[]{:S(2)}) %collective-permute-start.15) | collective-permute-done | bytes 45088 | tf_op jit(solution)/shard_map/ppermute | solution.py:522
  68.8 2.0 %collective-permute-start.16 = (f32[8,1408]{1,0:T(8,128)S(1)}, f32[8,1408]{1,0:T(8,128)S(1)}, u32[]{:S(2)}, u32[]{:S(2)}) collective-permute-start(f32[8,1408]{1,0:T(8,128)S(1)} %add.50), channel_id=1, source_target_pairs={{0,16},{4,20},{8,24},{12,28},{16,0},{20,4},{24,8},{28,12},{1,17},{... | collective-permute-start | bytes 135176 | tf_op jit(solution)/shard_map/ppermute | solution.py:522
  70.8 6.2 %strips.5.high_ref = bf16[5,1312,128]{2,1,0:T(8,128)(2,1)S(1)} custom-call(bf16[1280,640]{1,0:T(8,128)(2,1)S(1)} %get-tuple-element.20.w_ref, f32[16,640]{1,0:T(8,128)S(1)} %collective-permute-done.top_ref, f32[16,640]{1,0:T(8,128)S(1)} %collective-permute-done.1.bottom_ref, f32[8,1312]{1,0:T(8,128)S(1)} %collective-permute-done.2.left_ref, ...), custom_call_target="tpu_custom_call" | custom-call | tf_op jit(solution)/shard_map/strips/pallas_call | solution.py:601
  77.1 1.2 copy-done.1
  78.3 6.2 %strips.3.low_ref = bf16[5,1312,128]{2,1,0:T(8,128)(2,1)S(1)} custom-call(bf16[1280,640]{1,0:T(8,128)(2,1)S(1)} %get-tuple-element.20.w_ref, f32[16,640]{1,0:T(8,128)S(1)} %collective-permute-done.top_ref, f32[16,640]{1,0:T(8,128)S(1)} %collective-permute-done.1.bottom_ref, f32[8,1312]{1,0:T(8,128)S(1)} %collective-permute-done.2.left_ref, ...), custom_call_target="tpu_custom_call" | custom-call | tf_op jit(solution)/shard_map/strips/pallas_call | solution.py:601
  84.5 1.2 copy-done.2
  85.7 15.6 %observed.1 = (f32[5,1280,128]{2,1,0:T(8,128)}, f32[5,1280,128]{2,1,0:T(8,128)}, f32[5,1280,128]{2,1,0:T(8,128)}, f32[5,1280,128]{2,1,0:T(8,128)}, f32[5,1280,128]{2,1,0:T(8,128)}) custom-call(bf16[5,1312,128]{2,1,0:T(8,128)(2,1)} %copy-done.2, bf16[5,1312,128]{2,1,0:T(8,128)(2,1)} %copy-done, bf16[5,1312,128]{2,1,0:T(8,128)(2,1)} %copy-done.1, ...), custom_call_target="tpu_custom_call" | custom-call | tf_op jit(solution)/shard_map/observed/pallas_call | solution.py:644
  101.3 0.6 add.51.diag_ref
  101.9 33.0 %score.1 = f32[1280,640]{1,0:T(8,128)} custom-call(bf16[5,1312,128]{2,1,0:T(8,128)(2,1)} %copy-done.2, bf16[5,1312,128]{2,1,0:T(8,128)(2,1)} %copy-done, bf16[5,1312,128]{2,1,0:T(8,128)(2,1)} %copy-done.1, f32[8,1408]{1,0:T(8,128)} %add.51.diag_ref, f32[5,1280,128]{2,1,0:T(8,128)} %get-tuple-element.32.center_ref, ...), custom_call_target="tpu_custom_call" | custom-call | tf_op jit(solution)/shard_map/score/pallas_call | solution.py:654
  (24 shorter events, 0.1 us)
Async XLA Ops:
  0.6 1.4 %copy-start.3 = (bf16[1280,640]{1,0:T(8,128)(2,1)S(1)}, bf16[1280,640]{1,0:T(8,128)(2,1)}, u32[]{:S(2)}) copy-start(bf16[1280,640]{1,0:T(8,128)(2,1)} %x_ref.1) | copy-start | bytes 4915204
  2.1 0.7 copy-start.6
  2.7 0.7 copy-start.7
  7.0 1.4 %collective-permute-start.4 = (f32[40,128]{1,0:T(8,128)S(1)}, f32[40,128]{1,0:T(8,128)S(1)}, u32[]{:S(2)}, u32[]{:S(2)}) collective-permute-start(f32[40,128]{1,0:T(8,128)S(1)} %get-tuple-element.25), channel_id=1, source_target_pairs={{0,4},{4,0},{8,12},{12,8},{16,20},{20,16},{24,28},{28,24},{1,5},{5... | collective-permute-start | bytes 61448 | tf_op jit(solution)/shard_map/ppermute | solution.py:522
  8.4 4.6 %collective-permute-start.5 = (f32[40,128]{1,0:T(8,128)S(1)}, f32[40,128]{1,0:T(8,128)S(1)}, u32[]{:S(2)}, u32[]{:S(2)}) collective-permute-start(f32[40,128]{1,0:T(8,128)S(1)} %add.39), channel_id=1, source_target_pairs={{0,8},{4,12},{8,0},{12,4},{16,24},{20,28},{24,16},{28,20},{1,9},{5... | collective-permute-start | bytes 61448 | tf_op jit(solution)/shard_map/ppermute | solution.py:522
  13.0 3.8 %collective-permute-start.6 = (f32[40,128]{1,0:T(8,128)S(1)}, f32[40,128]{1,0:T(8,128)S(1)}, u32[]{:S(2)}, u32[]{:S(2)}) collective-permute-start(f32[40,128]{1,0:T(8,128)S(1)} %add.40), channel_id=1, source_target_pairs={{0,16},{4,20},{8,24},{12,28},{16,0},{20,4},{24,8},{28,12},{1,17},{... | collective-permute-start | bytes 61448 | tf_op jit(solution)/shard_map/ppermute | solution.py:522
  16.8 3.8 %collective-permute-start.7 = (f32[40,128]{1,0:T(8,128)S(1)}, f32[40,128]{1,0:T(8,128)S(1)}, u32[]{:S(2)}, u32[]{:S(2)}) collective-permute-start(f32[40,128]{1,0:T(8,128)S(1)} %add.41), channel_id=1, source_target_pairs={{0,1},{1,0},{2,3},{3,2},{4,5},{5,4},{6,7},{7,6},{8,9},{9,8},{10,11... | collective-permute-start | bytes 61448 | tf_op jit(solution)/shard_map/ppermute | solution.py:522
  20.6 4.8 %collective-permute-start.8 = (f32[40,128]{1,0:T(8,128)S(1)}, f32[40,128]{1,0:T(8,128)S(1)}, u32[]{:S(2)}, u32[]{:S(2)}) collective-permute-start(f32[40,128]{1,0:T(8,128)S(1)} %add.42), channel_id=1, source_target_pairs={{0,2},{1,3},{2,0},{3,1},{4,6},{5,7},{6,4},{7,5},{8,10},{9,11},{10,... | collective-permute-start | bytes 61448 | tf_op jit(solution)/shard_map/ppermute | solution.py:522
  28.2 5.2 %collective-permute-start.9 = (f32[40,128]{1,0:T(8,128)S(1)}, f32[40,128]{1,0:T(8,128)S(1)}, u32[]{:S(2)}, u32[]{:S(2)}) collective-permute-start(f32[40,128]{1,0:T(8,128)S(1)} %get-tuple-element.27), channel_id=1, source_target_pairs={{0,4},{4,0},{8,12},{12,8},{16,20},{20,16},{24,28},{28,24},{1,5},{5... | collective-permute-start | bytes 61448 | tf_op jit(solution)/shard_map/ppermute | solution.py:522
  28.3 10.5 %collective-permute-start = (f32[16,640]{1,0:T(8,128)S(1)}, f32[16,640]{1,0:T(8,128)S(1)}, u32[]{:S(2)}, u32[]{:S(2)}) collective-permute-start(f32[16,640]{1,0:T(8,128)S(1)} %get-tuple-element.21), channel_id=1, source_target_pairs={{0,1},{1,2},{2,3},{4,5},{5,6},{6,7},{8,9},{9,10},{10,11},{12,13},{... | collective-permute-start | bytes 122888 | tf_op jit(solution)/shard_map/ppermute | solution.py:541
  32.1 6.7 %collective-permute-start.1 = (f32[16,640]{1,0:T(8,128)S(1)}, f32[16,640]{1,0:T(8,128)S(1)}, u32[]{:S(2)}, u32[]{:S(2)}) collective-permute-start(f32[16,640]{1,0:T(8,128)S(1)} %get-tuple-element.22), channel_id=1, source_target_pairs={{1,0},{2,1},{3,2},{5,4},{6,5},{7,6},{9,8},{10,9},{11,10},{13,12},{... | collective-permute-start | bytes 122888 | tf_op jit(solution)/shard_map/ppermute | solution.py:541
  33.4 3.8 %collective-permute-start.10 = (f32[40,128]{1,0:T(8,128)S(1)}, f32[40,128]{1,0:T(8,128)S(1)}, u32[]{:S(2)}, u32[]{:S(2)}) collective-permute-start(f32[40,128]{1,0:T(8,128)S(1)} %add.44), channel_id=1, source_target_pairs={{0,8},{4,12},{8,0},{12,4},{16,24},{20,28},{24,16},{28,20},{1,9},{5... | collective-permute-start | bytes 61448 | tf_op jit(solution)/shard_map/ppermute | solution.py:522
  37.3 4.4 %collective-permute-start.11 = (f32[40,128]{1,0:T(8,128)S(1)}, f32[40,128]{1,0:T(8,128)S(1)}, u32[]{:S(2)}, u32[]{:S(2)}) collective-permute-start(f32[40,128]{1,0:T(8,128)S(1)} %add.45), channel_id=1, source_target_pairs={{0,16},{4,20},{8,24},{12,28},{16,0},{20,4},{24,8},{28,12},{1,17},{... | collective-permute-start | bytes 61448 | tf_op jit(solution)/shard_map/ppermute | solution.py:522
  39.1 10.1 %collective-permute-start.2 = (f32[8,1312]{1,0:T(8,128)S(1)}, f32[8,1312]{1,0:T(8,128)S(1)}, u32[]{:S(2)}, u32[]{:S(2)}) collective-permute-start(f32[8,1312]{1,0:T(8,128)S(1)} %get-tuple-element.23), channel_id=1, source_target_pairs={{0,4},{4,8},{8,12},{12,16},{16,20},{20,24},{24,28},{1,5},{5,9},{9,... | collective-permute-start | bytes 125960 | tf_op jit(solution)/shard_map/ppermute | solution.py:541
  40.4 8.8 %collective-permute-start.3 = (f32[8,1312]{1,0:T(8,128)S(1)}, f32[8,1312]{1,0:T(8,128)S(1)}, u32[]{:S(2)}, u32[]{:S(2)}) collective-permute-start(f32[8,1312]{1,0:T(8,128)S(1)} %get-tuple-element.24), channel_id=1, source_target_pairs={{4,0},{8,4},{12,8},{16,12},{20,16},{24,20},{28,24},{5,1},{9,5},{13... | collective-permute-start | bytes 125960 | tf_op jit(solution)/shard_map/ppermute | solution.py:541
  41.7 4.5 %collective-permute-start.12 = (f32[40,128]{1,0:T(8,128)S(1)}, f32[40,128]{1,0:T(8,128)S(1)}, u32[]{:S(2)}, u32[]{:S(2)}) collective-permute-start(f32[40,128]{1,0:T(8,128)S(1)} %add.46), channel_id=1, source_target_pairs={{0,1},{1,0},{2,3},{3,2},{4,5},{5,4},{6,7},{7,6},{8,9},{9,8},{10,11... | collective-permute-start | bytes 61448 | tf_op jit(solution)/shard_map/ppermute | solution.py:522
  46.2 8.9 %collective-permute-start.13 = (f32[40,128]{1,0:T(8,128)S(1)}, f32[40,128]{1,0:T(8,128)S(1)}, u32[]{:S(2)}, u32[]{:S(2)}) collective-permute-start(f32[40,128]{1,0:T(8,128)S(1)} %add.47), channel_id=1, source_target_pairs={{0,2},{1,3},{2,0},{3,1},{4,6},{5,7},{6,4},{7,5},{8,10},{9,11},{10,... | collective-permute-start | bytes 61448 | tf_op jit(solution)/shard_map/ppermute | solution.py:522
  55.1 29.4 %copy-start = (bf16[5,1312,128]{2,1,0:T(8,128)(2,1)}, bf16[5,1312,128]{2,1,0:T(8,128)(2,1)S(1)}, u32[]{:S(2)}) copy-start(bf16[5,1312,128]{2,1,0:T(8,128)(2,1)S(1)} %strips.4.mid_ref) | copy-start | bytes 5038084
  60.2 0.8 copy-start.4
  61.0 23.5 %copy-start.5 = (f32[24,128]{1,0:T(8,128)}, f32[24,128]{1,0:T(8,128)S(1)}, u32[]{:S(2)}) copy-start(f32[24,128]{1,0:T(8,128)S(1)} %get-tuple-element.30.near_ref) | copy-start | bytes 36868
  61.0 2.3 %collective-permute-start.14 = (f32[8,1408]{1,0:T(8,128)S(1)}, f32[8,1408]{1,0:T(8,128)S(1)}, u32[]{:S(2)}, u32[]{:S(2)}) collective-permute-start(f32[8,1408]{1,0:T(8,128)S(1)} %get-tuple-element.29), channel_id=1, source_target_pairs={{0,4},{4,0},{8,12},{12,8},{16,20},{20,16},{24,28},{28,24},{1,5},{5... | collective-permute-start | bytes 135176 | tf_op jit(solution)/shard_map/ppermute | solution.py:522
  63.3 5.5 %collective-permute-start.15 = (f32[8,1408]{1,0:T(8,128)S(1)}, f32[8,1408]{1,0:T(8,128)S(1)}, u32[]{:S(2)}, u32[]{:S(2)}) collective-permute-start(f32[8,1408]{1,0:T(8,128)S(1)} %add.49), channel_id=1, source_target_pairs={{0,8},{4,12},{8,0},{12,4},{16,24},{20,28},{24,16},{28,20},{1,9},{5... | collective-permute-start | bytes 135176 | tf_op jit(solution)/shard_map/ppermute | solution.py:522
  68.8 32.5 %collective-permute-start.16 = (f32[8,1408]{1,0:T(8,128)S(1)}, f32[8,1408]{1,0:T(8,128)S(1)}, u32[]{:S(2)}, u32[]{:S(2)}) collective-permute-start(f32[8,1408]{1,0:T(8,128)S(1)} %add.50), channel_id=1, source_target_pairs={{0,16},{4,20},{8,24},{12,28},{16,0},{20,4},{24,8},{28,12},{1,17},{... | collective-permute-start | bytes 135176 | tf_op jit(solution)/shard_map/ppermute | solution.py:522
  77.0 1.2 copy-start.1
  84.5 1.2 copy-start.2

commit v2 on v1

--- a/solution.py
+++ b/solution.py
@@ -8,13 +8,15 @@
 from jax.sharding import PartitionSpec as P
 
 RIM = 16
+STEP = 64
 SIDE = 8
 LANES = 128
 F32 = jnp.float32
 BF16 = jnp.bfloat16
 TINY = 2.0**-126
 VMEM = pl.BlockSpec(memory_space=pltpu.VMEM)
-SMEM = pl.BlockSpec(memory_space=pltpu.SMEM)
+HBM = pl.BlockSpec(memory_space=pltpu.HBM)
+ANY = pl.BlockSpec(memory_space=pl.ANY)
 NT = (((1,), (1,)), ((), ()))
 
 
@@ -132,8 +134,18 @@
     return jnp.where(hits > 0.0, 0.0, 1.0)
 
 
-def first_kernel(nd, nb, bounds_ref, x_ref, masked_ref, w_ref, part_ref, keep_ref, top_ref, bottom_ref,
-                 codes_ref, hank_ref, acc_ref, placed_ref):
+def first_kernel(nd, nb, bounds_hbm, x_hbm, masked_hbm, w_ref, part_ref, keep_ref, top_ref, bottom_ref,
+                 codes_ref, hank_ref, acc_ref, placed_ref, bounds_ref, x_ref, masked_ref, sems):
+    copies = [
+        pltpu.make_async_copy(source, target, sems.at[k])
+        for k, (source, target) in enumerate(
+            ((masked_hbm, masked_ref), (bounds_hbm, bounds_ref), (x_hbm, x_ref))
+        )
+    ]
+    for copy in copies:
+        copy.start()
+    copies[0].wait()
+    copies[1].wait()
     rows = keep_ref.shape[0]
     cols = nb // LANES
     span = -(-nd // LANES) + cols - 1
@@ -153,6 +165,7 @@
         code = codes_ref[pl.ds(row_own + c, 1), :]
         code = jnp.where(code < 0.0, -1.0, code)
         code_own.append(jnp.broadcast_to(code, (16, LANES)))
+    copies[2].wait()
 
     def entry(m, c, q0):
         here = (pl.ds(q0 + m * LANES, 16), slice(c * LANES, (c + 1) * LANES))
@@ -243,20 +256,20 @@
     def emit(block, at, side_at, rows):
         value = jnp.dot(block, perm, preferred_element_type=F32)
         if outer:
-            value = value + side_ref[pl.ds(side_at, rows), :]
+            value = value + side_ref[side_at : side_at + rows, :]
         for k in range(count):
-            out_ref[k, pl.ds(at, rows), :] = value[:, k * LANES : (k + 1) * LANES].astype(BF16)
+            out_ref[k, at : at + rows, :] = value[:, k * LANES : (k + 1) * LANES].astype(BF16)
 
     emit(top_ref[...].astype(BF16), 0, nd + RIM, RIM)
     emit(bottom_ref[...].astype(BF16), nd + RIM, nd, RIM)
-    step = 64
-
-    def body(i, _):
-        r0 = pl.multiple_of(i * step, step)
-        emit(w_ref[pl.ds(r0, step), :], r0 + RIM, r0, step)
-        return 0
-
-    lax.fori_loop(0, nd // step, body, 0)
+    emit(w_ref[...], RIM, 0, nd)
+
+
+def unstrip_kernel(nb, out_ref):
+    stride = nb // LANES
+    row, lane = iota((LANES, nb), 0), iota((LANES, nb), 1)
+    for s in range(stride):
+        out_ref[s * LANES : (s + 1) * LANES, :] = (lane == row * stride + s).astype(F32).astype(BF16)
 
 
 def column(row, out_ref, at):
@@ -339,102 +352,34 @@
 
     lax.fori_loop(0, total_rows // step, body, 0)
     ones = jnp.ones((8, 3 * LANES), BF16)
-    padded = diag_ref.shape[1]
+    padded = total_ref.shape[0]
+    tiles = padded // LANES
     if padded > total_rows:
         total_ref[total_rows:, :] = jnp.zeros((padded - total_rows, 4 * LANES), BF16)
     sums = lax.dot_general(ones, total_ref[:, : 3 * LANES], NT, preferred_element_type=F32)
     counts = lax.dot_general(ones[:, :LANES], total_ref[:, 3 * LANES :], NT, preferred_element_type=F32)
-    diag_ref[...] = jnp.where(iota((8, padded), 0) == 0, sums, counts)
-
-
-def windows(nd, stride, x_ref, tri_ref, u_ref, wd_ref, lp_ref):
-    step = 32
-    total_rows = nd + 2 * RIM
-
-    def tri(i, _):
-        r0 = pl.multiple_of(i * step + 8, 8)
-        for s in range(-4, stride + 4):
-            tri_ref[s + 4, pl.ds(r0, step), :] = (
-                x_ref[s + 4, pl.ds(r0 + 1, step), :]
-                + x_ref[s + 5, pl.ds(r0, step), :]
-                + x_ref[s + 6, pl.ds(r0 - 1, step), :]
-            )
-        return 0
-
-    lax.fori_loop(0, (total_rows - 32) // step, tri, 0)
-    for r0, size in ((1, 7), (total_rows - 24, 23)):
-        for s in range(-4, stride + 4):
-            tri_ref[s + 4, r0 : r0 + size, :] = (
-                x_ref[s + 4, r0 + 1 : r0 + 1 + size, :]
-                + x_ref[s + 5, r0 : r0 + size, :]
-                + x_ref[s + 6, r0 - 1 : r0 - 1 + size, :]
-            )
-
-    def mixed(r0, size):
-        for s in range(stride):
-            hp = tri_ref[s + 8, pl.ds(r0 - 4, size), :]
-            hm = tri_ref[s, pl.ds(r0 + 4, size), :]
-            ep = x_ref[s + 6, pl.ds(r0 - 1, size), :] + x_ref[s + 7, pl.ds(r0 - 2, size), :]
-            em = x_ref[s + 4, pl.ds(r0 + 1, size), :] + x_ref[s + 3, pl.ds(r0 + 2, size), :]
-            lp = hp + ep
-            u_ref[s, pl.ds(r0, size), :] = hp + hm
-            lp_ref[s, pl.ds(r0, size), :] = lp
-            wd_ref[s, pl.ds(r0, size), :] = lp + (hm + em)
-
-    def mixed_body(i, _):
-        mixed(pl.multiple_of(i * step + RIM, 16), step)
-        return 0
-
-    lax.fori_loop(0, nd // step, mixed_body, 0)
-    mixed(RIM - 8, 8)
-    mixed(RIM + nd, 8)
-
-    def runs(r0, size):
-        for s in range(stride):
-            wd_ref[s, pl.ds(r0, size), :] = (
-                wd_ref[s, pl.ds(r0, size), :] + wd_ref[s, pl.ds(r0 + 1, size), :] + wd_ref[s, pl.ds(r0 + 2, size), :]
-            )
-            tri_ref[s, pl.ds(r0, size), :] = (
-                tri_ref[s + 4, pl.ds(r0, size), :]
-                + tri_ref[s + 4, pl.ds(r0 + 1, size), :]
-                + tri_ref[s + 4, pl.ds(r0 + 2, size), :]
-            )
-
-    def runs_body(i, _):
-        runs(pl.multiple_of(i * step + RIM, 16) - 5, step)
-        return 0
-
-    lax.fori_loop(0, nd // step, runs_body, 0)
-    runs(RIM + nd - 5, 8)
-
-
-def sums_at(s, r0, size, tri_ref, u_ref, wd_ref, lp_ref):
-    at = lambda ref, k, shift: ref[k, pl.ds(r0 + shift, size), :]
-    u = [at(u_ref, s, shift) for shift in (-2, -1, 0, 1, 2)]
-    donut = at(wd_ref, s, -5) + at(wd_ref, s, 3) + (u[0] + u[1]) + (u[3] + u[4])
-    vertical = u[1] + u[2] + u[3]
-    horizontal = at(tri_ref, s, -5) + at(tri_ref, s, 3)
-    lower = (at(lp_ref, s, -5) + at(lp_ref, s, -4) + at(lp_ref, s, -3)) + (
-        at(tri_ref, s + 8, -6) + at(tri_ref, s + 8, -5)
-    )
-    return donut, lower, horizontal, vertical
-
-
-def scaled(nd, strips, near_ref, fan_ref, x_ref):
-    step = 32
-
-    def body(i, _):
-        r0 = pl.multiple_of(i * step, step)
-        for s, (ref, k) in strips.items():
-            w = ref[k, pl.ds(r0, step), :].astype(F32)
-            near = jnp.broadcast_to(near_ref[8 + s : 9 + s, :], (step, LANES))
-            x_ref[s + 5, pl.ds(r0, step), :] = w * near * fan_ref[pl.ds(r0 + 8 + s, step), :]
-        return 0
-
-    lax.fori_loop(0, (nd + 2 * RIM) // step, body, 0)
-
-
-def strips_of(stride, low_ref, mid_ref, high_ref):
+    for t in range(tiles):
+        diag_ref[t : t + 1, :] = sums[0:1, t * LANES : (t + 1) * LANES]
+        diag_ref[tiles + t : tiles + t + 1, :] = counts[0:1, t * LANES : (t + 1) * LANES]
+
+
+def over(start, count, step, run):
+    steps = count // step
+    if steps > 0:
+
+        def body(i, _):
+            run(pl.multiple_of(i * step + start, 8), step)
+            return 0
+
+        lax.fori_loop(0, steps, body, 0)
+    if count % step:
+        run(start + steps * step, count % step)
+
+
+def filter_kernel(nd, nb, chunk, step, low_ref, mid_ref, high_ref, near_ref, fan_ref, diag_ref, perm_ref, out_ref,
+                  col_ref, xo_ref, xe_ref, po_ref, pe_ref, ho_ref, he_ref, uo_ref, ue_ref,
+                  lo_ref, le_ref, wo_ref, we_ref, to_ref, te_ref):
+    stride = nb // LANES
     strips = {}
     for s in range(-5, 0):
         strips[s] = (low_ref, s + 5)
@@ -442,103 +387,118 @@
         strips[s] = (mid_ref, s)
     for s in range(stride, stride + 5):
         strips[s] = (high_ref, s - stride)
-    return strips
-
-
-def observed_kernel(nd, nb, low_ref, mid_ref, high_ref, near_ref, fan_ref, center_ref,
-                    donut_ref, lower_ref, horizontal_ref, vertical_ref,
-                    x_ref, tri_ref, u_ref, wd_ref, lp_ref):
-    stride = nb // LANES
-    scaled(nd, strips_of(stride, low_ref, mid_ref, high_ref), near_ref, fan_ref, x_ref)
-    windows(nd, stride, x_ref, tri_ref, u_ref, wd_ref, lp_ref)
-    step = 32
-
-    def body(i, _):
-        o0 = pl.multiple_of(i * step, step)
-        r0 = o0 + RIM
+    base = pl.multiple_of(pl.program_id(0) * chunk, 32)
+
+    @pl.when(pl.program_id(0) == 0)
+    def _():
+        tiles = diag_ref.shape[0] // 2
+        expected = diag_ref[:tiles, :] / jnp.maximum(diag_ref[tiles:, :], 1.0)
+        for t in range(tiles):
+            column(expected[t : t + 1, :], col_ref, t * LANES)
+
+    def fill(r0, size):
+        e = col_ref[pl.ds(base + r0, size), :]
+        for s, (ref, k) in strips.items():
+            w = ref[k, pl.ds(base + r0, size), :].astype(F32)
+            near = jnp.broadcast_to(near_ref[8 + s : 9 + s, :], (size, LANES))
+            xo_ref[s + 5, pl.ds(r0, size), :] = w * near * fan_ref[pl.ds(base + r0 + 8 + s, size), :]
+            xe_ref[s + 5, pl.ds(r0, size), :] = jnp.where(w > 0.0, e, 0.0)
+
+    over(0, chunk + 2 * RIM, 32, fill)
+    observed = (xo_ref, po_ref, ho_ref, uo_ref, lo_ref, wo_ref, to_ref)
+    expected = (xe_ref, pe_ref, he_ref, ue_ref, le_ref, we_ref, te_ref)
+
+    def pairs(r0, size):
+        for s in range(-4, stride + 3):
+            for x, p, *_ in (observed, expected):
+                p[s + 4, pl.ds(r0, size), :] = x[s + 5, pl.ds(r0, size), :] + x[s + 6, pl.ds(r0 - 1, size), :]
+
+    over(8, chunk + 24, step, pairs)
+
+    def mix(r0, size):
         for s in range(stride):
-            center_ref[s, pl.ds(o0, step), :] = x_ref[s + 5, pl.ds(r0, step), :]
-            sums = sums_at(s, r0, step, tri_ref, u_ref, wd_ref, lp_ref)
-            for ref, value in zip((donut_ref, lower_ref, horizontal_ref, vertical_ref), sums):
-                ref[s, pl.ds(o0, step), :] = value
-        return 0
-
-    lax.fori_loop(0, nd // step, body, 0)
-
-
-def score_kernel(nd, nb, low_ref, mid_ref, high_ref, diag_ref, center_ref,
-                 donut_ref, lower_ref, horizontal_ref, vertical_ref, out_ref,
-                 col_ref, x_ref, tri_ref, u_ref, wd_ref, lp_ref, perm_ref):
-    stride = nb // LANES
-    total_rows = nd + 2 * RIM
-    expected = diag_ref[0:1, :] / jnp.maximum(diag_ref[1:2, :], 1.0)
-    for t in range(diag_ref.shape[1] // LANES):
-        column(expected[:, t * LANES : (t + 1) * LANES], col_ref, t * LANES)
-    strips = strips_of(stride, low_ref, mid_ref, high_ref)
-    step = 32
-
-    def fill(i, _):
-        r0 = pl.multiple_of(i * step, step)
-        e = col_ref[pl.ds(r0, step), :]
-        for s, (ref, k) in strips.items():
-            w = ref[k, pl.ds(r0, step), :].astype(F32)
-            x_ref[s + 5, pl.ds(r0, step), :] = jnp.where(w > 0.0, e, 0.0)
-        return 0
-
-    lax.fori_loop(0, total_rows // step, fill, 0)
-    windows(nd, stride, x_ref, tri_ref, u_ref, wd_ref, lp_ref)
-    row, lane = iota((LANES, nb), 0), iota((LANES, nb), 1)
-    for s in range(stride):
-        perm_ref[s * LANES : (s + 1) * LANES, :] = (lane == row * stride + s).astype(F32).astype(BF16)
-    perm = perm_ref[...]
-
-    def body(i, _):
-        o0 = pl.multiple_of(i * step, step)
-        r0 = o0 + RIM
-        e = col_ref[pl.ds(r0, step), :]
+            for x, p, h, u, l, w, t in (observed, expected):
+                here = (s, pl.ds(r0, size), slice(None))
+                at = lambda ref, k, shift: ref[k, pl.ds(r0 + shift, size), :]
+                hp = at(p, s + 7, -3) + at(x, s + 10, -5)
+                hm = at(p, s, 4) + at(x, s, 5)
+                lp = hp + at(p, s + 5, -1)
+                h[here] = hp
+                u[here] = hp + hm
+                l[here] = lp
+                w[here] = lp + (hm + at(p, s + 2, 2))
+                t[here] = at(p, s + 4, 0) + at(x, s + 4, 1)
+
+    over(8, chunk + 16, step, mix)
+
+    def runs(r0, size):
+        for s in range(stride):
+            for _, _, _, _, _, w, t in (observed, expected):
+                for ref in (w, t):
+                    at = lambda shift: ref[s, pl.ds(r0 + shift, size), :]
+                    ref[s, pl.ds(r0, size), :] = at(0) + at(1) + at(2)
+
+    over(8, chunk + 16, step, runs)
+
+    def score(r0, size):
+        e = col_ref[pl.ds(base + r0, size), :]
         inverse = 1.0 / e
-        scores = []
         for s in range(stride):
-            sums = sums_at(s, r0, step, tri_ref, u_ref, wd_ref, lp_ref)
-            score = None
-            for ref, value in zip((donut_ref, lower_ref, horizontal_ref, vertical_ref), sums):
-                ratio = (value + e) / (ref[s, pl.ds(o0, step), :] + e)
-                score = ratio if score is None else jnp.minimum(score, ratio)
-            w = mid_ref[s, pl.ds(r0, step), :].astype(F32)
-            score = score * (center_ref[s, pl.ds(o0, step), :] * inverse)
-            scores.append(jnp.where(w > 0.0, score, 0.0))
-        scores = jnp.concatenate(scores, axis=1)
-        hi, mid, _ = split3(scores)
-        out_ref[pl.ds(o0, step), :] = jnp.dot(hi, perm, preferred_element_type=F32) + jnp.dot(
-            mid, perm, preferred_element_type=F32
-        )
-        return 0
-
-    lax.fori_loop(0, nd // step, body, 0)
-
-
-def exchange(x, axis, masks):
+            sums = []
+            for x, p, h, u, l, w, t in (observed, expected):
+                at = lambda ref, shift: ref[s, pl.ds(r0 + shift, size), :]
+                below, above = at(u, -1), at(u, 1)
+                donut = (at(w, -5) + at(w, 3)) + ((at(u, -2) + below) + (above + at(u, 2)))
+                lower = (at(l, -5) + at(l, -4) + at(l, -3)) + (at(h, -2) + at(h, -1))
+                sums.append((donut, lower, at(t, -5) + at(t, 3), below + at(u, 0) + above))
+            least = None
+            for seen, hoped in zip(*sums):
+                ratio = (hoped + e) / (seen + e)
+                least = ratio if least is None else jnp.minimum(least, ratio)
+            value = least * (xo_ref[s + 5, pl.ds(r0, size), :] * inverse)
+            value = jnp.where(xe_ref[s + 5, pl.ds(r0, size), :] > 0.0, value, 0.0)
+            hi = value.astype(BF16)
+            low = (value - hi.astype(F32)).astype(BF16)
+            perm = perm_ref[s * LANES : (s + 1) * LANES, :]
+            placed = jnp.dot(
+                jnp.concatenate([hi, low], axis=1), jnp.concatenate([perm, perm], axis=0), preferred_element_type=F32
+            )
+            here = pl.ds(r0 - RIM, size)
+            out_ref[here, :] = placed if s == 0 else out_ref[here, :] + placed
+
+    over(RIM, chunk, chunk // 2, score)
+
+
+def tie(x, state, names):
+    x, values = lax.optimization_barrier((x, tuple(state[name] for name in names)))
+    state.update(zip(names, values))
+    return x
+
+
+def total(x, axes, state=None, tasks={}, due={}):
+    rounds = []
+    for axis in axes:
+        size, bit = lax.axis_size(axis), 1
+        while bit < size:
+            rounds.append((axis, [(i, i ^ bit) for i in range(size)]))
+            bit *= 2
+    for k, (axis, pairs) in enumerate(rounds):
+        if k in tasks:
+            x = tie(x, state, tasks[k][0])
+        came = lax.ppermute(x, axis, pairs)
+        if k in tasks:
+            names, task = tasks[k]
+            state.update(task(*[state[name] for name in names]))
+        x = x + came
+        if k in due:
+            x = tie(x, state, due[k])
+    return x
+
+
+def shifted(x, axis, step):
     size = lax.axis_size(axis)
-    parts = [lax.ppermute(x, axis, [(i, i ^ mask) for i in range(size)]) for mask in masks]
-    for part in parts:
-        x = x + part
-    return x
-
-
-def total(x, axis):
-    size = lax.axis_size(axis)
-    bit = 1
-    while bit < size:
-        x = exchange(x, axis, [bit])
-        bit *= 2
-    return x
-
-
-def to_neighbours(before, after, axis):
-    size = lax.axis_size(axis)
-    up = [(i, i + 1) for i in range(size - 1)]
-    down = [(j, i) for i, j in up]
-    return lax.ppermute(before, axis, down), lax.ppermute(after, axis, up)
+    pairs = [(i, i + 1) for i in range(size - 1)]
+    return lax.ppermute(x, axis, pairs if step > 0 else [(j, i) for i, j in pairs])
 
 
 def on_device(contacts, masked_bins, chrom_bounds):
@@ -556,20 +516,44 @@
     w, part, keep, top, bottom = pl.pallas_call(
         functools.partial(first_kernel, nd, nb),
         out_shape=(shape((nd, nb), BF16), f(rows, LANES), f(rows, LANES), f(RIM, nb), f(RIM, nb)),
-        in_specs=[SMEM, VMEM, VMEM],
+        in_specs=[HBM] * 3,
         out_specs=(VMEM,) * 5,
         scratch_shapes=[
             pltpu.VMEM((tall, LANES), F32),
             pltpu.VMEM((LANES, span * LANES), F32),
             pltpu.VMEM((LANES, span * LANES), F32),
             pltpu.VMEM((tall, LANES), F32),
+            pltpu.SMEM(chrom_bounds.shape, jnp.int32),
+            pltpu.VMEM((nd, nb), BF16),
+            pltpu.VMEM((1,) + masked_bins.shape, jnp.int32),
+            pltpu.SemaphoreType.DMA((3,)),
         ],
-        compiler_params=params(),
+        compiler_params=params(12),
         name="first_sums",
-    )(chrom_bounds, contacts, masked_bins.reshape(1, -1))
-
-    bottom_rim, top_rim = to_neighbours(top, bottom, "offset")
-    sums = total(total(part, "genome"), "offset")
+    )(*(pltpu.with_memory_space_constraint(a, pltpu.HBM) for a in (chrom_bounds, contacts, masked_bins.reshape(1, -1))))
+
+    def sides(w, above, below):
+        return pl.pallas_call(
+            functools.partial(side_kernel, nd, nb),
+            out_shape=(f(SIDE, total_rows), f(SIDE, total_rows)),
+            in_specs=[VMEM] * 3,
+            out_specs=(VMEM,) * 2,
+            compiler_params=params(16),
+            name="sides",
+        )(w, above, below)
+
+    def first_side(w, above, below):
+        left, right = sides(w, above, below)
+        return dict(right=right, after=shifted(left, "genome", -1))
+
+    state = dict(w=w, top=top, bottom=bottom)
+    tasks = {
+        0: (("bottom",), lambda bottom: dict(above=shifted(bottom, "offset", 1))),
+        1: (("top",), lambda top: dict(below=shifted(top, "offset", -1))),
+        3: (("w", "above", "below"), first_side),
+    }
+    sums = total(part, ("genome", "offset"), state, tasks, {1: ("above",), 2: ("below",)})
+    w = state["w"]
 
     part, bias = pl.pallas_call(
         functools.partial(second_kernel, nd, nb),
@@ -586,19 +570,9 @@
         name="second_sums",
     )(w, sums, keep)
 
-    left, right = pl.pallas_call(
-        functools.partial(side_kernel, nd, nb),
-        out_shape=(f(SIDE, total_rows), f(SIDE, total_rows)),
-        in_specs=[VMEM] * 3,
-        out_specs=(VMEM,) * 2,
-        compiler_params=params(),
-        name="sides",
-    )(w, top_rim, bottom_rim)
-    right_rim, left_rim = to_neighbours(left, right, "genome")
-    strips = []
-    for first, count in ((-5, 5), (0, cols), (cols, 5)):
-        strips.append(
-            pl.pallas_call(
+    def strip(name, first, count):
+        def run(*operands):
+            strips = pl.pallas_call(
                 functools.partial(strip_kernel, nd, nb, first, count),
                 out_shape=shape((count, total_rows, LANES), BF16),
                 in_specs=[VMEM] * 5,
@@ -607,12 +581,33 @@
                     pltpu.VMEM((nb, count * LANES), BF16),
                     pltpu.VMEM((total_rows, count * LANES), F32),
                 ],
-                compiler_params=params(),
+                compiler_params=params(24),
                 name="strips",
-            )(w, top_rim, bottom_rim, left_rim, right_rim)
-        )
-    low, mid, high = strips
-    sums = total(total(part, "genome"), "offset")
+            )(*operands)
+            return {name: strips}
+
+        return ("w", "above", "below") + (("above", "below") if name == "mid" else ("before", "after")), run
+
+    def back(_, right):
+        matrix = pl.pallas_call(
+            functools.partial(unstrip_kernel, nb),
+            out_shape=shape((nb, nb), BF16),
+            out_specs=VMEM,
+            compiler_params=params(8),
+            name="unstrip",
+        )()
+        return dict(perm=matrix, before=shifted(right, "genome", 1))
+
+    tasks = {
+        0: (("keep", "right"), back),
+        2: strip("mid", 0, cols),
+        3: strip("high", cols, 5),
+        4: strip("low", -5, 5),
+    }
+    state["keep"] = keep
+    due = {0: ("perm", "after"), 2: ("mid", "before"), 3: ("high",), 4: ("low",)}
+    sums = total(part, ("genome", "offset"), state, tasks, due)
+    low, high, mid, perm, keep = (state[name] for name in ("low", "high", "mid", "perm", "keep"))
 
     padded = -(-total_rows // LANES) * LANES
     fan_len = fan_rows(nd)
@@ -621,7 +616,7 @@
     near_reach = -(-(near + cols * (LANES - 1) + LANES) // LANES) * LANES
     own, fans, nears, diag = pl.pallas_call(
         functools.partial(third_kernel, nd, nb),
-        out_shape=(f(cols, LANES), f(fan_len, LANES), f(near, LANES), f(8, padded)),
+        out_shape=(f(cols, LANES), f(fan_len, LANES), f(near, LANES), f(2 * padded // LANES, LANES)),
         in_specs=[VMEM] * 4,
         out_specs=(VMEM,) * 4,
         scratch_shapes=[
@@ -635,31 +630,25 @@
         compiler_params=params(),
         name="diagonal_sums",
     )(mid, sums, keep, bias)
-    diag = total(diag, "genome")
-
-    scratch = [
-        pltpu.VMEM((cols + 10, total_rows, LANES), F32),
-        pltpu.VMEM((cols + 8, total_rows, LANES), F32),
-    ] + [pltpu.VMEM((cols, total_rows, LANES), F32)] * 3
-    observed = pl.pallas_call(
-        functools.partial(observed_kernel, nd, nb),
-        out_shape=(f(cols, nd, LANES),) * 5,
-        in_specs=[VMEM] * 5,
-        out_specs=(VMEM,) * 5,
-        scratch_shapes=scratch,
-        compiler_params=params(60),
-        name="observed",
-    )(low, mid, high, nears, fans)
-
+    diag = total(diag, ("genome",))
+
+    chunk = next(c for c in (320, 256, 128, 64, 32) if nd % c == 0)
+    tall = chunk + 2 * RIM
+    twice = lambda tiles: [pltpu.VMEM((tiles, tall, LANES), F32)] * 2
+    whole = lambda a: pl.BlockSpec(a.shape, lambda i: (0,) * a.ndim)
+    operands = (low, mid, high, nears, fans, diag, perm)
     score = pl.pallas_call(
-        functools.partial(score_kernel, nd, nb),
+        functools.partial(filter_kernel, nd, nb, chunk, STEP),
         out_shape=f(nd, nb),
-        in_specs=[VMEM] * 9,
-        out_specs=VMEM,
-        scratch_shapes=[pltpu.VMEM((padded, LANES), F32)] + scratch + [pltpu.VMEM((nb, nb), BF16)],
-        compiler_params=params(60),
+        grid=(nd // chunk,),
+        in_specs=[whole(a) for a in operands],
+        out_specs=pl.BlockSpec((chunk, nb), lambda i: (i, 0)),
+        scratch_shapes=[pltpu.VMEM((padded, LANES), F32)]
+        + twice(cols + 10) + twice(cols + 7) + twice(cols) + twice(cols) + twice(cols) + twice(cols) + twice(cols)
+        ,
+        compiler_params=params(44),
         name="score",
-    )(low, mid, high, diag, *observed)
+    )(*operands)
     return score, own.reshape(nb)
 
 

time: 135 us -> 81.2 us (0.60)
  Pallas kernels: 78.6 us -> 37.6 us
  local copies, waits for them, and re-layouts: 5.95 us -> 0 us
  starting transfers between devices: 34 us -> 28.1 us
    pallas_call x6, Pallas kernels: 67.2 us -> 25.9 us  [the longest x1 18.8 us: on_device(): pl.pallas_call(functools.partial(filter_kernel, nd, nb, chunk, STEP), out...]
    unnamed x16 -> x0, local copies, waits for them, and re-layouts: 5.95 us -> none
    ppermute x17, starting transfers between devices: 34 us -> 28.1 us  [the longest x13 18.4 us: total(): came = lax.ppermute(x, axis, pairs)]
  transfers between devices with their start and end apart: 17 -> 17, of which waited for: 9 -> 9; matrix products, arithmetic and copies ran while one was open for 0% -> 0% of each run, Pallas kernels for 25% -> 12%
where the time goes in v2:
time: 81.2 us; the launch traced here: 80.9 us
  Pallas kernels  37.6 us (46%)
  starting transfers between devices  28.1 us (35%)
  waiting for transfers between devices  14.4 us (18%)
    pallas_call x1, Pallas kernels, on_device(): pl.pallas_call(functools.partial(filter_kernel, nd, nb, chunk, STEP), out...  18.8 us
    ppermute x13, starting transfers between devices, total(): came = lax.ppermute(x, axis, pairs)  18.4 us
    ppermute x13, waiting for transfers between devices, total(): came = lax.ppermute(x, axis, pairs)  14.4 us
    ppermute x4, starting transfers between devices, shifted(): lax.ppermute(x, axis, pairs if step > 0 else [(j, i) for i, j in pairs])  9.64 us
    pallas_call x3, Pallas kernels, run(): pl.pallas_call(functools.partial(strip_kernel, nd, nb, first, count), out...  6.67 us
    pallas_call x1, Pallas kernels, on_device(): pl.pallas_call(functools.partial(third_kernel, nd, nb), out_shape=(f(cols...  5.05 us
    pallas_call x1, Pallas kernels, on_device(): pl.pallas_call(functools.partial(first_kernel, nd, nb), out_shape=(shape(...  3.9 us
    pallas_call x1, Pallas kernels, on_device(): pl.pallas_call(functools.partial(second_kernel, nd, nb), out_shape=(f(row...  2.77 us
  transfers between devices with their start and end apart: 17, of which 9 were waited for; matrix products, arithmetic and copies ran while one was open for 0% of the time, Pallas kernels for 12%

profile of v2, /device:TPU:0, one launch (start us, length us, event | category | flops | bytes accessed | tf_op | source)
XLA Modules:
  0.0 80.9 jit_solution(7724772576019259110)
XLA Ops:
  0.6 3.9 %first_sums.1 = (bf16[1280,640]{1,0:T(8,128)(2,1)S(1)}, f32[40,128]{1,0:T(8,128)S(1)}, f32[40,128]{1,0:T(8,128)S(1)}, f32[16,640]{1,0:T(8,128)S(1)}, f32[16,640]{1,0:T(8,128)S(1)}) custom-call(s32[2]{0:T(128)} %bounds_hbm.1, bf16[1280,640]{1,0:T(8,128)(2,1)} %x_hbm.1, s32[1,128]{1,0:T(1,128)} %bitcast.2), custom_call_target="tpu_custom_call" | custom-call | tf_op jit(solution)/shard_map/first_sums/pallas_call | solution.py:516
  4.5 0.5 collective-permute-start
  5.1 4.5 %collective-permute-start.2 = (f32[16,640]{1,0:T(8,128)S(1)}, f32[16,640]{1,0:T(8,128)S(1)}, u32[]{:S(2)}, u32[]{:S(2)}) collective-permute-start(f32[16,640]{1,0:T(8,128)S(1)} %get-tuple-element.61), channel_id=1, source_target_pairs={{0,1},{1,2},{2,3},{4,5},{5,6},{6,7},{8,9},{9,10},{10,11},{12,13},{... | collective-permute-start | bytes 122888 | tf_op jit(solution)/shard_map/ppermute | solution.py:501
  9.5 0.0 collective-permute-done
  9.6 1.6 %collective-permute-start.1 = (f32[40,128]{1,0:T(8,128)S(1)}, f32[40,128]{1,0:T(8,128)S(1)}, u32[]{:S(2)}, u32[]{:S(2)}) collective-permute-start(f32[40,128]{1,0:T(8,128)S(1)} %add.39), channel_id=1, source_target_pairs={{0,8},{4,12},{8,0},{12,4},{16,24},{20,28},{24,16},{28,20},{1,9},{5... | collective-permute-start | bytes 61448 | tf_op jit(solution)/shard_map/ppermute | solution.py:488
  11.1 1.3 %collective-permute-start.4 = (f32[16,640]{1,0:T(8,128)S(1)}, f32[16,640]{1,0:T(8,128)S(1)}, u32[]{:S(2)}, u32[]{:S(2)}) collective-permute-start(f32[16,640]{1,0:T(8,128)S(1)} %get-tuple-element.63), channel_id=1, source_target_pairs={{1,0},{2,1},{3,2},{5,4},{6,5},{7,6},{9,8},{10,9},{11,10},{13,12},{... | collective-permute-start | bytes 122888 | tf_op jit(solution)/shard_map/ppermute | solution.py:501
  12.4 1.0 %collective-permute-done.1 = f32[40,128]{1,0:T(8,128)S(1)} collective-permute-done((f32[40,128]{1,0:T(8,128)S(1)}, f32[40,128]{1,0:T(8,128)S(1)}, u32[]{:S(2)}, u32[]{:S(2)}) %collective-permute-start.1) | collective-permute-done | bytes 20512 | tf_op jit(solution)/shard_map/ppermute | solution.py:488
  13.4 0.0 collective-permute-done.2.top_ref.left_ref
  13.4 1.6 %collective-permute-start.3 = (f32[40,128]{1,0:T(8,128)S(1)}, f32[40,128]{1,0:T(8,128)S(1)}, u32[]{:S(2)}, u32[]{:S(2)}) collective-permute-start(f32[40,128]{1,0:T(8,128)S(1)} %add.40), channel_id=1, source_target_pairs={{0,16},{4,20},{8,24},{12,28},{16,0},{20,4},{24,8},{28,12},{1,17},{... | collective-permute-start | bytes 61448 | tf_op jit(solution)/shard_map/ppermute | solution.py:488
  15.0 2.3 %collective-permute-done.3 = f32[40,128]{1,0:T(8,128)S(1)} collective-permute-done((f32[40,128]{1,0:T(8,128)S(1)}, f32[40,128]{1,0:T(8,128)S(1)}, u32[]{:S(2)}, u32[]{:S(2)}) %collective-permute-start.3) | collective-permute-done | bytes 20512 | tf_op jit(solution)/shard_map/ppermute | solution.py:488
  17.3 0.0 collective-permute-done.4.bottom_ref.right_ref
  17.3 1.7 %collective-permute-start.5 = (f32[40,128]{1,0:T(8,128)S(1)}, f32[40,128]{1,0:T(8,128)S(1)}, u32[]{:S(2)}, u32[]{:S(2)}) collective-permute-start(f32[40,128]{1,0:T(8,128)S(1)} %add.41), channel_id=1, source_target_pairs={{0,1},{1,0},{2,3},{3,2},{4,5},{5,4},{6,7},{7,6},{8,9},{9,8},{10,11... | collective-permute-start | bytes 61448 | tf_op jit(solution)/shard_map/ppermute | solution.py:488
  19.0 0.3 sides.1
  19.3 1.3 %collective-permute-start.8 = (f32[8,1312]{1,0:T(8,128)S(1)}, f32[8,1312]{1,0:T(8,128)S(1)}, u32[]{:S(2)}, u32[]{:S(2)}) collective-permute-start(f32[8,1312]{1,0:T(8,128)S(1)} %get-tuple-element.76), channel_id=1, source_target_pairs={{4,0},{8,4},{12,8},{16,12},{20,16},{24,20},{28,24},{5,1},{9,5},{13... | collective-permute-start | bytes 125960 | tf_op jit(solution)/shard_map/ppermute | solution.py:501
  20.6 0.5 collective-permute-done.5
  21.1 2.7 %collective-permute-start.6 = (f32[40,128]{1,0:T(8,128)S(1)}, f32[40,128]{1,0:T(8,128)S(1)}, u32[]{:S(2)}, u32[]{:S(2)}) collective-permute-start(f32[40,128]{1,0:T(8,128)S(1)} %add.42), channel_id=1, source_target_pairs={{0,2},{1,3},{2,0},{3,1},{4,6},{5,7},{6,4},{7,5},{8,10},{9,11},{10,... | collective-permute-start | bytes 61448 | tf_op jit(solution)/shard_map/ppermute | solution.py:488
  23.8 2.0 %collective-permute-done.6 = f32[40,128]{1,0:T(8,128)S(1)} collective-permute-done((f32[40,128]{1,0:T(8,128)S(1)}, f32[40,128]{1,0:T(8,128)S(1)}, u32[]{:S(2)}, u32[]{:S(2)}) %collective-permute-start.6) | collective-permute-done | bytes 20512 | tf_op jit(solution)/shard_map/ppermute | solution.py:488
  25.8 2.8 %second_sums.1 = (f32[40,128]{1,0:T(8,128)S(1)}, f32[40,128]{1,0:T(8,128)S(1)}) custom-call(bf16[1280,640]{1,0:T(8,128)(2,1)S(1)} %get-tuple-element.94.w_ref, f32[40,128]{1,0:T(8,128)S(1)} %add.43.sums_ref, f32[40,128]{1,0:T(8,128)S(1)} %get-tuple-element.103.keep_ref), custom_call_target="tpu_custom_call" | custom-call | tf_op jit(solution)/shard_map/second_sums/pallas_call | solution.py:558
  28.6 0.1 collective-permute-start.7
  28.7 2.6 %collective-permute-start.11 = (f32[8,1312]{1,0:T(8,128)S(1)}, f32[8,1312]{1,0:T(8,128)S(1)}, u32[]{:S(2)}, u32[]{:S(2)}) collective-permute-start(f32[8,1312]{1,0:T(8,128)S(1)} %get-tuple-element.82), channel_id=1, source_target_pairs={{0,4},{4,8},{8,12},{12,16},{16,20},{20,24},{24,28},{1,5},{5,9},{9,... | collective-permute-start | bytes 125960 | tf_op jit(solution)/shard_map/ppermute | solution.py:501
  31.3 0.2 unstrip.1.perm_ref
  31.4 0.0 collective-permute-done.7
  31.4 0.0 collective-permute-done.8.right_ref
  31.5 1.7 %collective-permute-start.9 = (f32[40,128]{1,0:T(8,128)S(1)}, f32[40,128]{1,0:T(8,128)S(1)}, u32[]{:S(2)}, u32[]{:S(2)}) collective-permute-start(f32[40,128]{1,0:T(8,128)S(1)} %add.44), channel_id=1, source_target_pairs={{0,8},{4,12},{8,0},{12,4},{16,24},{20,28},{24,16},{28,20},{1,9},{5... | collective-permute-start | bytes 61448 | tf_op jit(solution)/shard_map/ppermute | solution.py:488
  33.1 2.3 %collective-permute-done.9 = f32[40,128]{1,0:T(8,128)S(1)} collective-permute-done((f32[40,128]{1,0:T(8,128)S(1)}, f32[40,128]{1,0:T(8,128)S(1)}, u32[]{:S(2)}, u32[]{:S(2)}) %collective-permute-start.9) | collective-permute-done | bytes 20512 | tf_op jit(solution)/shard_map/ppermute | solution.py:488
  35.4 1.7 %collective-permute-start.10 = (f32[40,128]{1,0:T(8,128)S(1)}, f32[40,128]{1,0:T(8,128)S(1)}, u32[]{:S(2)}, u32[]{:S(2)}) collective-permute-start(f32[40,128]{1,0:T(8,128)S(1)} %add.45), channel_id=1, source_target_pairs={{0,16},{4,20},{8,24},{12,28},{16,0},{20,4},{24,8},{28,12},{1,17},{... | collective-permute-start | bytes 61448 | tf_op jit(solution)/shard_map/ppermute | solution.py:488
  37.2 2.0 %strips.3.mid_ref = bf16[5,1312,128]{2,1,0:T(8,128)(2,1)S(1)} custom-call(bf16[1280,640]{1,0:T(8,128)(2,1)S(1)} %get-tuple-element.94.w_ref, f32[16,640]{1,0:T(8,128)S(1)} %collective-permute-done.2.top_ref.left_ref, f32[16,640]{1,0:T(8,128)S(1)} %collective-permute-done.4.bottom_ref.right_ref, f32[16,640]{1,0:T(8,128)S(1)} %collective-permute-done.2.top_ref.left_ref, ...), custom_call_target="tpu_custom_call" | custom-call | tf_op jit(solution)/shard_map/strips/pallas_call | solution.py:575
  39.1 0.1 collective-permute-done.10
  39.2 0.0 collective-permute-done.11.left_ref
  39.2 1.7 %collective-permute-start.12 = (f32[40,128]{1,0:T(8,128)S(1)}, f32[40,128]{1,0:T(8,128)S(1)}, u32[]{:S(2)}, u32[]{:S(2)}) collective-permute-start(f32[40,128]{1,0:T(8,128)S(1)} %add.46), channel_id=1, source_target_pairs={{0,1},{1,0},{2,3},{3,2},{4,5},{5,4},{6,7},{7,6},{8,9},{9,8},{10,11... | collective-permute-start | bytes 61448 | tf_op jit(solution)/shard_map/ppermute | solution.py:488
  41.0 2.3 %strips.4.high_ref = bf16[5,1312,128]{2,1,0:T(8,128)(2,1)S(1)} custom-call(bf16[1280,640]{1,0:T(8,128)(2,1)S(1)} %get-tuple-element.94.w_ref, f32[16,640]{1,0:T(8,128)S(1)} %collective-permute-done.2.top_ref.left_ref, f32[16,640]{1,0:T(8,128)S(1)} %collective-permute-done.4.bottom_ref.right_ref, f32[8,1312]{1,0:T(8,128)S(1)} %collective-permute-done.11.left_ref, ...), custom_call_target="tpu_custom_call" | custom-call | tf_op jit(solution)/shard_map/strips/pallas_call | solution.py:575
  43.3 0.0 collective-permute-done.12
  43.4 2.8 %collective-permute-start.13 = (f32[40,128]{1,0:T(8,128)S(1)}, f32[40,128]{1,0:T(8,128)S(1)}, u32[]{:S(2)}, u32[]{:S(2)}) collective-permute-start(f32[40,128]{1,0:T(8,128)S(1)} %add.47), channel_id=1, source_target_pairs={{0,2},{1,3},{2,0},{3,1},{4,6},{5,7},{6,4},{7,5},{8,10},{9,11},{10,... | collective-permute-start | bytes 61448 | tf_op jit(solution)/shard_map/ppermute | solution.py:488
  46.1 2.3 %strips.5.low_ref = bf16[5,1312,128]{2,1,0:T(8,128)(2,1)S(1)} custom-call(bf16[1280,640]{1,0:T(8,128)(2,1)S(1)} %get-tuple-element.94.w_ref, f32[16,640]{1,0:T(8,128)S(1)} %collective-permute-done.2.top_ref.left_ref, f32[16,640]{1,0:T(8,128)S(1)} %collective-permute-done.4.bottom_ref.right_ref, f32[8,1312]{1,0:T(8,128)S(1)} %collective-permute-done.11.left_ref, ...), custom_call_target="tpu_custom_call" | custom-call | tf_op jit(solution)/shard_map/strips/pallas_call | solution.py:575
  48.5 0.0 collective-permute-done.13
  48.5 5.1 %diagonal_sums.1 = (f32[5,128]{1,0:T(8,128)}, f32[1344,128]{1,0:T(8,128)S(1)}, f32[24,128]{1,0:T(8,128)S(1)}, f32[22,128]{1,0:T(8,128)S(1)}) custom-call(bf16[5,1312,128]{2,1,0:T(8,128)(2,1)S(1)} %strips.3.mid_ref, f32[40,128]{1,0:T(8,128)S(1)} %add.48.sums_ref, f32[40,128]{1,0:T(8,128)S(1)} %get-tuple-element.103.keep_ref, ...), custom_call_target="tpu_custom_call" | custom-call | tf_op jit(solution)/shard_map/diagonal_sums/pallas_call | solution.py:617
  53.6 0.0 collective-permute-start.14
  53.6 1.2 %collective-permute-done.14 = f32[22,128]{1,0:T(8,128)S(1)} collective-permute-done((f32[22,128]{1,0:T(8,128)S(1)}, f32[22,128]{1,0:T(8,128)S(1)}, u32[]{:S(2)}, u32[]{:S(2)}) %collective-permute-start.14) | collective-permute-done | bytes 11296 | tf_op jit(solution)/shard_map/ppermute | solution.py:488
  54.7 0.9 %collective-permute-start.15 = (f32[22,128]{1,0:T(8,128)S(1)}, f32[22,128]{1,0:T(8,128)S(1)}, u32[]{:S(2)}, u32[]{:S(2)}) collective-permute-start(f32[22,128]{1,0:T(8,128)S(1)} %add.49), channel_id=1, source_target_pairs={{0,8},{4,12},{8,0},{12,4},{16,24},{20,28},{24,16},{28,20},{1,9},{5... | collective-permute-start | bytes 33800 | tf_op jit(solution)/shard_map/ppermute | solution.py:488
  55.7 2.8 %collective-permute-done.15 = f32[22,128]{1,0:T(8,128)S(1)} collective-permute-done((f32[22,128]{1,0:T(8,128)S(1)}, f32[22,128]{1,0:T(8,128)S(1)}, u32[]{:S(2)}, u32[]{:S(2)}) %collective-permute-start.15) | collective-permute-done | bytes 11296 | tf_op jit(solution)/shard_map/ppermute | solution.py:488
  58.4 1.5 %collective-permute-start.16 = (f32[22,128]{1,0:T(8,128)S(1)}, f32[22,128]{1,0:T(8,128)S(1)}, u32[]{:S(2)}, u32[]{:S(2)}) collective-permute-start(f32[22,128]{1,0:T(8,128)S(1)} %add.50), channel_id=1, source_target_pairs={{0,16},{4,20},{8,24},{12,28},{16,0},{20,4},{24,8},{28,12},{1,17},{... | collective-permute-start | bytes 33800 | tf_op jit(solution)/shard_map/ppermute | solution.py:488
  59.9 2.2 %collective-permute-done.16 = f32[22,128]{1,0:T(8,128)S(1)} collective-permute-done((f32[22,128]{1,0:T(8,128)S(1)}, f32[22,128]{1,0:T(8,128)S(1)}, u32[]{:S(2)}, u32[]{:S(2)}) %collective-permute-start.16) | collective-permute-done | bytes 11296 | tf_op jit(solution)/shard_map/ppermute | solution.py:488
  62.1 18.8 %score.1 = f32[1280,640]{1,0:T(8,128)} custom-call(bf16[5,1312,128]{2,1,0:T(8,128)(2,1)S(1)} %strips.5.low_ref, bf16[5,1312,128]{2,1,0:T(8,128)(2,1)S(1)} %strips.3.mid_ref, bf16[5,1312,128]{2,1,0:T(8,128)(2,1)S(1)} %strips.4.high_ref, f32[24,128]{1,0:T(8,128)S(1)} %get-tuple-element.105.near_ref, f32[1344,128]{1,0:T(8,128)S(1)} %get-tuple-element.106.fan_ref, ...), custom_call_target="tpu_custom_call" | custom-call | tf_op jit(solution)/shard_map/score/pallas_call | solution.py:640
  (13 shorter events, 0.1 us)
Async XLA Ops:
  4.5 5.0 %collective-permute-start = (f32[40,128]{1,0:T(8,128)S(1)}, f32[40,128]{1,0:T(8,128)S(1)}, u32[]{:S(2)}, u32[]{:S(2)}) collective-permute-start(f32[40,128]{1,0:T(8,128)S(1)} %get-tuple-element.58), channel_id=1, source_target_pairs={{0,4},{4,0},{8,12},{12,8},{16,20},{20,16},{24,28},{28,24},{1,5},{5... | collective-permute-start | bytes 61448 | tf_op jit(solution)/shard_map/ppermute | solution.py:488
  5.1 8.4 %collective-permute-start.2 = (f32[16,640]{1,0:T(8,128)S(1)}, f32[16,640]{1,0:T(8,128)S(1)}, u32[]{:S(2)}, u32[]{:S(2)}) collective-permute-start(f32[16,640]{1,0:T(8,128)S(1)} %get-tuple-element.61), channel_id=1, source_target_pairs={{0,1},{1,2},{2,3},{4,5},{5,6},{6,7},{8,9},{9,10},{10,11},{12,13},{... | collective-permute-start | bytes 122888 | tf_op jit(solution)/shard_map/ppermute | solution.py:501
  9.6 3.8 %collective-permute-start.1 = (f32[40,128]{1,0:T(8,128)S(1)}, f32[40,128]{1,0:T(8,128)S(1)}, u32[]{:S(2)}, u32[]{:S(2)}) collective-permute-start(f32[40,128]{1,0:T(8,128)S(1)} %add.39), channel_id=1, source_target_pairs={{0,8},{4,12},{8,0},{12,4},{16,24},{20,28},{24,16},{28,20},{1,9},{5... | collective-permute-start | bytes 61448 | tf_op jit(solution)/shard_map/ppermute | solution.py:488
  11.1 6.2 %collective-permute-start.4 = (f32[16,640]{1,0:T(8,128)S(1)}, f32[16,640]{1,0:T(8,128)S(1)}, u32[]{:S(2)}, u32[]{:S(2)}) collective-permute-start(f32[16,640]{1,0:T(8,128)S(1)} %get-tuple-element.63), channel_id=1, source_target_pairs={{1,0},{2,1},{3,2},{5,4},{6,5},{7,6},{9,8},{10,9},{11,10},{13,12},{... | collective-permute-start | bytes 122888 | tf_op jit(solution)/shard_map/ppermute | solution.py:501
  13.4 3.8 %collective-permute-start.3 = (f32[40,128]{1,0:T(8,128)S(1)}, f32[40,128]{1,0:T(8,128)S(1)}, u32[]{:S(2)}, u32[]{:S(2)}) collective-permute-start(f32[40,128]{1,0:T(8,128)S(1)} %add.40), channel_id=1, source_target_pairs={{0,16},{4,20},{8,24},{12,28},{16,0},{20,4},{24,8},{28,12},{1,17},{... | collective-permute-start | bytes 61448 | tf_op jit(solution)/shard_map/ppermute | solution.py:488
  17.3 3.8 %collective-permute-start.5 = (f32[40,128]{1,0:T(8,128)S(1)}, f32[40,128]{1,0:T(8,128)S(1)}, u32[]{:S(2)}, u32[]{:S(2)}) collective-permute-start(f32[40,128]{1,0:T(8,128)S(1)} %add.41), channel_id=1, source_target_pairs={{0,1},{1,0},{2,3},{3,2},{4,5},{5,4},{6,7},{7,6},{8,9},{9,8},{10,11... | collective-permute-start | bytes 61448 | tf_op jit(solution)/shard_map/ppermute | solution.py:488
  19.3 12.2 %collective-permute-start.8 = (f32[8,1312]{1,0:T(8,128)S(1)}, f32[8,1312]{1,0:T(8,128)S(1)}, u32[]{:S(2)}, u32[]{:S(2)}) collective-permute-start(f32[8,1312]{1,0:T(8,128)S(1)} %get-tuple-element.76), channel_id=1, source_target_pairs={{4,0},{8,4},{12,8},{16,12},{20,16},{24,20},{28,24},{5,1},{9,5},{13... | collective-permute-start | bytes 125960 | tf_op jit(solution)/shard_map/ppermute | solution.py:501
  21.1 4.7 %collective-permute-start.6 = (f32[40,128]{1,0:T(8,128)S(1)}, f32[40,128]{1,0:T(8,128)S(1)}, u32[]{:S(2)}, u32[]{:S(2)}) collective-permute-start(f32[40,128]{1,0:T(8,128)S(1)} %add.42), channel_id=1, source_target_pairs={{0,2},{1,3},{2,0},{3,1},{4,6},{5,7},{6,4},{7,5},{8,10},{9,11},{10,... | collective-permute-start | bytes 61448 | tf_op jit(solution)/shard_map/ppermute | solution.py:488
  28.6 2.8 %collective-permute-start.7 = (f32[40,128]{1,0:T(8,128)S(1)}, f32[40,128]{1,0:T(8,128)S(1)}, u32[]{:S(2)}, u32[]{:S(2)}) collective-permute-start(f32[40,128]{1,0:T(8,128)S(1)} %get-tuple-element.75), channel_id=1, source_target_pairs={{0,4},{4,0},{8,12},{12,8},{16,20},{20,16},{24,28},{28,24},{1,5},{5... | collective-permute-start | bytes 61448 | tf_op jit(solution)/shard_map/ppermute | solution.py:488
  28.7 10.6 %collective-permute-start.11 = (f32[8,1312]{1,0:T(8,128)S(1)}, f32[8,1312]{1,0:T(8,128)S(1)}, u32[]{:S(2)}, u32[]{:S(2)}) collective-permute-start(f32[8,1312]{1,0:T(8,128)S(1)} %get-tuple-element.82), channel_id=1, source_target_pairs={{0,4},{4,8},{8,12},{12,16},{16,20},{20,24},{24,28},{1,5},{5,9},{9,... | collective-permute-start | bytes 125960 | tf_op jit(solution)/shard_map/ppermute | solution.py:501
  31.5 4.0 %collective-permute-start.9 = (f32[40,128]{1,0:T(8,128)S(1)}, f32[40,128]{1,0:T(8,128)S(1)}, u32[]{:S(2)}, u32[]{:S(2)}) collective-permute-start(f32[40,128]{1,0:T(8,128)S(1)} %add.44), channel_id=1, source_target_pairs={{0,8},{4,12},{8,0},{12,4},{16,24},{20,28},{24,16},{28,20},{1,9},{5... | collective-permute-start | bytes 61448 | tf_op jit(solution)/shard_map/ppermute | solution.py:488
  35.4 3.8 %collective-permute-start.10 = (f32[40,128]{1,0:T(8,128)S(1)}, f32[40,128]{1,0:T(8,128)S(1)}, u32[]{:S(2)}, u32[]{:S(2)}) collective-permute-start(f32[40,128]{1,0:T(8,128)S(1)} %add.45), channel_id=1, source_target_pairs={{0,16},{4,20},{8,24},{12,28},{16,0},{20,4},{24,8},{28,12},{1,17},{... | collective-permute-start | bytes 61448 | tf_op jit(solution)/shard_map/ppermute | solution.py:488
  39.2 4.1 %collective-permute-start.12 = (f32[40,128]{1,0:T(8,128)S(1)}, f32[40,128]{1,0:T(8,128)S(1)}, u32[]{:S(2)}, u32[]{:S(2)}) collective-permute-start(f32[40,128]{1,0:T(8,128)S(1)} %add.46), channel_id=1, source_target_pairs={{0,1},{1,0},{2,3},{3,2},{4,5},{5,4},{6,7},{7,6},{8,9},{9,8},{10,11... | collective-permute-start | bytes 61448 | tf_op jit(solution)/shard_map/ppermute | solution.py:488
  43.4 5.1 %collective-permute-start.13 = (f32[40,128]{1,0:T(8,128)S(1)}, f32[40,128]{1,0:T(8,128)S(1)}, u32[]{:S(2)}, u32[]{:S(2)}) collective-permute-start(f32[40,128]{1,0:T(8,128)S(1)} %add.47), channel_id=1, source_target_pairs={{0,2},{1,3},{2,0},{3,1},{4,6},{5,7},{6,4},{7,5},{8,10},{9,11},{10,... | collective-permute-start | bytes 61448 | tf_op jit(solution)/shard_map/ppermute | solution.py:488
  53.6 1.2 %collective-permute-start.14 = (f32[22,128]{1,0:T(8,128)S(1)}, f32[22,128]{1,0:T(8,128)S(1)}, u32[]{:S(2)}, u32[]{:S(2)}) collective-permute-start(f32[22,128]{1,0:T(8,128)S(1)} %get-tuple-element.107), channel_id=1, source_target_pairs={{0,4},{4,0},{8,12},{12,8},{16,20},{20,16},{24,28},{28,24},{1,5},{5... | collective-permute-start | bytes 33800 | tf_op jit(solution)/shard_map/ppermute | solution.py:488
  54.7 3.7 %collective-permute-start.15 = (f32[22,128]{1,0:T(8,128)S(1)}, f32[22,128]{1,0:T(8,128)S(1)}, u32[]{:S(2)}, u32[]{:S(2)}) collective-permute-start(f32[22,128]{1,0:T(8,128)S(1)} %add.49), channel_id=1, source_target_pairs={{0,8},{4,12},{8,0},{12,4},{16,24},{20,28},{24,16},{28,20},{1,9},{5... | collective-permute-start | bytes 33800 | tf_op jit(solution)/shard_map/ppermute | solution.py:488
  58.4 3.7 %collective-permute-start.16 = (f32[22,128]{1,0:T(8,128)S(1)}, f32[22,128]{1,0:T(8,128)S(1)}, u32[]{:S(2)}, u32[]{:S(2)}) collective-permute-start(f32[22,128]{1,0:T(8,128)S(1)} %add.50), channel_id=1, source_target_pairs={{0,16},{4,20},{8,24},{12,28},{16,0},{20,4},{24,8},{28,12},{1,17},{... | collective-permute-start | bytes 33800 | tf_op jit(solution)/shard_map/ppermute | solution.py:488

commit v3 on v2

--- a/solution.py
+++ b/solution.py
@@ -1,4 +1,5 @@
 import functools
+import math
 
 import jax
 import jax.numpy as jnp
@@ -8,7 +9,7 @@
 from jax.sharding import PartitionSpec as P
 
 RIM = 16
-STEP = 64
+STEP = 176
 SIDE = 8
 LANES = 128
 F32 = jnp.float32
@@ -272,13 +273,15 @@
         out_ref[s * LANES : (s + 1) * LANES, :] = (lane == row * stride + s).astype(F32).astype(BF16)
 
 
-def column(row, out_ref, at):
+def columns(rows, out_ref):
     eye = iota((LANES, LANES), 0) == iota((LANES, LANES), 1)
-    diag = jnp.where(eye, jnp.broadcast_to(row, (LANES, LANES)), 0.0)
-    value = jnp.dot(
-        jnp.concatenate(split3(diag), axis=1), jnp.ones((3 * LANES, LANES), BF16), preferred_element_type=F32
+    blocks = []
+    for row in rows:
+        parts = [jnp.where(eye, jnp.broadcast_to(part.astype(F32), (LANES, LANES)), 0.0) for part in split3(row)]
+        blocks.append(jnp.concatenate([part.astype(BF16) for part in parts], axis=1))
+    out_ref[...] = jnp.dot(
+        jnp.concatenate(blocks, axis=0), jnp.ones((3 * LANES, LANES), BF16), preferred_element_type=F32
     )
-    out_ref[at : at + LANES, :] = value
 
 
 def fan(col_ref, other_ref, start, rows, stride, out_ref):
@@ -290,21 +293,13 @@
         need = -(-need // 8) * 8
         if bit == 1:
             target = out_ref
-        step = 32 if need >= 32 else 8
-
         def move(at, size, source=source, target=target, offset=offset, bit=bit):
             low = source[pl.ds(offset + at, size), :]
             high = source[pl.ds(offset + at + stride * bit, size), :]
             odd = (iota((size, LANES), 1) & bit) > 0
             target[pl.ds(at, size), :] = jnp.where(odd, high, low)
 
-        def body(i, _, move=move):
-            move(pl.multiple_of(i * 32, 32), 32)
-            return 0
-
-        lax.fori_loop(0, need // 32, body, 0)
-        for at in range(need // 32 * 32, need, 8):
-            move(at, 8)
+        over(0, need, 208 if need > 208 else need, move)
         source, target, offset = target, source, 0
 
 
@@ -324,33 +319,29 @@
     for c in range(cols):
         own_ref[c : c + 1, :] = window_ref[pl.ds(8 + row_own + c, 1), :]
     tiles = col_ref.shape[0] // LANES
-    for t in range(tiles):
-        column(window_ref[pl.ds(7 + row_partner + t, 1), :], col_ref, t * LANES)
+    columns([window_ref[pl.ds(7 + row_partner + t, 1), :] for t in range(tiles)], col_ref)
     start = LANES - RIM - 8
     if nd % LANES:
         start = start + lane0
     fan(col_ref, other_ref, start, fan_rows(nd), stride, fan_ref)
-    for t in range(ncol_ref.shape[0] // LANES):
-        column(window_ref[pl.ds(7 + row_own + t, 1), :], ncol_ref, t * LANES)
+    columns([window_ref[pl.ds(7 + row_own + t, 1), :] for t in range(ncol_ref.shape[0] // LANES)], ncol_ref)
     fan(ncol_ref, nother_ref, LANES - 8, near_ref.shape[0], stride, near_ref)
     total_rows = nd + 2 * RIM
-    step = 32
-
-    def body(i, _):
-        r0 = pl.multiple_of(i * step, step)
+
+    def add(r0, size):
         total, count = None, None
         for s in range(stride):
-            w = mid_ref[s, pl.ds(r0, step), :].astype(F32)
-            b = w * jnp.broadcast_to(near_ref[8 + s : 9 + s, :], (step, LANES)) * fan_ref[pl.ds(r0 + 8 + s, step), :]
+            w = mid_ref[s, pl.ds(r0, size), :].astype(F32)
+            near = jnp.broadcast_to(near_ref[8 + s : 9 + s, :], (size, LANES))
+            b = w * near * fan_ref[pl.ds(r0 + 8 + s, size), :]
             v = jnp.where(w > 0.0, 1.0, 0.0)
             total = b if total is None else total + b
             count = v if count is None else count + v
         hi, mid, low = split3(total)
         for k, part in enumerate((hi, mid, low, count.astype(BF16))):
-            total_ref[pl.ds(r0, step), k * LANES : (k + 1) * LANES] = part
-        return 0
-
-    lax.fori_loop(0, total_rows // step, body, 0)
+            total_ref[pl.ds(r0, size), k * LANES : (k + 1) * LANES] = part
+
+    over(0, total_rows, 160, add)
     ones = jnp.ones((8, 3 * LANES), BF16)
     padded = total_ref.shape[0]
     tiles = padded // LANES
@@ -368,7 +359,7 @@
     if steps > 0:
 
         def body(i, _):
-            run(pl.multiple_of(i * step + start, 8), step)
+            run(pl.multiple_of(i * step + start, math.gcd(start, step)), step)
             return 0
 
         lax.fori_loop(0, steps, body, 0)
@@ -376,10 +367,7 @@
         run(start + steps * step, count % step)
 
 
-def filter_kernel(nd, nb, chunk, step, low_ref, mid_ref, high_ref, near_ref, fan_ref, diag_ref, perm_ref, out_ref,
-                  col_ref, xo_ref, xe_ref, po_ref, pe_ref, ho_ref, he_ref, uo_ref, ue_ref,
-                  lo_ref, le_ref, wo_ref, we_ref, to_ref, te_ref):
-    stride = nb // LANES
+def strips_of(stride, low_ref, mid_ref, high_ref):
     strips = {}
     for s in range(-5, 0):
         strips[s] = (low_ref, s + 5)
@@ -387,86 +375,129 @@
         strips[s] = (mid_ref, s)
     for s in range(stride, stride + 5):
         strips[s] = (high_ref, s - stride)
-    base = pl.multiple_of(pl.program_id(0) * chunk, 32)
-
-    @pl.when(pl.program_id(0) == 0)
-    def _():
-        tiles = diag_ref.shape[0] // 2
-        expected = diag_ref[:tiles, :] / jnp.maximum(diag_ref[tiles:, :], 1.0)
-        for t in range(tiles):
-            column(expected[t : t + 1, :], col_ref, t * LANES)
+    return strips
+
+
+def shift_sums(chunk, stride, step, x, p, h, u, l, w, t):
+    def pairs(r0, size):
+        for s in range(-4, stride + 3):
+            p[s + 4, pl.ds(r0, size), :] = x[s + 5, pl.ds(r0, size), :] + x[s + 6, pl.ds(r0 - 1, size), :]
+
+    over(8, chunk + 24, step, pairs)
+
+    def mix(r0, size):
+        for s in range(stride):
+            here = (s, pl.ds(r0, size), slice(None))
+            at = lambda ref, k, shift: ref[k, pl.ds(r0 + shift, size), :]
+            hp = at(p, s + 7, -3) + at(x, s + 10, -5)
+            hm = at(p, s, 4) + at(x, s, 5)
+            lp = hp + at(p, s + 5, -1)
+            h[here] = hp
+            u[here] = hp + hm
+            l[here] = lp
+            w[here] = lp + (hm + at(p, s + 2, 2))
+            t[here] = at(p, s + 4, 0) + at(x, s + 4, 1)
+
+    over(8, chunk + 16, step, mix)
+
+    def runs(r0, size):
+        for s in range(stride):
+            for ref in (w, t):
+                at = lambda shift: ref[s, pl.ds(r0 + shift, size), :]
+                ref[s, pl.ds(r0, size), :] = at(0) + at(1) + at(2)
+
+    over(8, chunk + 16, step, runs)
+
+
+def four_sums(s, r0, size, h, u, l, w, t):
+    at = lambda ref, shift: ref[s, pl.ds(r0 + shift, size), :]
+    below, above = at(u, -1), at(u, 1)
+    donut = (at(w, -5) + at(w, 3)) + ((at(u, -2) + below) + (above + at(u, 2)))
+    lower = (at(l, -5) + at(l, -4) + at(l, -3)) + (at(h, -2) + at(h, -1))
+    return donut, lower, at(t, -5) + at(t, 3), below + at(u, 0) + above
+
+
+def observed_kernel(nd, nb, chunk, step, base, low_ref, mid_ref, high_ref, near_ref, fan_ref, out_ref, x_ref, *refs):
+    stride = nb // LANES
+    strips = strips_of(stride, low_ref, mid_ref, high_ref)
 
     def fill(r0, size):
-        e = col_ref[pl.ds(base + r0, size), :]
         for s, (ref, k) in strips.items():
             w = ref[k, pl.ds(base + r0, size), :].astype(F32)
             near = jnp.broadcast_to(near_ref[8 + s : 9 + s, :], (size, LANES))
-            xo_ref[s + 5, pl.ds(r0, size), :] = w * near * fan_ref[pl.ds(base + r0 + 8 + s, size), :]
-            xe_ref[s + 5, pl.ds(r0, size), :] = jnp.where(w > 0.0, e, 0.0)
-
-    over(0, chunk + 2 * RIM, 32, fill)
-    observed = (xo_ref, po_ref, ho_ref, uo_ref, lo_ref, wo_ref, to_ref)
-    expected = (xe_ref, pe_ref, he_ref, ue_ref, le_ref, we_ref, te_ref)
-
-    def pairs(r0, size):
-        for s in range(-4, stride + 3):
-            for x, p, *_ in (observed, expected):
-                p[s + 4, pl.ds(r0, size), :] = x[s + 5, pl.ds(r0, size), :] + x[s + 6, pl.ds(r0 - 1, size), :]
-
-    over(8, chunk + 24, step, pairs)
-
-    def mix(r0, size):
+            x_ref[s + 5, pl.ds(r0, size), :] = w * near * fan_ref[pl.ds(base + r0 + 8 + s, size), :]
+
+    over(0, chunk + 2 * RIM, step, fill)
+    shift_sums(chunk, stride, step, x_ref, *refs)
+
+    def emit(r0, size):
         for s in range(stride):
-            for x, p, h, u, l, w, t in (observed, expected):
-                here = (s, pl.ds(r0, size), slice(None))
-                at = lambda ref, k, shift: ref[k, pl.ds(r0 + shift, size), :]
-                hp = at(p, s + 7, -3) + at(x, s + 10, -5)
-                hm = at(p, s, 4) + at(x, s, 5)
-                lp = hp + at(p, s + 5, -1)
-                h[here] = hp
-                u[here] = hp + hm
-                l[here] = lp
-                w[here] = lp + (hm + at(p, s + 2, 2))
-                t[here] = at(p, s + 4, 0) + at(x, s + 4, 1)
-
-    over(8, chunk + 16, step, mix)
-
-    def runs(r0, size):
-        for s in range(stride):
-            for _, _, _, _, _, w, t in (observed, expected):
-                for ref in (w, t):
-                    at = lambda shift: ref[s, pl.ds(r0 + shift, size), :]
-                    ref[s, pl.ds(r0, size), :] = at(0) + at(1) + at(2)
-
-    over(8, chunk + 16, step, runs)
-
-    def score(r0, size):
+            sums = four_sums(s, r0, size, *refs[1:])
+            for k, value in enumerate(sums + (x_ref[s + 5, pl.ds(r0, size), :],)):
+                out_ref[5 * s + k, pl.ds(r0 - RIM, size), :] = value
+
+    over(RIM, chunk, step, emit)
+
+
+def score_kernel(nd, nb, chunk, step, low_ref, mid_ref, high_ref, diag_ref, perm_ref, *rest):
+    stride = nb // LANES
+    count = nd // chunk
+    seen_refs, out_hbm = rest[:count], rest[count]
+    col_ref, out_ref, sems, x_ref = rest[count + 1 : count + 5]
+    refs = rest[count + 5 :]
+    strips = strips_of(stride, low_ref, mid_ref, high_ref)
+    tiles = diag_ref.shape[0] // 2
+    expected = diag_ref[:tiles, :] / jnp.maximum(diag_ref[tiles:, :], 1.0)
+    columns([expected[t : t + 1, :] for t in range(tiles)], col_ref)
+
+    def leave(i):
+        here = (pl.ds(pl.multiple_of(i * chunk, 32), chunk), slice(None))
+        return pltpu.make_async_copy(out_ref.at[here], out_hbm.at[here], sems.at[i])
+
+    def score(seen_ref, base, r0, size):
         e = col_ref[pl.ds(base + r0, size), :]
         inverse = 1.0 / e
         for s in range(stride):
-            sums = []
-            for x, p, h, u, l, w, t in (observed, expected):
-                at = lambda ref, shift: ref[s, pl.ds(r0 + shift, size), :]
-                below, above = at(u, -1), at(u, 1)
-                donut = (at(w, -5) + at(w, 3)) + ((at(u, -2) + below) + (above + at(u, 2)))
-                lower = (at(l, -5) + at(l, -4) + at(l, -3)) + (at(h, -2) + at(h, -1))
-                sums.append((donut, lower, at(t, -5) + at(t, 3), below + at(u, 0) + above))
+            sums = four_sums(s, r0, size, *refs[1:])
+            seen = [seen_ref[5 * s + k, pl.ds(r0 - RIM, size), :] for k in range(5)]
             least = None
-            for seen, hoped in zip(*sums):
-                ratio = (hoped + e) / (seen + e)
+            for k in range(4):
+                ratio = (sums[k] + e) / (seen[k] + e)
                 least = ratio if least is None else jnp.minimum(least, ratio)
-            value = least * (xo_ref[s + 5, pl.ds(r0, size), :] * inverse)
-            value = jnp.where(xe_ref[s + 5, pl.ds(r0, size), :] > 0.0, value, 0.0)
+            value = least * (seen[4] * inverse)
+            value = jnp.where(x_ref[s + 5, pl.ds(r0, size), :] > 0.0, value, 0.0)
             hi = value.astype(BF16)
             low = (value - hi.astype(F32)).astype(BF16)
             perm = perm_ref[s * LANES : (s + 1) * LANES, :]
             placed = jnp.dot(
                 jnp.concatenate([hi, low], axis=1), jnp.concatenate([perm, perm], axis=0), preferred_element_type=F32
             )
-            here = pl.ds(r0 - RIM, size)
+            here = pl.ds(base + r0 - RIM, size)
             out_ref[here, :] = placed if s == 0 else out_ref[here, :] + placed
 
-    over(RIM, chunk, chunk // 2, score)
+    def body(i, _):
+        base = pl.multiple_of(i * chunk, 32)
+
+        def fill(r0, size):
+            e = col_ref[pl.ds(base + r0, size), :]
+            for s, (ref, k) in strips.items():
+                w = ref[k, pl.ds(base + r0, size), :].astype(F32)
+                x_ref[s + 5, pl.ds(r0, size), :] = jnp.where(w > 0.0, e, 0.0)
+
+        over(0, chunk + 2 * RIM, step, fill)
+        shift_sums(chunk, stride, step, x_ref, *refs)
+        for c in range(count):
+
+            @pl.when(i == c)
+            def _():
+                over(RIM, chunk, chunk, functools.partial(score, seen_refs[c], base))
+
+        leave(i).start()
+        return 0
+
+    lax.fori_loop(0, count, body, 0)
+    for i in range(count):
+        leave(i).wait()
 
 
 def tie(x, state, names):
@@ -630,23 +661,54 @@
         compiler_params=params(),
         name="diagonal_sums",
     )(mid, sums, keep, bias)
-    diag = total(diag, ("genome",))
-
     chunk = next(c for c in (320, 256, 128, 64, 32) if nd % c == 0)
+    count = nd // chunk
     tall = chunk + 2 * RIM
-    twice = lambda tiles: [pltpu.VMEM((tiles, tall, LANES), F32)] * 2
-    whole = lambda a: pl.BlockSpec(a.shape, lambda i: (0,) * a.ndim)
-    operands = (low, mid, high, nears, fans, diag, perm)
+    scratch = [pltpu.VMEM((tiles, tall, LANES), F32) for tiles in (cols + 10, cols + 7) + (cols,) * 5]
+
+    def observe(*which):
+        def run(*operands):
+            made = {}
+            for c in which:
+                made[f"seen{c}"] = pl.pallas_call(
+                    functools.partial(observed_kernel, nd, nb, chunk, STEP, c * chunk),
+                    out_shape=f(5 * cols, chunk, LANES),
+                    in_specs=[VMEM] * 5,
+                    out_specs=VMEM,
+                    scratch_shapes=scratch,
+                    compiler_params=params(20),
+                    name="observed",
+                )(*operands)
+            return made
+
+        return ("low", "mid", "high", "near", "fan"), run
+
+    rounds = (lax.axis_size("genome") - 1).bit_length()
+    turns = {}
+    for c in range(count):
+        turns.setdefault(min(c, rounds - 1), []).append(c)
+    state.update(near=nears, fan=fans)
+    diag = total(
+        diag,
+        ("genome",),
+        state,
+        {k: observe(*which) for k, which in turns.items()},
+        {k: tuple(f"seen{c}" for c in which) for k, which in turns.items()},
+    )
+
+    operands = (low, mid, high, diag, perm) + tuple(state[f"seen{c}"] for c in range(count))
     score = pl.pallas_call(
-        functools.partial(filter_kernel, nd, nb, chunk, STEP),
+        functools.partial(score_kernel, nd, nb, chunk, STEP),
         out_shape=f(nd, nb),
-        grid=(nd // chunk,),
-        in_specs=[whole(a) for a in operands],
-        out_specs=pl.BlockSpec((chunk, nb), lambda i: (i, 0)),
-        scratch_shapes=[pltpu.VMEM((padded, LANES), F32)]
-        + twice(cols + 10) + twice(cols + 7) + twice(cols) + twice(cols) + twice(cols) + twice(cols) + twice(cols)
-        ,
-        compiler_params=params(44),
+        in_specs=[VMEM] * len(operands),
+        out_specs=HBM,
+        scratch_shapes=[
+            pltpu.VMEM((padded, LANES), F32),
+            pltpu.VMEM((nd, nb), F32),
+            pltpu.SemaphoreType.DMA((count,)),
+        ]
+        + scratch,
+        compiler_params=params(24),
         name="score",
     )(*operands)
     return score, own.reshape(nb)

time: 81.2 us -> 77 us (0.948)
  waiting for transfers between devices: 14.4 us -> 9.43 us
  Pallas kernels: 37.6 us -> 38.6 us
    ppermute x13, waiting for transfers between devices: 14.4 us -> 9.42 us  [total(): came = lax.ppermute(x, axis, pairs)]
    pallas_call x1 -> x5, Pallas kernels: 18.8 us -> 20.8 us  [the longest x1 13.4 us: on_device(): pl.pallas_call(functools.partial(score_kernel, nd, nb, chunk, STEP), out_...]
    pallas_call x1, Pallas kernels: 5.05 us -> 3.99 us  [on_device(): pl.pallas_call(functools.partial(third_kernel, nd, nb), out_shape=(f(cols...]
  transfers between devices with their start and end apart: 17 -> 17, of which waited for: 9 -> 7; matrix products, arithmetic and copies ran while one was open for 0% -> 0% of each run, Pallas kernels for 12% -> 23%
where the time goes in v3:
time: 77 us; the launch traced here: 76.8 us
  Pallas kernels  38.6 us (50%)
  starting transfers between devices  27.6 us (36%)
  waiting for transfers between devices  9.43 us (12%)
  between operations  1.03 us (1%)
    ppermute x13, starting transfers between devices, total(): came = lax.ppermute(x, axis, pairs)  18.2 us
    pallas_call x1, Pallas kernels, on_device(): pl.pallas_call(functools.partial(score_kernel, nd, nb, chunk, STEP), out_...  13.4 us
    ppermute x4, starting transfers between devices, shifted(): lax.ppermute(x, axis, pairs if step > 0 else [(j, i) for i, j in pairs])  9.46 us
    ppermute x13, waiting for transfers between devices, total(): came = lax.ppermute(x, axis, pairs)  9.42 us
    pallas_call x4, Pallas kernels, run(): pl.pallas_call(functools.partial(observed_kernel, nd, nb, chunk, STEP, c...  7.32 us
    pallas_call x3, Pallas kernels, run(): pl.pallas_call(functools.partial(strip_kernel, nd, nb, first, count), out...  6.79 us
    pallas_call x1, Pallas kernels, on_device(): pl.pallas_call(functools.partial(third_kernel, nd, nb), out_shape=(f(cols...  3.99 us
    pallas_call x1, Pallas kernels, on_device(): pl.pallas_call(functools.partial(first_kernel, nd, nb), out_shape=(shape(...  3.9 us
  transfers between devices with their start and end apart: 17, of which 7 were waited for; matrix products, arithmetic and copies ran while one was open for 0% of the time, Pallas kernels for 23%

profile of v3, /device:TPU:0, one launch (start us, length us, event | category | flops | bytes accessed | tf_op | source)
XLA Modules:
  0.0 76.8 jit_solution(9727852287715604439)
XLA Ops:
  0.6 3.9 %first_sums.1 = (bf16[1280,640]{1,0:T(8,128)(2,1)S(1)}, f32[40,128]{1,0:T(8,128)S(1)}, f32[40,128]{1,0:T(8,128)S(1)}, f32[16,640]{1,0:T(8,128)S(1)}, f32[16,640]{1,0:T(8,128)S(1)}) custom-call(s32[2]{0:T(128)} %bounds_hbm.1, bf16[1280,640]{1,0:T(8,128)(2,1)} %x_hbm.1, s32[1,128]{1,0:T(1,128)} %bitcast.2), custom_call_target="tpu_custom_call" | custom-call | tf_op jit(solution)/shard_map/first_sums/pallas_call | solution.py:547
  4.5 0.5 collective-permute-start
  5.1 4.5 %collective-permute-start.2 = (f32[16,640]{1,0:T(8,128)S(1)}, f32[16,640]{1,0:T(8,128)S(1)}, u32[]{:S(2)}, u32[]{:S(2)}) collective-permute-start(f32[16,640]{1,0:T(8,128)S(1)} %get-tuple-element.86), channel_id=1, source_target_pairs={{0,1},{1,2},{2,3},{4,5},{5,6},{6,7},{8,9},{9,10},{10,11},{12,13},{... | collective-permute-start | bytes 122888 | tf_op jit(solution)/shard_map/ppermute | solution.py:532
  9.5 0.0 collective-permute-done
  9.6 1.6 %collective-permute-start.1 = (f32[40,128]{1,0:T(8,128)S(1)}, f32[40,128]{1,0:T(8,128)S(1)}, u32[]{:S(2)}, u32[]{:S(2)}) collective-permute-start(f32[40,128]{1,0:T(8,128)S(1)} %add.39), channel_id=1, source_target_pairs={{0,8},{4,12},{8,0},{12,4},{16,24},{20,28},{24,16},{28,20},{1,9},{5... | collective-permute-start | bytes 61448 | tf_op jit(solution)/shard_map/ppermute | solution.py:519
  11.1 1.3 %collective-permute-start.4 = (f32[16,640]{1,0:T(8,128)S(1)}, f32[16,640]{1,0:T(8,128)S(1)}, u32[]{:S(2)}, u32[]{:S(2)}) collective-permute-start(f32[16,640]{1,0:T(8,128)S(1)} %get-tuple-element.88), channel_id=1, source_target_pairs={{1,0},{2,1},{3,2},{5,4},{6,5},{7,6},{9,8},{10,9},{11,10},{13,12},{... | collective-permute-start | bytes 122888 | tf_op jit(solution)/shard_map/ppermute | solution.py:532
  12.4 1.0 %collective-permute-done.1 = f32[40,128]{1,0:T(8,128)S(1)} collective-permute-done((f32[40,128]{1,0:T(8,128)S(1)}, f32[40,128]{1,0:T(8,128)S(1)}, u32[]{:S(2)}, u32[]{:S(2)}) %collective-permute-start.1) | collective-permute-done | bytes 20512 | tf_op jit(solution)/shard_map/ppermute | solution.py:519
  13.4 0.0 collective-permute-done.2.top_ref.left_ref
  13.4 1.6 %collective-permute-start.3 = (f32[40,128]{1,0:T(8,128)S(1)}, f32[40,128]{1,0:T(8,128)S(1)}, u32[]{:S(2)}, u32[]{:S(2)}) collective-permute-start(f32[40,128]{1,0:T(8,128)S(1)} %add.40), channel_id=1, source_target_pairs={{0,16},{4,20},{8,24},{12,28},{16,0},{20,4},{24,8},{28,12},{1,17},{... | collective-permute-start | bytes 61448 | tf_op jit(solution)/shard_map/ppermute | solution.py:519
  15.0 2.3 %collective-permute-done.3 = f32[40,128]{1,0:T(8,128)S(1)} collective-permute-done((f32[40,128]{1,0:T(8,128)S(1)}, f32[40,128]{1,0:T(8,128)S(1)}, u32[]{:S(2)}, u32[]{:S(2)}) %collective-permute-start.3) | collective-permute-done | bytes 20512 | tf_op jit(solution)/shard_map/ppermute | solution.py:519
  17.3 0.0 collective-permute-done.4.bottom_ref.right_ref
  17.3 1.7 %collective-permute-start.5 = (f32[40,128]{1,0:T(8,128)S(1)}, f32[40,128]{1,0:T(8,128)S(1)}, u32[]{:S(2)}, u32[]{:S(2)}) collective-permute-start(f32[40,128]{1,0:T(8,128)S(1)} %add.41), channel_id=1, source_target_pairs={{0,1},{1,0},{2,3},{3,2},{4,5},{5,4},{6,7},{7,6},{8,9},{9,8},{10,11... | collective-permute-start | bytes 61448 | tf_op jit(solution)/shard_map/ppermute | solution.py:519
  19.0 0.3 sides.1
  19.3 1.3 %collective-permute-start.8 = (f32[8,1312]{1,0:T(8,128)S(1)}, f32[8,1312]{1,0:T(8,128)S(1)}, u32[]{:S(2)}, u32[]{:S(2)}) collective-permute-start(f32[8,1312]{1,0:T(8,128)S(1)} %get-tuple-element.101), channel_id=1, source_target_pairs={{4,0},{8,4},{12,8},{16,12},{20,16},{24,20},{28,24},{5,1},{9,5},{13... | collective-permute-start | bytes 125960 | tf_op jit(solution)/shard_map/ppermute | solution.py:532
  20.6 0.5 collective-permute-done.5
  21.1 2.7 %collective-permute-start.6 = (f32[40,128]{1,0:T(8,128)S(1)}, f32[40,128]{1,0:T(8,128)S(1)}, u32[]{:S(2)}, u32[]{:S(2)}) collective-permute-start(f32[40,128]{1,0:T(8,128)S(1)} %add.42), channel_id=1, source_target_pairs={{0,2},{1,3},{2,0},{3,1},{4,6},{5,7},{6,4},{7,5},{8,10},{9,11},{10,... | collective-permute-start | bytes 61448 | tf_op jit(solution)/shard_map/ppermute | solution.py:519
  23.8 2.0 %collective-permute-done.6 = f32[40,128]{1,0:T(8,128)S(1)} collective-permute-done((f32[40,128]{1,0:T(8,128)S(1)}, f32[40,128]{1,0:T(8,128)S(1)}, u32[]{:S(2)}, u32[]{:S(2)}) %collective-permute-start.6) | collective-permute-done | bytes 20512 | tf_op jit(solution)/shard_map/ppermute | solution.py:519
  25.8 2.8 %second_sums.1 = (f32[40,128]{1,0:T(8,128)S(1)}, f32[40,128]{1,0:T(8,128)S(1)}) custom-call(bf16[1280,640]{1,0:T(8,128)(2,1)S(1)} %get-tuple-element.119.w_ref, f32[40,128]{1,0:T(8,128)S(1)} %add.43.sums_ref, f32[40,128]{1,0:T(8,128)S(1)} %get-tuple-element.128.keep_ref), custom_call_target="tpu_custom_call" | custom-call | tf_op jit(solution)/shard_map/second_sums/pallas_call | solution.py:589
  28.6 0.1 collective-permute-start.7
  28.7 2.4 %collective-permute-start.11 = (f32[8,1312]{1,0:T(8,128)S(1)}, f32[8,1312]{1,0:T(8,128)S(1)}, u32[]{:S(2)}, u32[]{:S(2)}) collective-permute-start(f32[8,1312]{1,0:T(8,128)S(1)} %get-tuple-element.107), channel_id=1, source_target_pairs={{0,4},{4,8},{8,12},{12,16},{16,20},{20,24},{24,28},{1,5},{5,9},{9,... | collective-permute-start | bytes 125960 | tf_op jit(solution)/shard_map/ppermute | solution.py:532
  31.1 0.2 unstrip.1.perm_ref
  31.2 0.0 collective-permute-done.7
  31.3 0.0 collective-permute-done.8.right_ref
  31.3 1.7 %collective-permute-start.9 = (f32[40,128]{1,0:T(8,128)S(1)}, f32[40,128]{1,0:T(8,128)S(1)}, u32[]{:S(2)}, u32[]{:S(2)}) collective-permute-start(f32[40,128]{1,0:T(8,128)S(1)} %add.44), channel_id=1, source_target_pairs={{0,8},{4,12},{8,0},{12,4},{16,24},{20,28},{24,16},{28,20},{1,9},{5... | collective-permute-start | bytes 61448 | tf_op jit(solution)/shard_map/ppermute | solution.py:519
  32.9 2.4 %collective-permute-done.9 = f32[40,128]{1,0:T(8,128)S(1)} collective-permute-done((f32[40,128]{1,0:T(8,128)S(1)}, f32[40,128]{1,0:T(8,128)S(1)}, u32[]{:S(2)}, u32[]{:S(2)}) %collective-permute-start.9) | collective-permute-done | bytes 20512 | tf_op jit(solution)/shard_map/ppermute | solution.py:519
  35.4 1.6 %collective-permute-start.10 = (f32[40,128]{1,0:T(8,128)S(1)}, f32[40,128]{1,0:T(8,128)S(1)}, u32[]{:S(2)}, u32[]{:S(2)}) collective-permute-start(f32[40,128]{1,0:T(8,128)S(1)} %add.45), channel_id=1, source_target_pairs={{0,16},{4,20},{8,24},{12,28},{16,0},{20,4},{24,8},{28,12},{1,17},{... | collective-permute-start | bytes 61448 | tf_op jit(solution)/shard_map/ppermute | solution.py:519
  37.0 2.0 %strips.3.mid_ref = bf16[5,1312,128]{2,1,0:T(8,128)(2,1)S(1)} custom-call(bf16[1280,640]{1,0:T(8,128)(2,1)S(1)} %get-tuple-element.119.w_ref, f32[16,640]{1,0:T(8,128)S(1)} %collective-permute-done.2.top_ref.left_ref, f32[16,640]{1,0:T(8,128)S(1)} %collective-permute-done.4.bottom_ref.right_ref, f32[16,640]{1,0:T(8,128)S(1)} %collective-permute-done.2.top_ref.left_ref, ...), custom_call_target="tpu_custom_call" | custom-call | tf_op jit(solution)/shard_map/strips/pallas_call | solution.py:606
  39.0 0.1 collective-permute-done.10
  39.1 0.0 collective-permute-done.11.left_ref
  39.1 1.6 %collective-permute-start.12 = (f32[40,128]{1,0:T(8,128)S(1)}, f32[40,128]{1,0:T(8,128)S(1)}, u32[]{:S(2)}, u32[]{:S(2)}) collective-permute-start(f32[40,128]{1,0:T(8,128)S(1)} %add.46), channel_id=1, source_target_pairs={{0,1},{1,0},{2,3},{3,2},{4,5},{5,4},{6,7},{7,6},{8,9},{9,8},{10,11... | collective-permute-start | bytes 61448 | tf_op jit(solution)/shard_map/ppermute | solution.py:519
  40.8 2.4 %strips.4.high_ref = bf16[5,1312,128]{2,1,0:T(8,128)(2,1)S(1)} custom-call(bf16[1280,640]{1,0:T(8,128)(2,1)S(1)} %get-tuple-element.119.w_ref, f32[16,640]{1,0:T(8,128)S(1)} %collective-permute-done.2.top_ref.left_ref, f32[16,640]{1,0:T(8,128)S(1)} %collective-permute-done.4.bottom_ref.right_ref, f32[8,1312]{1,0:T(8,128)S(1)} %collective-permute-done.11.left_ref, ...), custom_call_target="tpu_custom_call" | custom-call | tf_op jit(solution)/shard_map/strips/pallas_call | solution.py:606
  43.2 0.0 collective-permute-done.12
  43.2 2.9 %collective-permute-start.13 = (f32[40,128]{1,0:T(8,128)S(1)}, f32[40,128]{1,0:T(8,128)S(1)}, u32[]{:S(2)}, u32[]{:S(2)}) collective-permute-start(f32[40,128]{1,0:T(8,128)S(1)} %add.47), channel_id=1, source_target_pairs={{0,2},{1,3},{2,0},{3,1},{4,6},{5,7},{6,4},{7,5},{8,10},{9,11},{10,... | collective-permute-start | bytes 61448 | tf_op jit(solution)/shard_map/ppermute | solution.py:519
  46.1 2.4 %strips.5.low_ref = bf16[5,1312,128]{2,1,0:T(8,128)(2,1)S(1)} custom-call(bf16[1280,640]{1,0:T(8,128)(2,1)S(1)} %get-tuple-element.119.w_ref, f32[16,640]{1,0:T(8,128)S(1)} %collective-permute-done.2.top_ref.left_ref, f32[16,640]{1,0:T(8,128)S(1)} %collective-permute-done.4.bottom_ref.right_ref, f32[8,1312]{1,0:T(8,128)S(1)} %collective-permute-done.11.left_ref, ...), custom_call_target="tpu_custom_call" | custom-call | tf_op jit(solution)/shard_map/strips/pallas_call | solution.py:606
  48.5 0.0 collective-permute-done.13
  48.5 4.0 %diagonal_sums.1 = (f32[5,128]{1,0:T(8,128)}, f32[1344,128]{1,0:T(8,128)S(1)}, f32[24,128]{1,0:T(8,128)S(1)}, f32[22,128]{1,0:T(8,128)S(1)}) custom-call(bf16[5,1312,128]{2,1,0:T(8,128)(2,1)S(1)} %strips.3.mid_ref, f32[40,128]{1,0:T(8,128)S(1)} %add.48.sums_ref, f32[40,128]{1,0:T(8,128)S(1)} %get-tuple-element.128.keep_ref, ...), custom_call_target="tpu_custom_call" | custom-call | tf_op jit(solution)/shard_map/diagonal_sums/pallas_call | solution.py:648
  52.5 0.0 collective-permute-start.14
  52.5 1.8 %observed.4.rest_0_ = f32[25,320,128]{2,1,0:T(8,128)S(1)} custom-call(bf16[5,1312,128]{2,1,0:T(8,128)(2,1)S(1)} %strips.5.low_ref, bf16[5,1312,128]{2,1,0:T(8,128)(2,1)S(1)} %strips.3.mid_ref, bf16[5,1312,128]{2,1,0:T(8,128)(2,1)S(1)} %strips.4.high_ref, f32[24,128]{1,0:T(8,128)S(1)} %get-tuple-element.151.near_ref, f32[1344,128]{1,0:T(8,128)S(1)} %get-tuple-element.152.fan_ref), custom_call_target="tpu_custom_call" | custom-call | tf_op jit(solution)/shard_map/observed/pallas_call | solution.py:673
  54.3 0.0 collective-permute-done.14
  54.3 0.9 %collective-permute-start.15 = (f32[22,128]{1,0:T(8,128)S(1)}, f32[22,128]{1,0:T(8,128)S(1)}, u32[]{:S(2)}, u32[]{:S(2)}) collective-permute-start(f32[22,128]{1,0:T(8,128)S(1)} %add.49), channel_id=1, source_target_pairs={{0,8},{4,12},{8,0},{12,4},{16,24},{20,28},{24,16},{28,20},{1,9},{5... | collective-permute-start | bytes 33800 | tf_op jit(solution)/shard_map/ppermute | solution.py:519
  55.2 1.8 %observed.5.rest_1_ = f32[25,320,128]{2,1,0:T(8,128)S(1)} custom-call(bf16[5,1312,128]{2,1,0:T(8,128)(2,1)S(1)} %strips.5.low_ref, bf16[5,1312,128]{2,1,0:T(8,128)(2,1)S(1)} %strips.3.mid_ref, bf16[5,1312,128]{2,1,0:T(8,128)(2,1)S(1)} %strips.4.high_ref, f32[24,128]{1,0:T(8,128)S(1)} %get-tuple-element.151.near_ref, f32[1344,128]{1,0:T(8,128)S(1)} %get-tuple-element.152.fan_ref), custom_call_target="tpu_custom_call" | custom-call | tf_op jit(solution)/shard_map/observed/pallas_call | solution.py:673
  57.0 1.1 %collective-permute-done.15 = f32[22,128]{1,0:T(8,128)S(1)} collective-permute-done((f32[22,128]{1,0:T(8,128)S(1)}, f32[22,128]{1,0:T(8,128)S(1)}, u32[]{:S(2)}, u32[]{:S(2)}) %collective-permute-start.15) | collective-permute-done | bytes 11296 | tf_op jit(solution)/shard_map/ppermute | solution.py:519
  58.1 1.4 %collective-permute-start.16 = (f32[22,128]{1,0:T(8,128)S(1)}, f32[22,128]{1,0:T(8,128)S(1)}, u32[]{:S(2)}, u32[]{:S(2)}) collective-permute-start(f32[22,128]{1,0:T(8,128)S(1)} %add.50), channel_id=1, source_target_pairs={{0,16},{4,20},{8,24},{12,28},{16,0},{20,4},{24,8},{28,12},{1,17},{... | collective-permute-start | bytes 33800 | tf_op jit(solution)/shard_map/ppermute | solution.py:519
  59.5 1.8 %observed.7.rest_3_ = f32[25,320,128]{2,1,0:T(8,128)S(1)} custom-call(bf16[5,1312,128]{2,1,0:T(8,128)(2,1)S(1)} %strips.5.low_ref, bf16[5,1312,128]{2,1,0:T(8,128)(2,1)S(1)} %strips.3.mid_ref, bf16[5,1312,128]{2,1,0:T(8,128)(2,1)S(1)} %strips.4.high_ref, f32[24,128]{1,0:T(8,128)S(1)} %get-tuple-element.151.near_ref, f32[1344,128]{1,0:T(8,128)S(1)} %get-tuple-element.152.fan_ref), custom_call_target="tpu_custom_call" | custom-call | tf_op jit(solution)/shard_map/observed/pallas_call | solution.py:673
  61.3 1.8 %observed.6.rest_2_ = f32[25,320,128]{2,1,0:T(8,128)S(1)} custom-call(bf16[5,1312,128]{2,1,0:T(8,128)(2,1)S(1)} %strips.5.low_ref, bf16[5,1312,128]{2,1,0:T(8,128)(2,1)S(1)} %strips.3.mid_ref, bf16[5,1312,128]{2,1,0:T(8,128)(2,1)S(1)} %strips.4.high_ref, f32[24,128]{1,0:T(8,128)S(1)} %get-tuple-element.151.near_ref, f32[1344,128]{1,0:T(8,128)S(1)} %get-tuple-element.152.fan_ref), custom_call_target="tpu_custom_call" | custom-call | tf_op jit(solution)/shard_map/observed/pallas_call | solution.py:673
  63.2 0.0 collective-permute-done.16
  63.2 13.4 %score.1 = f32[1280,640]{1,0:T(8,128)} custom-call(bf16[5,1312,128]{2,1,0:T(8,128)(2,1)S(1)} %strips.5.low_ref, bf16[5,1312,128]{2,1,0:T(8,128)(2,1)S(1)} %strips.3.mid_ref, bf16[5,1312,128]{2,1,0:T(8,128)(2,1)S(1)} %strips.4.high_ref, f32[22,128]{1,0:T(8,128)S(1)} %add.51.diag_ref, bf16[640,640]{1,0:T(8,128)(2,1)S(1)} %unstrip.1.perm_ref, ...), custom_call_target="tpu_custom_call" | custom-call | tf_op jit(solution)/shard_map/score/pallas_call | solution.py:700
  (13 shorter events, 0.1 us)
Async XLA Ops:
  4.5 5.0 %collective-permute-start = (f32[40,128]{1,0:T(8,128)S(1)}, f32[40,128]{1,0:T(8,128)S(1)}, u32[]{:S(2)}, u32[]{:S(2)}) collective-permute-start(f32[40,128]{1,0:T(8,128)S(1)} %get-tuple-element.83), channel_id=1, source_target_pairs={{0,4},{4,0},{8,12},{12,8},{16,20},{20,16},{24,28},{28,24},{1,5},{5... | collective-permute-start | bytes 61448 | tf_op jit(solution)/shard_map/ppermute | solution.py:519
  5.1 8.4 %collective-permute-start.2 = (f32[16,640]{1,0:T(8,128)S(1)}, f32[16,640]{1,0:T(8,128)S(1)}, u32[]{:S(2)}, u32[]{:S(2)}) collective-permute-start(f32[16,640]{1,0:T(8,128)S(1)} %get-tuple-element.86), channel_id=1, source_target_pairs={{0,1},{1,2},{2,3},{4,5},{5,6},{6,7},{8,9},{9,10},{10,11},{12,13},{... | collective-permute-start | bytes 122888 | tf_op jit(solution)/shard_map/ppermute | solution.py:532
  9.6 3.8 %collective-permute-start.1 = (f32[40,128]{1,0:T(8,128)S(1)}, f32[40,128]{1,0:T(8,128)S(1)}, u32[]{:S(2)}, u32[]{:S(2)}) collective-permute-start(f32[40,128]{1,0:T(8,128)S(1)} %add.39), channel_id=1, source_target_pairs={{0,8},{4,12},{8,0},{12,4},{16,24},{20,28},{24,16},{28,20},{1,9},{5... | collective-permute-start | bytes 61448 | tf_op jit(solution)/shard_map/ppermute | solution.py:519
  11.1 6.2 %collective-permute-start.4 = (f32[16,640]{1,0:T(8,128)S(1)}, f32[16,640]{1,0:T(8,128)S(1)}, u32[]{:S(2)}, u32[]{:S(2)}) collective-permute-start(f32[16,640]{1,0:T(8,128)S(1)} %get-tuple-element.88), channel_id=1, source_target_pairs={{1,0},{2,1},{3,2},{5,4},{6,5},{7,6},{9,8},{10,9},{11,10},{13,12},{... | collective-permute-start | bytes 122888 | tf_op jit(solution)/shard_map/ppermute | solution.py:532
  13.4 3.8 %collective-permute-start.3 = (f32[40,128]{1,0:T(8,128)S(1)}, f32[40,128]{1,0:T(8,128)S(1)}, u32[]{:S(2)}, u32[]{:S(2)}) collective-permute-start(f32[40,128]{1,0:T(8,128)S(1)} %add.40), channel_id=1, source_target_pairs={{0,16},{4,20},{8,24},{12,28},{16,0},{20,4},{24,8},{28,12},{1,17},{... | collective-permute-start | bytes 61448 | tf_op jit(solution)/shard_map/ppermute | solution.py:519
  17.3 3.8 %collective-permute-start.5 = (f32[40,128]{1,0:T(8,128)S(1)}, f32[40,128]{1,0:T(8,128)S(1)}, u32[]{:S(2)}, u32[]{:S(2)}) collective-permute-start(f32[40,128]{1,0:T(8,128)S(1)} %add.41), channel_id=1, source_target_pairs={{0,1},{1,0},{2,3},{3,2},{4,5},{5,4},{6,7},{7,6},{8,9},{9,8},{10,11... | collective-permute-start | bytes 61448 | tf_op jit(solution)/shard_map/ppermute | solution.py:519
  19.3 12.0 %collective-permute-start.8 = (f32[8,1312]{1,0:T(8,128)S(1)}, f32[8,1312]{1,0:T(8,128)S(1)}, u32[]{:S(2)}, u32[]{:S(2)}) collective-permute-start(f32[8,1312]{1,0:T(8,128)S(1)} %get-tuple-element.101), channel_id=1, source_target_pairs={{4,0},{8,4},{12,8},{16,12},{20,16},{24,20},{28,24},{5,1},{9,5},{13... | collective-permute-start | bytes 125960 | tf_op jit(solution)/shard_map/ppermute | solution.py:532
  21.1 4.7 %collective-permute-start.6 = (f32[40,128]{1,0:T(8,128)S(1)}, f32[40,128]{1,0:T(8,128)S(1)}, u32[]{:S(2)}, u32[]{:S(2)}) collective-permute-start(f32[40,128]{1,0:T(8,128)S(1)} %add.42), channel_id=1, source_target_pairs={{0,2},{1,3},{2,0},{3,1},{4,6},{5,7},{6,4},{7,5},{8,10},{9,11},{10,... | collective-permute-start | bytes 61448 | tf_op jit(solution)/shard_map/ppermute | solution.py:519
  28.6 2.6 %collective-permute-start.7 = (f32[40,128]{1,0:T(8,128)S(1)}, f32[40,128]{1,0:T(8,128)S(1)}, u32[]{:S(2)}, u32[]{:S(2)}) collective-permute-start(f32[40,128]{1,0:T(8,128)S(1)} %get-tuple-element.100), channel_id=1, source_target_pairs={{0,4},{4,0},{8,12},{12,8},{16,20},{20,16},{24,28},{28,24},{1,5},{5... | collective-permute-start | bytes 61448 | tf_op jit(solution)/shard_map/ppermute | solution.py:519
  28.7 10.5 %collective-permute-start.11 = (f32[8,1312]{1,0:T(8,128)S(1)}, f32[8,1312]{1,0:T(8,128)S(1)}, u32[]{:S(2)}, u32[]{:S(2)}) collective-permute-start(f32[8,1312]{1,0:T(8,128)S(1)} %get-tuple-element.107), channel_id=1, source_target_pairs={{0,4},{4,8},{8,12},{12,16},{16,20},{20,24},{24,28},{1,5},{5,9},{9,... | collective-permute-start | bytes 125960 | tf_op jit(solution)/shard_map/ppermute | solution.py:532
  31.3 4.1 %collective-permute-start.9 = (f32[40,128]{1,0:T(8,128)S(1)}, f32[40,128]{1,0:T(8,128)S(1)}, u32[]{:S(2)}, u32[]{:S(2)}) collective-permute-start(f32[40,128]{1,0:T(8,128)S(1)} %add.44), channel_id=1, source_target_pairs={{0,8},{4,12},{8,0},{12,4},{16,24},{20,28},{24,16},{28,20},{1,9},{5... | collective-permute-start | bytes 61448 | tf_op jit(solution)/shard_map/ppermute | solution.py:519
  35.4 3.8 %collective-permute-start.10 = (f32[40,128]{1,0:T(8,128)S(1)}, f32[40,128]{1,0:T(8,128)S(1)}, u32[]{:S(2)}, u32[]{:S(2)}) collective-permute-start(f32[40,128]{1,0:T(8,128)S(1)} %add.45), channel_id=1, source_target_pairs={{0,16},{4,20},{8,24},{12,28},{16,0},{20,4},{24,8},{28,12},{1,17},{... | collective-permute-start | bytes 61448 | tf_op jit(solution)/shard_map/ppermute | solution.py:519
  39.1 4.0 %collective-permute-start.12 = (f32[40,128]{1,0:T(8,128)S(1)}, f32[40,128]{1,0:T(8,128)S(1)}, u32[]{:S(2)}, u32[]{:S(2)}) collective-permute-start(f32[40,128]{1,0:T(8,128)S(1)} %add.46), channel_id=1, source_target_pairs={{0,1},{1,0},{2,3},{3,2},{4,5},{5,4},{6,7},{7,6},{8,9},{9,8},{10,11... | collective-permute-start | bytes 61448 | tf_op jit(solution)/shard_map/ppermute | solution.py:519
  43.2 5.3 %collective-permute-start.13 = (f32[40,128]{1,0:T(8,128)S(1)}, f32[40,128]{1,0:T(8,128)S(1)}, u32[]{:S(2)}, u32[]{:S(2)}) collective-permute-start(f32[40,128]{1,0:T(8,128)S(1)} %add.47), channel_id=1, source_target_pairs={{0,2},{1,3},{2,0},{3,1},{4,6},{5,7},{6,4},{7,5},{8,10},{9,11},{10,... | collective-permute-start | bytes 61448 | tf_op jit(solution)/shard_map/ppermute | solution.py:519
  52.5 1.8 %collective-permute-start.14 = (f32[22,128]{1,0:T(8,128)S(1)}, f32[22,128]{1,0:T(8,128)S(1)}, u32[]{:S(2)}, u32[]{:S(2)}) collective-permute-start(f32[22,128]{1,0:T(8,128)S(1)} %get-tuple-element.133), channel_id=1, source_target_pairs={{0,4},{4,0},{8,12},{12,8},{16,20},{20,16},{24,28},{28,24},{1,5},{5... | collective-permute-start | bytes 33800 | tf_op jit(solution)/shard_map/ppermute | solution.py:519
  54.3 3.8 %collective-permute-start.15 = (f32[22,128]{1,0:T(8,128)S(1)}, f32[22,128]{1,0:T(8,128)S(1)}, u32[]{:S(2)}, u32[]{:S(2)}) collective-permute-start(f32[22,128]{1,0:T(8,128)S(1)} %add.49), channel_id=1, source_target_pairs={{0,8},{4,12},{8,0},{12,4},{16,24},{20,28},{24,16},{28,20},{1,9},{5... | collective-permute-start | bytes 33800 | tf_op jit(solution)/shard_map/ppermute | solution.py:519
  58.1 5.1 %collective-permute-start.16 = (f32[22,128]{1,0:T(8,128)S(1)}, f32[22,128]{1,0:T(8,128)S(1)}, u32[]{:S(2)}, u32[]{:S(2)}) collective-permute-start(f32[22,128]{1,0:T(8,128)S(1)} %add.50), channel_id=1, source_target_pairs={{0,16},{4,20},{8,24},{12,28},{16,0},{20,4},{24,8},{28,12},{1,17},{... | collective-permute-start | bytes 33800 | tf_op jit(solution)/shard_map/ppermute | solution.py:519

commit v4 on v3

--- a/solution.py
+++ b/solution.py
@@ -27,14 +27,6 @@
 
 def iota(shape, dim):
     return lax.broadcasted_iota(jnp.int32, shape, dim)
-
-
-def split3(x):
-    hi = x.astype(BF16)
-    rest = x - hi.astype(F32)
-    mid = rest.astype(BF16)
-    low = (rest - mid.astype(F32)).astype(BF16)
-    return hi, mid, low
 
 
 def place(nd, nb):
@@ -71,10 +63,12 @@
 def antidiagonal(acc_ref, tiles, lane0):
     extra = 1 if lane0 is None else 2
     pad = jnp.zeros((8, extra * LANES), F32)
-    total = None
-    for r in range(15, -1, -1):
-        part = jnp.concatenate([acc_ref[8 * r : 8 * r + 8, : tiles * LANES], pad], axis=1)
-        total = part if total is None else roll(total, 8) + part
+    parts = [jnp.concatenate([acc_ref[8 * r : 8 * r + 8, : tiles * LANES], pad], axis=1) for r in range(16)]
+    shift = 8
+    while len(parts) > 1:
+        parts = [low + roll(high, shift) for low, high in zip(parts[::2], parts[1::2])]
+        shift *= 2
+    total = parts[0]
     sub = iota(total.shape, 0)
     for bit in (4, 2, 1):
         total = jnp.where((sub & bit) > 0, roll(total, bit), total)
@@ -274,14 +268,8 @@
 
 
 def columns(rows, out_ref):
-    eye = iota((LANES, LANES), 0) == iota((LANES, LANES), 1)
-    blocks = []
-    for row in rows:
-        parts = [jnp.where(eye, jnp.broadcast_to(part.astype(F32), (LANES, LANES)), 0.0) for part in split3(row)]
-        blocks.append(jnp.concatenate([part.astype(BF16) for part in parts], axis=1))
-    out_ref[...] = jnp.dot(
-        jnp.concatenate(blocks, axis=0), jnp.ones((3 * LANES, LANES), BF16), preferred_element_type=F32
-    )
+    for k, row in enumerate(rows):
+        out_ref[k * LANES : (k + 1) * LANES, :] = jnp.broadcast_to(row, (LANES, LANES)).T
 
 
 def fan(col_ref, other_ref, start, rows, stride, out_ref):
@@ -299,7 +287,7 @@
             odd = (iota((size, LANES), 1) & bit) > 0
             target[pl.ds(at, size), :] = jnp.where(odd, high, low)
 
-        over(0, need, 208 if need > 208 else need, move)
+        move(0, need)
         source, target, offset = target, source, 0
 
 
@@ -337,21 +325,18 @@
             v = jnp.where(w > 0.0, 1.0, 0.0)
             total = b if total is None else total + b
             count = v if count is None else count + v
-        hi, mid, low = split3(total)
-        for k, part in enumerate((hi, mid, low, count.astype(BF16))):
-            total_ref[pl.ds(r0, size), k * LANES : (k + 1) * LANES] = part
-
-    over(0, total_rows, 160, add)
-    ones = jnp.ones((8, 3 * LANES), BF16)
+        total_ref[pl.ds(r0, size), :LANES] = total
+        total_ref[pl.ds(r0, size), LANES:] = count
+
+    over(0, total_rows, total_rows // 2, add)
     padded = total_ref.shape[0]
     tiles = padded // LANES
     if padded > total_rows:
-        total_ref[total_rows:, :] = jnp.zeros((padded - total_rows, 4 * LANES), BF16)
-    sums = lax.dot_general(ones, total_ref[:, : 3 * LANES], NT, preferred_element_type=F32)
-    counts = lax.dot_general(ones[:, :LANES], total_ref[:, 3 * LANES :], NT, preferred_element_type=F32)
+        total_ref[total_rows:, :] = jnp.zeros((padded - total_rows, 2 * LANES), F32)
     for t in range(tiles):
-        diag_ref[t : t + 1, :] = sums[0:1, t * LANES : (t + 1) * LANES]
-        diag_ref[tiles + t : tiles + t + 1, :] = counts[0:1, t * LANES : (t + 1) * LANES]
+        for k in range(2):
+            block = total_ref[t * LANES : (t + 1) * LANES, k * LANES : (k + 1) * LANES]
+            diag_ref[k * tiles + t : k * tiles + t + 1, :] = jnp.sum(block.T, axis=0, keepdims=True)
 
 
 def over(start, count, step, run):
@@ -448,6 +433,7 @@
     strips = strips_of(stride, low_ref, mid_ref, high_ref)
     tiles = diag_ref.shape[0] // 2
     expected = diag_ref[:tiles, :] / jnp.maximum(diag_ref[tiles:, :], 1.0)
+    expected = jnp.where(expected > 0.0, expected, 1.0)
     columns([expected[t : t + 1, :] for t in range(tiles)], col_ref)
 
     def leave(i):
@@ -465,7 +451,6 @@
                 ratio = (sums[k] + e) / (seen[k] + e)
                 least = ratio if least is None else jnp.minimum(least, ratio)
             value = least * (seen[4] * inverse)
-            value = jnp.where(x_ref[s + 5, pl.ds(r0, size), :] > 0.0, value, 0.0)
             hi = value.astype(BF16)
             low = (value - hi.astype(F32)).astype(BF16)
             perm = perm_ref[s * LANES : (s + 1) * LANES, :]
@@ -617,7 +602,8 @@
             )(*operands)
             return {name: strips}
 
-        return ("w", "above", "below") + (("above", "below") if name == "mid" else ("before", "after")), run
+        side = dict(low="before", mid="above", high="after")[name]
+        return ("w", "above", "below", side, side), run
 
     def back(_, right):
         matrix = pl.pallas_call(
@@ -631,12 +617,12 @@
 
     tasks = {
         0: (("keep", "right"), back),
-        2: strip("mid", 0, cols),
-        3: strip("high", cols, 5),
-        4: strip("low", -5, 5),
+        1: strip("mid", 0, cols),
+        2: strip("high", cols, 5),
+        3: strip("low", -5, 5),
     }
     state["keep"] = keep
-    due = {0: ("perm", "after"), 2: ("mid", "before"), 3: ("high",), 4: ("low",)}
+    due = {0: ("perm", "after"), 1: ("mid",), 2: ("high", "before"), 3: ("low",)}
     sums = total(part, ("genome", "offset"), state, tasks, due)
     low, high, mid, perm, keep = (state[name] for name in ("low", "high", "mid", "perm", "keep"))
 
@@ -656,7 +642,7 @@
             pltpu.VMEM((reach, LANES), F32),
             pltpu.VMEM((near_reach, LANES), F32),
             pltpu.VMEM((near_reach, LANES), F32),
-            pltpu.VMEM((padded, 4 * LANES), BF16),
+            pltpu.VMEM((padded, 2 * LANES), F32),
         ],
         compiler_params=params(),
         name="diagonal_sums",
@@ -686,7 +672,7 @@
     rounds = (lax.axis_size("genome") - 1).bit_length()
     turns = {}
     for c in range(count):
-        turns.setdefault(min(c, rounds - 1), []).append(c)
+        turns.setdefault((c + 1) * (rounds - 1) // count, []).append(c)
     state.update(near=nears, fan=fans)
     diag = total(
         diag,

time: 77 us -> 72.5 us (0.942)
  Pallas kernels: 38.6 us -> 34.5 us
    pallas_call x1, Pallas kernels: 3.99 us -> 2.3 us  [on_device(): pl.pallas_call(functools.partial(third_kernel, nd, nb), out_shape=(f(cols...]
    pallas_call x1, Pallas kernels: 3.9 us -> 2.98 us  [on_device(): pl.pallas_call(functools.partial(first_kernel, nd, nb), out_shape=(shape(...]
    pallas_call x1, Pallas kernels: 2.78 us -> 1.86 us  [on_device(): pl.pallas_call(functools.partial(second_kernel, nd, nb), out_shape=(f(row...]
where the time goes in v4:
time: 72.5 us; the launch traced here: 72.3 us
  Pallas kernels  34.5 us (48%)
  starting transfers between devices  28 us (39%)
  waiting for transfers between devices  8.77 us (12%)
  between operations  1.05 us (1%)
    ppermute x13, starting transfers between devices, total(): came = lax.ppermute(x, axis, pairs)  18.5 us
    pallas_call x1, Pallas kernels, on_device(): pl.pallas_call(functools.partial(score_kernel, nd, nb, chunk, STEP), out_...  12.8 us
    ppermute x4, starting transfers between devices, shifted(): lax.ppermute(x, axis, pairs if step > 0 else [(j, i) for i, j in pairs])  9.47 us
    ppermute x13, waiting for transfers between devices, total(): came = lax.ppermute(x, axis, pairs)  8.76 us
    pallas_call x4, Pallas kernels, run(): pl.pallas_call(functools.partial(observed_kernel, nd, nb, chunk, STEP, c...  7.33 us
    pallas_call x3, Pallas kernels, run(): pl.pallas_call(functools.partial(strip_kernel, nd, nb, first, count), out...  6.79 us
    pallas_call x1, Pallas kernels, on_device(): pl.pallas_call(functools.partial(first_kernel, nd, nb), out_shape=(shape(...  2.98 us
    pallas_call x1, Pallas kernels, on_device(): pl.pallas_call(functools.partial(third_kernel, nd, nb), out_shape=(f(cols...  2.3 us
  transfers between devices with their start and end apart: 17, of which 7 were waited for; matrix products, arithmetic and copies ran while one was open for 0% of the time, Pallas kernels for 23%

profile of v4, /device:TPU:0, one launch (start us, length us, event | category | flops | bytes accessed | tf_op | source)
XLA Modules:
  0.0 72.3 jit_solution(15286740834638462245)
XLA Ops:
  0.6 3.0 %first_sums.1 = (bf16[1280,640]{1,0:T(8,128)(2,1)S(1)}, f32[40,128]{1,0:T(8,128)S(1)}, f32[40,128]{1,0:T(8,128)S(1)}, f32[16,640]{1,0:T(8,128)S(1)}, f32[16,640]{1,0:T(8,128)S(1)}) custom-call(s32[2]{0:T(128)} %bounds_hbm.1, bf16[1280,640]{1,0:T(8,128)(2,1)} %x_hbm.1, s32[1,128]{1,0:T(1,128)} %bitcast.2), custom_call_target="tpu_custom_call" | custom-call | tf_op jit(solution)/shard_map/first_sums/pallas_call | solution.py:532
  3.6 0.5 collective-permute-start
  4.1 4.5 %collective-permute-start.2 = (f32[16,640]{1,0:T(8,128)S(1)}, f32[16,640]{1,0:T(8,128)S(1)}, u32[]{:S(2)}, u32[]{:S(2)}) collective-permute-start(f32[16,640]{1,0:T(8,128)S(1)} %get-tuple-element.84), channel_id=1, source_target_pairs={{0,1},{1,2},{2,3},{4,5},{5,6},{6,7},{8,9},{9,10},{10,11},{12,13},{... | collective-permute-start | bytes 122888 | tf_op jit(solution)/shard_map/ppermute | solution.py:517
  8.6 0.0 collective-permute-done
  8.7 1.6 %collective-permute-start.1 = (f32[40,128]{1,0:T(8,128)S(1)}, f32[40,128]{1,0:T(8,128)S(1)}, u32[]{:S(2)}, u32[]{:S(2)}) collective-permute-start(f32[40,128]{1,0:T(8,128)S(1)} %add.39), channel_id=1, source_target_pairs={{0,8},{4,12},{8,0},{12,4},{16,24},{20,28},{24,16},{28,20},{1,9},{5... | collective-permute-start | bytes 61448 | tf_op jit(solution)/shard_map/ppermute | solution.py:504
  10.2 1.3 %collective-permute-start.4 = (f32[16,640]{1,0:T(8,128)S(1)}, f32[16,640]{1,0:T(8,128)S(1)}, u32[]{:S(2)}, u32[]{:S(2)}) collective-permute-start(f32[16,640]{1,0:T(8,128)S(1)} %get-tuple-element.86), channel_id=1, source_target_pairs={{1,0},{2,1},{3,2},{5,4},{6,5},{7,6},{9,8},{10,9},{11,10},{13,12},{... | collective-permute-start | bytes 122888 | tf_op jit(solution)/shard_map/ppermute | solution.py:517
  11.5 1.0 %collective-permute-done.1 = f32[40,128]{1,0:T(8,128)S(1)} collective-permute-done((f32[40,128]{1,0:T(8,128)S(1)}, f32[40,128]{1,0:T(8,128)S(1)}, u32[]{:S(2)}, u32[]{:S(2)}) %collective-permute-start.1) | collective-permute-done | bytes 20512 | tf_op jit(solution)/shard_map/ppermute | solution.py:504
  12.5 0.0 collective-permute-done.2.top_ref.left_ref.right_ref
  12.5 1.6 %collective-permute-start.3 = (f32[40,128]{1,0:T(8,128)S(1)}, f32[40,128]{1,0:T(8,128)S(1)}, u32[]{:S(2)}, u32[]{:S(2)}) collective-permute-start(f32[40,128]{1,0:T(8,128)S(1)} %add.40), channel_id=1, source_target_pairs={{0,16},{4,20},{8,24},{12,28},{16,0},{20,4},{24,8},{28,12},{1,17},{... | collective-permute-start | bytes 61448 | tf_op jit(solution)/shard_map/ppermute | solution.py:504
  14.1 2.3 %collective-permute-done.3 = f32[40,128]{1,0:T(8,128)S(1)} collective-permute-done((f32[40,128]{1,0:T(8,128)S(1)}, f32[40,128]{1,0:T(8,128)S(1)}, u32[]{:S(2)}, u32[]{:S(2)}) %collective-permute-start.3) | collective-permute-done | bytes 20512 | tf_op jit(solution)/shard_map/ppermute | solution.py:504
  16.4 0.0 collective-permute-done.4.bottom_ref
  16.4 1.7 %collective-permute-start.5 = (f32[40,128]{1,0:T(8,128)S(1)}, f32[40,128]{1,0:T(8,128)S(1)}, u32[]{:S(2)}, u32[]{:S(2)}) collective-permute-start(f32[40,128]{1,0:T(8,128)S(1)} %add.41), channel_id=1, source_target_pairs={{0,1},{1,0},{2,3},{3,2},{4,5},{5,4},{6,7},{7,6},{8,9},{9,8},{10,11... | collective-permute-start | bytes 61448 | tf_op jit(solution)/shard_map/ppermute | solution.py:504
  18.1 0.3 sides.1
  18.4 1.3 %collective-permute-start.8 = (f32[8,1312]{1,0:T(8,128)S(1)}, f32[8,1312]{1,0:T(8,128)S(1)}, u32[]{:S(2)}, u32[]{:S(2)}) collective-permute-start(f32[8,1312]{1,0:T(8,128)S(1)} %get-tuple-element.99), channel_id=1, source_target_pairs={{4,0},{8,4},{12,8},{16,12},{20,16},{24,20},{28,24},{5,1},{9,5},{13... | collective-permute-start | bytes 125960 | tf_op jit(solution)/shard_map/ppermute | solution.py:517
  19.7 0.5 collective-permute-done.5
  20.2 2.7 %collective-permute-start.6 = (f32[40,128]{1,0:T(8,128)S(1)}, f32[40,128]{1,0:T(8,128)S(1)}, u32[]{:S(2)}, u32[]{:S(2)}) collective-permute-start(f32[40,128]{1,0:T(8,128)S(1)} %add.42), channel_id=1, source_target_pairs={{0,2},{1,3},{2,0},{3,1},{4,6},{5,7},{6,4},{7,5},{8,10},{9,11},{10,... | collective-permute-start | bytes 61448 | tf_op jit(solution)/shard_map/ppermute | solution.py:504
  22.9 2.0 %collective-permute-done.6 = f32[40,128]{1,0:T(8,128)S(1)} collective-permute-done((f32[40,128]{1,0:T(8,128)S(1)}, f32[40,128]{1,0:T(8,128)S(1)}, u32[]{:S(2)}, u32[]{:S(2)}) %collective-permute-start.6) | collective-permute-done | bytes 20512 | tf_op jit(solution)/shard_map/ppermute | solution.py:504
  24.9 1.9 %second_sums.1 = (f32[40,128]{1,0:T(8,128)S(1)}, f32[40,128]{1,0:T(8,128)S(1)}) custom-call(bf16[1280,640]{1,0:T(8,128)(2,1)S(1)} %get-tuple-element.116.w_ref, f32[40,128]{1,0:T(8,128)S(1)} %add.43.sums_ref, f32[40,128]{1,0:T(8,128)S(1)} %get-tuple-element.124.keep_ref), custom_call_target="tpu_custom_call" | custom-call | tf_op jit(solution)/shard_map/second_sums/pallas_call | solution.py:574
  26.8 0.1 collective-permute-start.7
  26.9 0.2 unstrip.1.perm_ref
  27.0 2.4 %collective-permute-start.11 = (f32[8,1312]{1,0:T(8,128)S(1)}, f32[8,1312]{1,0:T(8,128)S(1)}, u32[]{:S(2)}, u32[]{:S(2)}) collective-permute-start(f32[8,1312]{1,0:T(8,128)S(1)} %get-tuple-element.112), channel_id=1, source_target_pairs={{0,4},{4,8},{8,12},{12,16},{16,20},{20,24},{24,28},{1,5},{5,9},{9,... | collective-permute-start | bytes 125960 | tf_op jit(solution)/shard_map/ppermute | solution.py:517
  29.4 0.0 collective-permute-done.7
  29.4 0.0 collective-permute-done.8.left_ref.right_ref
  29.5 1.7 %collective-permute-start.9 = (f32[40,128]{1,0:T(8,128)S(1)}, f32[40,128]{1,0:T(8,128)S(1)}, u32[]{:S(2)}, u32[]{:S(2)}) collective-permute-start(f32[40,128]{1,0:T(8,128)S(1)} %add.44), channel_id=1, source_target_pairs={{0,8},{4,12},{8,0},{12,4},{16,24},{20,28},{24,16},{28,20},{1,9},{5... | collective-permute-start | bytes 61448 | tf_op jit(solution)/shard_map/ppermute | solution.py:504
  31.1 2.0 %strips.3.mid_ref = bf16[5,1312,128]{2,1,0:T(8,128)(2,1)S(1)} custom-call(bf16[1280,640]{1,0:T(8,128)(2,1)S(1)} %get-tuple-element.116.w_ref, f32[16,640]{1,0:T(8,128)S(1)} %collective-permute-done.2.top_ref.left_ref.right_ref, f32[16,640]{1,0:T(8,128)S(1)} %collective-permute-done.4.bottom_ref, ...), custom_call_target="tpu_custom_call" | custom-call | tf_op jit(solution)/shard_map/strips/pallas_call | solution.py:591
  33.1 0.4 collective-permute-done.9
  33.5 1.6 %collective-permute-start.10 = (f32[40,128]{1,0:T(8,128)S(1)}, f32[40,128]{1,0:T(8,128)S(1)}, u32[]{:S(2)}, u32[]{:S(2)}) collective-permute-start(f32[40,128]{1,0:T(8,128)S(1)} %add.45), channel_id=1, source_target_pairs={{0,16},{4,20},{8,24},{12,28},{16,0},{20,4},{24,8},{28,12},{1,17},{... | collective-permute-start | bytes 61448 | tf_op jit(solution)/shard_map/ppermute | solution.py:504
  35.2 2.4 %strips.4.high_ref = bf16[5,1312,128]{2,1,0:T(8,128)(2,1)S(1)} custom-call(bf16[1280,640]{1,0:T(8,128)(2,1)S(1)} %get-tuple-element.116.w_ref, f32[16,640]{1,0:T(8,128)S(1)} %collective-permute-done.2.top_ref.left_ref.right_ref, f32[16,640]{1,0:T(8,128)S(1)} %collective-permute-done.4.bottom_ref, f32[8,1312]{1,0:T(8,128)S(1)} %collective-permute-done.8.left_ref.right_ref, ...), custom_call_target="tpu_custom_call" | custom-call | tf_op jit(solution)/shard_map/strips/pallas_call | solution.py:591
  37.6 0.0 collective-permute-done.10
  37.6 0.0 collective-permute-done.11.left_ref.right_ref
  37.6 1.6 %collective-permute-start.12 = (f32[40,128]{1,0:T(8,128)S(1)}, f32[40,128]{1,0:T(8,128)S(1)}, u32[]{:S(2)}, u32[]{:S(2)}) collective-permute-start(f32[40,128]{1,0:T(8,128)S(1)} %add.46), channel_id=1, source_target_pairs={{0,1},{1,0},{2,3},{3,2},{4,5},{5,4},{6,7},{7,6},{8,9},{9,8},{10,11... | collective-permute-start | bytes 61448 | tf_op jit(solution)/shard_map/ppermute | solution.py:504
  39.2 2.4 %strips.5.low_ref = bf16[5,1312,128]{2,1,0:T(8,128)(2,1)S(1)} custom-call(bf16[1280,640]{1,0:T(8,128)(2,1)S(1)} %get-tuple-element.116.w_ref, f32[16,640]{1,0:T(8,128)S(1)} %collective-permute-done.2.top_ref.left_ref.right_ref, f32[16,640]{1,0:T(8,128)S(1)} %collective-permute-done.4.bottom_ref, f32[8,1312]{1,0:T(8,128)S(1)} %collective-permute-done.11.left_ref.right_ref, ...), custom_call_target="tpu_custom_call" | custom-call | tf_op jit(solution)/shard_map/strips/pallas_call | solution.py:591
  41.6 0.0 collective-permute-done.12
  41.6 2.7 %collective-permute-start.13 = (f32[40,128]{1,0:T(8,128)S(1)}, f32[40,128]{1,0:T(8,128)S(1)}, u32[]{:S(2)}, u32[]{:S(2)}) collective-permute-start(f32[40,128]{1,0:T(8,128)S(1)} %add.47), channel_id=1, source_target_pairs={{0,2},{1,3},{2,0},{3,1},{4,6},{5,7},{6,4},{7,5},{8,10},{9,11},{10,... | collective-permute-start | bytes 61448 | tf_op jit(solution)/shard_map/ppermute | solution.py:504
  44.3 2.1 %collective-permute-done.13 = f32[40,128]{1,0:T(8,128)S(1)} collective-permute-done((f32[40,128]{1,0:T(8,128)S(1)}, f32[40,128]{1,0:T(8,128)S(1)}, u32[]{:S(2)}, u32[]{:S(2)}) %collective-permute-start.13) | collective-permute-done | bytes 20512 | tf_op jit(solution)/shard_map/ppermute | solution.py:504
  46.3 2.3 %diagonal_sums.1 = (f32[5,128]{1,0:T(8,128)}, f32[1344,128]{1,0:T(8,128)S(1)}, f32[24,128]{1,0:T(8,128)S(1)}, f32[22,128]{1,0:T(8,128)S(1)}) custom-call(bf16[5,1312,128]{2,1,0:T(8,128)(2,1)S(1)} %strips.3.mid_ref, f32[40,128]{1,0:T(8,128)S(1)} %add.48.sums_ref, f32[40,128]{1,0:T(8,128)S(1)} %get-tuple-element.124.keep_ref, ...), custom_call_target="tpu_custom_call" | custom-call | tf_op jit(solution)/shard_map/diagonal_sums/pallas_call | solution.py:634
  48.6 0.1 collective-permute-start.14
  48.7 1.8 %observed.4.rest_0_ = f32[25,320,128]{2,1,0:T(8,128)S(1)} custom-call(bf16[5,1312,128]{2,1,0:T(8,128)(2,1)S(1)} %strips.5.low_ref, bf16[5,1312,128]{2,1,0:T(8,128)(2,1)S(1)} %strips.3.mid_ref, bf16[5,1312,128]{2,1,0:T(8,128)(2,1)S(1)} %strips.4.high_ref, f32[24,128]{1,0:T(8,128)S(1)} %get-tuple-element.147.near_ref, f32[1344,128]{1,0:T(8,128)S(1)} %get-tuple-element.148.fan_ref), custom_call_target="tpu_custom_call" | custom-call | tf_op jit(solution)/shard_map/observed/pallas_call | solution.py:659
  50.6 0.0 collective-permute-done.14
  50.6 1.3 %collective-permute-start.15 = (f32[22,128]{1,0:T(8,128)S(1)}, f32[22,128]{1,0:T(8,128)S(1)}, u32[]{:S(2)}, u32[]{:S(2)}) collective-permute-start(f32[22,128]{1,0:T(8,128)S(1)} %add.49), channel_id=1, source_target_pairs={{0,8},{4,12},{8,0},{12,4},{16,24},{20,28},{24,16},{28,20},{1,9},{5... | collective-permute-start | bytes 33800 | tf_op jit(solution)/shard_map/ppermute | solution.py:504
  51.9 1.8 %observed.6.rest_2_ = f32[25,320,128]{2,1,0:T(8,128)S(1)} custom-call(bf16[5,1312,128]{2,1,0:T(8,128)(2,1)S(1)} %strips.5.low_ref, bf16[5,1312,128]{2,1,0:T(8,128)(2,1)S(1)} %strips.3.mid_ref, bf16[5,1312,128]{2,1,0:T(8,128)(2,1)S(1)} %strips.4.high_ref, f32[24,128]{1,0:T(8,128)S(1)} %get-tuple-element.147.near_ref, f32[1344,128]{1,0:T(8,128)S(1)} %get-tuple-element.148.fan_ref), custom_call_target="tpu_custom_call" | custom-call | tf_op jit(solution)/shard_map/observed/pallas_call | solution.py:659
  53.7 1.8 %observed.5.rest_1_ = f32[25,320,128]{2,1,0:T(8,128)S(1)} custom-call(bf16[5,1312,128]{2,1,0:T(8,128)(2,1)S(1)} %strips.5.low_ref, bf16[5,1312,128]{2,1,0:T(8,128)(2,1)S(1)} %strips.3.mid_ref, bf16[5,1312,128]{2,1,0:T(8,128)(2,1)S(1)} %strips.4.high_ref, f32[24,128]{1,0:T(8,128)S(1)} %get-tuple-element.147.near_ref, f32[1344,128]{1,0:T(8,128)S(1)} %get-tuple-element.148.fan_ref), custom_call_target="tpu_custom_call" | custom-call | tf_op jit(solution)/shard_map/observed/pallas_call | solution.py:659
  55.6 0.0 collective-permute-done.15
  55.6 1.4 %collective-permute-start.16 = (f32[22,128]{1,0:T(8,128)S(1)}, f32[22,128]{1,0:T(8,128)S(1)}, u32[]{:S(2)}, u32[]{:S(2)}) collective-permute-start(f32[22,128]{1,0:T(8,128)S(1)} %add.50), channel_id=1, source_target_pairs={{0,16},{4,20},{8,24},{12,28},{16,0},{20,4},{24,8},{28,12},{1,17},{... | collective-permute-start | bytes 33800 | tf_op jit(solution)/shard_map/ppermute | solution.py:504
  57.0 1.8 %observed.7.rest_3_ = f32[25,320,128]{2,1,0:T(8,128)S(1)} custom-call(bf16[5,1312,128]{2,1,0:T(8,128)(2,1)S(1)} %strips.5.low_ref, bf16[5,1312,128]{2,1,0:T(8,128)(2,1)S(1)} %strips.3.mid_ref, bf16[5,1312,128]{2,1,0:T(8,128)(2,1)S(1)} %strips.4.high_ref, f32[24,128]{1,0:T(8,128)S(1)} %get-tuple-element.147.near_ref, f32[1344,128]{1,0:T(8,128)S(1)} %get-tuple-element.148.fan_ref), custom_call_target="tpu_custom_call" | custom-call | tf_op jit(solution)/shard_map/observed/pallas_call | solution.py:659
  58.9 0.5 collective-permute-done.16
  59.4 12.8 %score.1 = f32[1280,640]{1,0:T(8,128)} custom-call(bf16[5,1312,128]{2,1,0:T(8,128)(2,1)S(1)} %strips.5.low_ref, bf16[5,1312,128]{2,1,0:T(8,128)(2,1)S(1)} %strips.3.mid_ref, bf16[5,1312,128]{2,1,0:T(8,128)(2,1)S(1)} %strips.4.high_ref, f32[22,128]{1,0:T(8,128)S(1)} %add.51.diag_ref, bf16[640,640]{1,0:T(8,128)(2,1)S(1)} %unstrip.1.perm_ref, ...), custom_call_target="tpu_custom_call" | custom-call | tf_op jit(solution)/shard_map/score/pallas_call | solution.py:686
  (13 shorter events, 0.1 us)
Async XLA Ops:
  3.6 5.0 %collective-permute-start = (f32[40,128]{1,0:T(8,128)S(1)}, f32[40,128]{1,0:T(8,128)S(1)}, u32[]{:S(2)}, u32[]{:S(2)}) collective-permute-start(f32[40,128]{1,0:T(8,128)S(1)} %get-tuple-element.81), channel_id=1, source_target_pairs={{0,4},{4,0},{8,12},{12,8},{16,20},{20,16},{24,28},{28,24},{1,5},{5... | collective-permute-start | bytes 61448 | tf_op jit(solution)/shard_map/ppermute | solution.py:504
  4.1 8.4 %collective-permute-start.2 = (f32[16,640]{1,0:T(8,128)S(1)}, f32[16,640]{1,0:T(8,128)S(1)}, u32[]{:S(2)}, u32[]{:S(2)}) collective-permute-start(f32[16,640]{1,0:T(8,128)S(1)} %get-tuple-element.84), channel_id=1, source_target_pairs={{0,1},{1,2},{2,3},{4,5},{5,6},{6,7},{8,9},{9,10},{10,11},{12,13},{... | collective-permute-start | bytes 122888 | tf_op jit(solution)/shard_map/ppermute | solution.py:517
  8.7 3.8 %collective-permute-start.1 = (f32[40,128]{1,0:T(8,128)S(1)}, f32[40,128]{1,0:T(8,128)S(1)}, u32[]{:S(2)}, u32[]{:S(2)}) collective-permute-start(f32[40,128]{1,0:T(8,128)S(1)} %add.39), channel_id=1, source_target_pairs={{0,8},{4,12},{8,0},{12,4},{16,24},{20,28},{24,16},{28,20},{1,9},{5... | collective-permute-start | bytes 61448 | tf_op jit(solution)/shard_map/ppermute | solution.py:504
  10.2 6.2 %collective-permute-start.4 = (f32[16,640]{1,0:T(8,128)S(1)}, f32[16,640]{1,0:T(8,128)S(1)}, u32[]{:S(2)}, u32[]{:S(2)}) collective-permute-start(f32[16,640]{1,0:T(8,128)S(1)} %get-tuple-element.86), channel_id=1, source_target_pairs={{1,0},{2,1},{3,2},{5,4},{6,5},{7,6},{9,8},{10,9},{11,10},{13,12},{... | collective-permute-start | bytes 122888 | tf_op jit(solution)/shard_map/ppermute | solution.py:517
  12.5 3.8 %collective-permute-start.3 = (f32[40,128]{1,0:T(8,128)S(1)}, f32[40,128]{1,0:T(8,128)S(1)}, u32[]{:S(2)}, u32[]{:S(2)}) collective-permute-start(f32[40,128]{1,0:T(8,128)S(1)} %add.40), channel_id=1, source_target_pairs={{0,16},{4,20},{8,24},{12,28},{16,0},{20,4},{24,8},{28,12},{1,17},{... | collective-permute-start | bytes 61448 | tf_op jit(solution)/shard_map/ppermute | solution.py:504
  16.4 3.8 %collective-permute-start.5 = (f32[40,128]{1,0:T(8,128)S(1)}, f32[40,128]{1,0:T(8,128)S(1)}, u32[]{:S(2)}, u32[]{:S(2)}) collective-permute-start(f32[40,128]{1,0:T(8,128)S(1)} %add.41), channel_id=1, source_target_pairs={{0,1},{1,0},{2,3},{3,2},{4,5},{5,4},{6,7},{7,6},{8,9},{9,8},{10,11... | collective-permute-start | bytes 61448 | tf_op jit(solution)/shard_map/ppermute | solution.py:504
  18.4 11.1 %collective-permute-start.8 = (f32[8,1312]{1,0:T(8,128)S(1)}, f32[8,1312]{1,0:T(8,128)S(1)}, u32[]{:S(2)}, u32[]{:S(2)}) collective-permute-start(f32[8,1312]{1,0:T(8,128)S(1)} %get-tuple-element.99), channel_id=1, source_target_pairs={{4,0},{8,4},{12,8},{16,12},{20,16},{24,20},{28,24},{5,1},{9,5},{13... | collective-permute-start | bytes 125960 | tf_op jit(solution)/shard_map/ppermute | solution.py:517
  20.2 4.7 %collective-permute-start.6 = (f32[40,128]{1,0:T(8,128)S(1)}, f32[40,128]{1,0:T(8,128)S(1)}, u32[]{:S(2)}, u32[]{:S(2)}) collective-permute-start(f32[40,128]{1,0:T(8,128)S(1)} %add.42), channel_id=1, source_target_pairs={{0,2},{1,3},{2,0},{3,1},{4,6},{5,7},{6,4},{7,5},{8,10},{9,11},{10,... | collective-permute-start | bytes 61448 | tf_op jit(solution)/shard_map/ppermute | solution.py:504
  26.8 2.6 %collective-permute-start.7 = (f32[40,128]{1,0:T(8,128)S(1)}, f32[40,128]{1,0:T(8,128)S(1)}, u32[]{:S(2)}, u32[]{:S(2)}) collective-permute-start(f32[40,128]{1,0:T(8,128)S(1)} %get-tuple-element.98), channel_id=1, source_target_pairs={{0,4},{4,0},{8,12},{12,8},{16,20},{20,16},{24,28},{28,24},{1,5},{5... | collective-permute-start | bytes 61448 | tf_op jit(solution)/shard_map/ppermute | solution.py:504
  27.0 10.6 %collective-permute-start.11 = (f32[8,1312]{1,0:T(8,128)S(1)}, f32[8,1312]{1,0:T(8,128)S(1)}, u32[]{:S(2)}, u32[]{:S(2)}) collective-permute-start(f32[8,1312]{1,0:T(8,128)S(1)} %get-tuple-element.112), channel_id=1, source_target_pairs={{0,4},{4,8},{8,12},{12,16},{16,20},{20,24},{24,28},{1,5},{5,9},{9,... | collective-permute-start | bytes 125960 | tf_op jit(solution)/shard_map/ppermute | solution.py:517
  29.5 4.1 %collective-permute-start.9 = (f32[40,128]{1,0:T(8,128)S(1)}, f32[40,128]{1,0:T(8,128)S(1)}, u32[]{:S(2)}, u32[]{:S(2)}) collective-permute-start(f32[40,128]{1,0:T(8,128)S(1)} %add.44), channel_id=1, source_target_pairs={{0,8},{4,12},{8,0},{12,4},{16,24},{20,28},{24,16},{28,20},{1,9},{5... | collective-permute-start | bytes 61448 | tf_op jit(solution)/shard_map/ppermute | solution.py:504
  33.5 4.0 %collective-permute-start.10 = (f32[40,128]{1,0:T(8,128)S(1)}, f32[40,128]{1,0:T(8,128)S(1)}, u32[]{:S(2)}, u32[]{:S(2)}) collective-permute-start(f32[40,128]{1,0:T(8,128)S(1)} %add.45), channel_id=1, source_target_pairs={{0,16},{4,20},{8,24},{12,28},{16,0},{20,4},{24,8},{28,12},{1,17},{... | collective-permute-start | bytes 61448 | tf_op jit(solution)/shard_map/ppermute | solution.py:504
  37.6 4.0 %collective-permute-start.12 = (f32[40,128]{1,0:T(8,128)S(1)}, f32[40,128]{1,0:T(8,128)S(1)}, u32[]{:S(2)}, u32[]{:S(2)}) collective-permute-start(f32[40,128]{1,0:T(8,128)S(1)} %add.46), channel_id=1, source_target_pairs={{0,1},{1,0},{2,3},{3,2},{4,5},{5,4},{6,7},{7,6},{8,9},{9,8},{10,11... | collective-permute-start | bytes 61448 | tf_op jit(solution)/shard_map/ppermute | solution.py:504
  41.6 4.7 %collective-permute-start.13 = (f32[40,128]{1,0:T(8,128)S(1)}, f32[40,128]{1,0:T(8,128)S(1)}, u32[]{:S(2)}, u32[]{:S(2)}) collective-permute-start(f32[40,128]{1,0:T(8,128)S(1)} %add.47), channel_id=1, source_target_pairs={{0,2},{1,3},{2,0},{3,1},{4,6},{5,7},{6,4},{7,5},{8,10},{9,11},{10,... | collective-permute-start | bytes 61448 | tf_op jit(solution)/shard_map/ppermute | solution.py:504
  48.6 1.9 %collective-permute-start.14 = (f32[22,128]{1,0:T(8,128)S(1)}, f32[22,128]{1,0:T(8,128)S(1)}, u32[]{:S(2)}, u32[]{:S(2)}) collective-permute-start(f32[22,128]{1,0:T(8,128)S(1)} %get-tuple-element.129), channel_id=1, source_target_pairs={{0,4},{4,0},{8,12},{12,8},{16,20},{20,16},{24,28},{28,24},{1,5},{5... | collective-permute-start | bytes 33800 | tf_op jit(solution)/shard_map/ppermute | solution.py:504
  50.6 5.0 %collective-permute-start.15 = (f32[22,128]{1,0:T(8,128)S(1)}, f32[22,128]{1,0:T(8,128)S(1)}, u32[]{:S(2)}, u32[]{:S(2)}) collective-permute-start(f32[22,128]{1,0:T(8,128)S(1)} %add.49), channel_id=1, source_target_pairs={{0,8},{4,12},{8,0},{12,4},{16,24},{20,28},{24,16},{28,20},{1,9},{5... | collective-permute-start | bytes 33800 | tf_op jit(solution)/shard_map/ppermute | solution.py:504
  55.6 3.8 %collective-permute-start.16 = (f32[22,128]{1,0:T(8,128)S(1)}, f32[22,128]{1,0:T(8,128)S(1)}, u32[]{:S(2)}, u32[]{:S(2)}) collective-permute-start(f32[22,128]{1,0:T(8,128)S(1)} %add.50), channel_id=1, source_target_pairs={{0,16},{4,20},{8,24},{12,28},{16,0},{20,4},{24,8},{28,12},{1,17},{... | collective-permute-start | bytes 33800 | tf_op jit(solution)/shard_map/ppermute | solution.py:504

commit v5 on v4

--- a/solution.py
+++ b/solution.py
@@ -363,43 +363,31 @@
     return strips
 
 
-def shift_sums(chunk, stride, step, x, p, h, u, l, w, t):
-    def pairs(r0, size):
-        for s in range(-4, stride + 3):
-            p[s + 4, pl.ds(r0, size), :] = x[s + 5, pl.ds(r0, size), :] + x[s + 6, pl.ds(r0 - 1, size), :]
-
-    over(8, chunk + 24, step, pairs)
-
+def shift_sums(chunk, stride, step, x, h, u, l, w, t):
     def mix(r0, size):
         for s in range(stride):
             here = (s, pl.ds(r0, size), slice(None))
             at = lambda ref, k, shift: ref[k, pl.ds(r0 + shift, size), :]
-            hp = at(p, s + 7, -3) + at(x, s + 10, -5)
-            hm = at(p, s, 4) + at(x, s, 5)
-            lp = hp + at(p, s + 5, -1)
+            hp = at(x, s + 8, -3) + at(x, s + 9, -4) + at(x, s + 10, -5)
+            hm = at(x, s, 5) + at(x, s + 1, 4) + at(x, s + 2, 3)
+            ahead, behind = at(x, s + 6, -1), at(x, s + 4, 1)
+            lp = hp + (ahead + at(x, s + 7, -2))
             h[here] = hp
             u[here] = hp + hm
             l[here] = lp
-            w[here] = lp + (hm + at(p, s + 2, 2))
-            t[here] = at(p, s + 4, 0) + at(x, s + 4, 1)
+            w[here] = lp + (hm + (behind + at(x, s + 3, 2)))
+            t[here] = ahead + at(x, s + 5, 0) + behind
 
     over(8, chunk + 16, step, mix)
-
-    def runs(r0, size):
-        for s in range(stride):
-            for ref in (w, t):
-                at = lambda shift: ref[s, pl.ds(r0 + shift, size), :]
-                ref[s, pl.ds(r0, size), :] = at(0) + at(1) + at(2)
-
-    over(8, chunk + 16, step, runs)
 
 
 def four_sums(s, r0, size, h, u, l, w, t):
     at = lambda ref, shift: ref[s, pl.ds(r0 + shift, size), :]
     below, above = at(u, -1), at(u, 1)
-    donut = (at(w, -5) + at(w, 3)) + ((at(u, -2) + below) + (above + at(u, 2)))
+    six = lambda ref: (at(ref, -5) + at(ref, -4) + at(ref, -3)) + (at(ref, 3) + at(ref, 4) + at(ref, 5))
+    donut = six(w) + ((at(u, -2) + below) + (above + at(u, 2)))
     lower = (at(l, -5) + at(l, -4) + at(l, -3)) + (at(h, -2) + at(h, -1))
-    return donut, lower, at(t, -5) + at(t, 3), below + at(u, 0) + above
+    return donut, lower, six(t), below + at(u, 0) + above
 
 
 def observed_kernel(nd, nb, chunk, step, base, low_ref, mid_ref, high_ref, near_ref, fan_ref, out_ref, x_ref, *refs):
@@ -417,7 +405,7 @@
 
     def emit(r0, size):
         for s in range(stride):
-            sums = four_sums(s, r0, size, *refs[1:])
+            sums = four_sums(s, r0, size, *refs)
             for k, value in enumerate(sums + (x_ref[s + 5, pl.ds(r0, size), :],)):
                 out_ref[5 * s + k, pl.ds(r0 - RIM, size), :] = value
 
@@ -444,7 +432,7 @@
         e = col_ref[pl.ds(base + r0, size), :]
         inverse = 1.0 / e
         for s in range(stride):
-            sums = four_sums(s, r0, size, *refs[1:])
+            sums = four_sums(s, r0, size, *refs)
             seen = [seen_ref[5 * s + k, pl.ds(r0 - RIM, size), :] for k in range(5)]
             least = None
             for k in range(4):
@@ -650,7 +638,7 @@
     chunk = next(c for c in (320, 256, 128, 64, 32) if nd % c == 0)
     count = nd // chunk
     tall = chunk + 2 * RIM
-    scratch = [pltpu.VMEM((tiles, tall, LANES), F32) for tiles in (cols + 10, cols + 7) + (cols,) * 5]
+    scratch = [pltpu.VMEM((tiles, tall, LANES), F32) for tiles in (cols + 10,) + (cols,) * 5]
 
     def observe(*which):
         def run(*operands):

time: 72.5 us -> 71.5 us (0.986)
  Pallas kernels: 34.5 us -> 33.3 us
  transfers between devices with their start and end apart: 17 -> 17, of which waited for: 7 -> 7; matrix products, arithmetic and copies ran while one was open for 0% -> 0% of each run, Pallas kernels for 23% -> 22%
where the time goes in v5:
time: 71.5 us; the launch traced here: 71.3 us
  Pallas kernels  33.3 us (47%)
  starting transfers between devices  28 us (39%)
  waiting for transfers between devices  8.88 us (12%)
  between operations  1.04 us (1%)
    ppermute x13, starting transfers between devices, total(): came = lax.ppermute(x, axis, pairs)  18.5 us
    pallas_call x1, Pallas kernels, on_device(): pl.pallas_call(functools.partial(score_kernel, nd, nb, chunk, STEP), out_...  12 us
    ppermute x4, starting transfers between devices, shifted(): lax.ppermute(x, axis, pairs if step > 0 else [(j, i) for i, j in pairs])  9.47 us
    ppermute x13, waiting for transfers between devices, total(): came = lax.ppermute(x, axis, pairs)  8.87 us
    pallas_call x4, Pallas kernels, run(): pl.pallas_call(functools.partial(observed_kernel, nd, nb, chunk, STEP, c...  6.9 us
    pallas_call x3, Pallas kernels, run(): pl.pallas_call(functools.partial(strip_kernel, nd, nb, first, count), out...  6.79 us
    pallas_call x1, Pallas kernels, on_device(): pl.pallas_call(functools.partial(first_kernel, nd, nb), out_shape=(shape(...  2.98 us
    pallas_call x1, Pallas kernels, on_device(): pl.pallas_call(functools.partial(third_kernel, nd, nb), out_shape=(f(cols...  2.3 us
  transfers between devices with their start and end apart: 17, of which 7 were waited for; matrix products, arithmetic and copies ran while one was open for 0% of the time, Pallas kernels for 22%

profile of v5, /device:TPU:0, one launch (start us, length us, event | category | flops | bytes accessed | tf_op | source)
XLA Modules:
  0.0 71.3 jit_solution(17791316195174736999)
XLA Ops:
  0.6 3.0 %first_sums.1 = (bf16[1280,640]{1,0:T(8,128)(2,1)S(1)}, f32[40,128]{1,0:T(8,128)S(1)}, f32[40,128]{1,0:T(8,128)S(1)}, f32[16,640]{1,0:T(8,128)S(1)}, f32[16,640]{1,0:T(8,128)S(1)}) custom-call(s32[2]{0:T(128)} %bounds_hbm.1, bf16[1280,640]{1,0:T(8,128)(2,1)} %x_hbm.1, s32[1,128]{1,0:T(1,128)} %bitcast.2), custom_call_target="tpu_custom_call" | custom-call | tf_op jit(solution)/shard_map/first_sums/pallas_call | solution.py:520
  3.6 0.5 collective-permute-start
  4.1 4.5 %collective-permute-start.2 = (f32[16,640]{1,0:T(8,128)S(1)}, f32[16,640]{1,0:T(8,128)S(1)}, u32[]{:S(2)}, u32[]{:S(2)}) collective-permute-start(f32[16,640]{1,0:T(8,128)S(1)} %get-tuple-element.84), channel_id=1, source_target_pairs={{0,1},{1,2},{2,3},{4,5},{5,6},{6,7},{8,9},{9,10},{10,11},{12,13},{... | collective-permute-start | bytes 122888 | tf_op jit(solution)/shard_map/ppermute | solution.py:505
  8.6 0.0 collective-permute-done
  8.7 1.6 %collective-permute-start.1 = (f32[40,128]{1,0:T(8,128)S(1)}, f32[40,128]{1,0:T(8,128)S(1)}, u32[]{:S(2)}, u32[]{:S(2)}) collective-permute-start(f32[40,128]{1,0:T(8,128)S(1)} %add.39), channel_id=1, source_target_pairs={{0,8},{4,12},{8,0},{12,4},{16,24},{20,28},{24,16},{28,20},{1,9},{5... | collective-permute-start | bytes 61448 | tf_op jit(solution)/shard_map/ppermute | solution.py:492
  10.2 1.3 %collective-permute-start.4 = (f32[16,640]{1,0:T(8,128)S(1)}, f32[16,640]{1,0:T(8,128)S(1)}, u32[]{:S(2)}, u32[]{:S(2)}) collective-permute-start(f32[16,640]{1,0:T(8,128)S(1)} %get-tuple-element.86), channel_id=1, source_target_pairs={{1,0},{2,1},{3,2},{5,4},{6,5},{7,6},{9,8},{10,9},{11,10},{13,12},{... | collective-permute-start | bytes 122888 | tf_op jit(solution)/shard_map/ppermute | solution.py:505
  11.5 1.0 %collective-permute-done.1 = f32[40,128]{1,0:T(8,128)S(1)} collective-permute-done((f32[40,128]{1,0:T(8,128)S(1)}, f32[40,128]{1,0:T(8,128)S(1)}, u32[]{:S(2)}, u32[]{:S(2)}) %collective-permute-start.1) | collective-permute-done | bytes 20512 | tf_op jit(solution)/shard_map/ppermute | solution.py:492
  12.5 0.0 collective-permute-done.2.top_ref.left_ref.right_ref
  12.5 1.6 %collective-permute-start.3 = (f32[40,128]{1,0:T(8,128)S(1)}, f32[40,128]{1,0:T(8,128)S(1)}, u32[]{:S(2)}, u32[]{:S(2)}) collective-permute-start(f32[40,128]{1,0:T(8,128)S(1)} %add.40), channel_id=1, source_target_pairs={{0,16},{4,20},{8,24},{12,28},{16,0},{20,4},{24,8},{28,12},{1,17},{... | collective-permute-start | bytes 61448 | tf_op jit(solution)/shard_map/ppermute | solution.py:492
  14.1 2.3 %collective-permute-done.3 = f32[40,128]{1,0:T(8,128)S(1)} collective-permute-done((f32[40,128]{1,0:T(8,128)S(1)}, f32[40,128]{1,0:T(8,128)S(1)}, u32[]{:S(2)}, u32[]{:S(2)}) %collective-permute-start.3) | collective-permute-done | bytes 20512 | tf_op jit(solution)/shard_map/ppermute | solution.py:492
  16.4 0.0 collective-permute-done.4.bottom_ref
  16.4 1.7 %collective-permute-start.5 = (f32[40,128]{1,0:T(8,128)S(1)}, f32[40,128]{1,0:T(8,128)S(1)}, u32[]{:S(2)}, u32[]{:S(2)}) collective-permute-start(f32[40,128]{1,0:T(8,128)S(1)} %add.41), channel_id=1, source_target_pairs={{0,1},{1,0},{2,3},{3,2},{4,5},{5,4},{6,7},{7,6},{8,9},{9,8},{10,11... | collective-permute-start | bytes 61448 | tf_op jit(solution)/shard_map/ppermute | solution.py:492
  18.1 0.3 sides.1
  18.4 1.3 %collective-permute-start.8 = (f32[8,1312]{1,0:T(8,128)S(1)}, f32[8,1312]{1,0:T(8,128)S(1)}, u32[]{:S(2)}, u32[]{:S(2)}) collective-permute-start(f32[8,1312]{1,0:T(8,128)S(1)} %get-tuple-element.99), channel_id=1, source_target_pairs={{4,0},{8,4},{12,8},{16,12},{20,16},{24,20},{28,24},{5,1},{9,5},{13... | collective-permute-start | bytes 125960 | tf_op jit(solution)/shard_map/ppermute | solution.py:505
  19.7 0.5 collective-permute-done.5
  20.2 2.7 %collective-permute-start.6 = (f32[40,128]{1,0:T(8,128)S(1)}, f32[40,128]{1,0:T(8,128)S(1)}, u32[]{:S(2)}, u32[]{:S(2)}) collective-permute-start(f32[40,128]{1,0:T(8,128)S(1)} %add.42), channel_id=1, source_target_pairs={{0,2},{1,3},{2,0},{3,1},{4,6},{5,7},{6,4},{7,5},{8,10},{9,11},{10,... | collective-permute-start | bytes 61448 | tf_op jit(solution)/shard_map/ppermute | solution.py:492
  22.9 2.0 %collective-permute-done.6 = f32[40,128]{1,0:T(8,128)S(1)} collective-permute-done((f32[40,128]{1,0:T(8,128)S(1)}, f32[40,128]{1,0:T(8,128)S(1)}, u32[]{:S(2)}, u32[]{:S(2)}) %collective-permute-start.6) | collective-permute-done | bytes 20512 | tf_op jit(solution)/shard_map/ppermute | solution.py:492
  24.9 1.9 %second_sums.1 = (f32[40,128]{1,0:T(8,128)S(1)}, f32[40,128]{1,0:T(8,128)S(1)}) custom-call(bf16[1280,640]{1,0:T(8,128)(2,1)S(1)} %get-tuple-element.116.w_ref, f32[40,128]{1,0:T(8,128)S(1)} %add.43.sums_ref, f32[40,128]{1,0:T(8,128)S(1)} %get-tuple-element.124.keep_ref), custom_call_target="tpu_custom_call" | custom-call | tf_op jit(solution)/shard_map/second_sums/pallas_call | solution.py:562
  26.8 0.1 collective-permute-start.7
  26.9 0.2 unstrip.1.perm_ref
  27.0 2.4 %collective-permute-start.11 = (f32[8,1312]{1,0:T(8,128)S(1)}, f32[8,1312]{1,0:T(8,128)S(1)}, u32[]{:S(2)}, u32[]{:S(2)}) collective-permute-start(f32[8,1312]{1,0:T(8,128)S(1)} %get-tuple-element.112), channel_id=1, source_target_pairs={{0,4},{4,8},{8,12},{12,16},{16,20},{20,24},{24,28},{1,5},{5,9},{9,... | collective-permute-start | bytes 125960 | tf_op jit(solution)/shard_map/ppermute | solution.py:505
  29.4 0.0 collective-permute-done.7
  29.4 0.0 collective-permute-done.8.left_ref.right_ref
  29.5 1.7 %collective-permute-start.9 = (f32[40,128]{1,0:T(8,128)S(1)}, f32[40,128]{1,0:T(8,128)S(1)}, u32[]{:S(2)}, u32[]{:S(2)}) collective-permute-start(f32[40,128]{1,0:T(8,128)S(1)} %add.44), channel_id=1, source_target_pairs={{0,8},{4,12},{8,0},{12,4},{16,24},{20,28},{24,16},{28,20},{1,9},{5... | collective-permute-start | bytes 61448 | tf_op jit(solution)/shard_map/ppermute | solution.py:492
  31.1 2.0 %strips.3.mid_ref = bf16[5,1312,128]{2,1,0:T(8,128)(2,1)S(1)} custom-call(bf16[1280,640]{1,0:T(8,128)(2,1)S(1)} %get-tuple-element.116.w_ref, f32[16,640]{1,0:T(8,128)S(1)} %collective-permute-done.2.top_ref.left_ref.right_ref, f32[16,640]{1,0:T(8,128)S(1)} %collective-permute-done.4.bottom_ref, ...), custom_call_target="tpu_custom_call" | custom-call | tf_op jit(solution)/shard_map/strips/pallas_call | solution.py:579
  33.1 0.4 collective-permute-done.9
  33.5 1.6 %collective-permute-start.10 = (f32[40,128]{1,0:T(8,128)S(1)}, f32[40,128]{1,0:T(8,128)S(1)}, u32[]{:S(2)}, u32[]{:S(2)}) collective-permute-start(f32[40,128]{1,0:T(8,128)S(1)} %add.45), channel_id=1, source_target_pairs={{0,16},{4,20},{8,24},{12,28},{16,0},{20,4},{24,8},{28,12},{1,17},{... | collective-permute-start | bytes 61448 | tf_op jit(solution)/shard_map/ppermute | solution.py:492
  35.2 2.4 %strips.4.high_ref = bf16[5,1312,128]{2,1,0:T(8,128)(2,1)S(1)} custom-call(bf16[1280,640]{1,0:T(8,128)(2,1)S(1)} %get-tuple-element.116.w_ref, f32[16,640]{1,0:T(8,128)S(1)} %collective-permute-done.2.top_ref.left_ref.right_ref, f32[16,640]{1,0:T(8,128)S(1)} %collective-permute-done.4.bottom_ref, f32[8,1312]{1,0:T(8,128)S(1)} %collective-permute-done.8.left_ref.right_ref, ...), custom_call_target="tpu_custom_call" | custom-call | tf_op jit(solution)/shard_map/strips/pallas_call | solution.py:579
  37.6 0.0 collective-permute-done.10
  37.6 0.0 collective-permute-done.11.left_ref.right_ref
  37.6 1.6 %collective-permute-start.12 = (f32[40,128]{1,0:T(8,128)S(1)}, f32[40,128]{1,0:T(8,128)S(1)}, u32[]{:S(2)}, u32[]{:S(2)}) collective-permute-start(f32[40,128]{1,0:T(8,128)S(1)} %add.46), channel_id=1, source_target_pairs={{0,1},{1,0},{2,3},{3,2},{4,5},{5,4},{6,7},{7,6},{8,9},{9,8},{10,11... | collective-permute-start | bytes 61448 | tf_op jit(solution)/shard_map/ppermute | solution.py:492
  39.2 2.4 %strips.5.low_ref = bf16[5,1312,128]{2,1,0:T(8,128)(2,1)S(1)} custom-call(bf16[1280,640]{1,0:T(8,128)(2,1)S(1)} %get-tuple-element.116.w_ref, f32[16,640]{1,0:T(8,128)S(1)} %collective-permute-done.2.top_ref.left_ref.right_ref, f32[16,640]{1,0:T(8,128)S(1)} %collective-permute-done.4.bottom_ref, f32[8,1312]{1,0:T(8,128)S(1)} %collective-permute-done.11.left_ref.right_ref, ...), custom_call_target="tpu_custom_call" | custom-call | tf_op jit(solution)/shard_map/strips/pallas_call | solution.py:579
  41.6 0.0 collective-permute-done.12
  41.6 2.7 %collective-permute-start.13 = (f32[40,128]{1,0:T(8,128)S(1)}, f32[40,128]{1,0:T(8,128)S(1)}, u32[]{:S(2)}, u32[]{:S(2)}) collective-permute-start(f32[40,128]{1,0:T(8,128)S(1)} %add.47), channel_id=1, source_target_pairs={{0,2},{1,3},{2,0},{3,1},{4,6},{5,7},{6,4},{7,5},{8,10},{9,11},{10,... | collective-permute-start | bytes 61448 | tf_op jit(solution)/shard_map/ppermute | solution.py:492
  44.3 2.1 %collective-permute-done.13 = f32[40,128]{1,0:T(8,128)S(1)} collective-permute-done((f32[40,128]{1,0:T(8,128)S(1)}, f32[40,128]{1,0:T(8,128)S(1)}, u32[]{:S(2)}, u32[]{:S(2)}) %collective-permute-start.13) | collective-permute-done | bytes 20512 | tf_op jit(solution)/shard_map/ppermute | solution.py:492
  46.3 2.3 %diagonal_sums.1 = (f32[5,128]{1,0:T(8,128)}, f32[1344,128]{1,0:T(8,128)S(1)}, f32[24,128]{1,0:T(8,128)S(1)}, f32[22,128]{1,0:T(8,128)S(1)}) custom-call(bf16[5,1312,128]{2,1,0:T(8,128)(2,1)S(1)} %strips.3.mid_ref, f32[40,128]{1,0:T(8,128)S(1)} %add.48.sums_ref, f32[40,128]{1,0:T(8,128)S(1)} %get-tuple-element.124.keep_ref, ...), custom_call_target="tpu_custom_call" | custom-call | tf_op jit(solution)/shard_map/diagonal_sums/pallas_call | solution.py:622
  48.6 0.1 collective-permute-start.14
  48.7 1.7 %observed.4.rest_0_ = f32[25,320,128]{2,1,0:T(8,128)S(1)} custom-call(bf16[5,1312,128]{2,1,0:T(8,128)(2,1)S(1)} %strips.5.low_ref, bf16[5,1312,128]{2,1,0:T(8,128)(2,1)S(1)} %strips.3.mid_ref, bf16[5,1312,128]{2,1,0:T(8,128)(2,1)S(1)} %strips.4.high_ref, f32[24,128]{1,0:T(8,128)S(1)} %get-tuple-element.147.near_ref, f32[1344,128]{1,0:T(8,128)S(1)} %get-tuple-element.148.fan_ref), custom_call_target="tpu_custom_call" | custom-call | tf_op jit(solution)/shard_map/observed/pallas_call | solution.py:647
  50.4 0.0 collective-permute-done.14
  50.5 1.3 %collective-permute-start.15 = (f32[22,128]{1,0:T(8,128)S(1)}, f32[22,128]{1,0:T(8,128)S(1)}, u32[]{:S(2)}, u32[]{:S(2)}) collective-permute-start(f32[22,128]{1,0:T(8,128)S(1)} %add.49), channel_id=1, source_target_pairs={{0,8},{4,12},{8,0},{12,4},{16,24},{20,28},{24,16},{28,20},{1,9},{5... | collective-permute-start | bytes 33800 | tf_op jit(solution)/shard_map/ppermute | solution.py:492
  51.8 1.7 %observed.6.rest_2_ = f32[25,320,128]{2,1,0:T(8,128)S(1)} custom-call(bf16[5,1312,128]{2,1,0:T(8,128)(2,1)S(1)} %strips.5.low_ref, bf16[5,1312,128]{2,1,0:T(8,128)(2,1)S(1)} %strips.3.mid_ref, bf16[5,1312,128]{2,1,0:T(8,128)(2,1)S(1)} %strips.4.high_ref, f32[24,128]{1,0:T(8,128)S(1)} %get-tuple-element.147.near_ref, f32[1344,128]{1,0:T(8,128)S(1)} %get-tuple-element.148.fan_ref), custom_call_target="tpu_custom_call" | custom-call | tf_op jit(solution)/shard_map/observed/pallas_call | solution.py:647
  53.5 1.7 %observed.5.rest_1_ = f32[25,320,128]{2,1,0:T(8,128)S(1)} custom-call(bf16[5,1312,128]{2,1,0:T(8,128)(2,1)S(1)} %strips.5.low_ref, bf16[5,1312,128]{2,1,0:T(8,128)(2,1)S(1)} %strips.3.mid_ref, bf16[5,1312,128]{2,1,0:T(8,128)(2,1)S(1)} %strips.4.high_ref, f32[24,128]{1,0:T(8,128)S(1)} %get-tuple-element.147.near_ref, f32[1344,128]{1,0:T(8,128)S(1)} %get-tuple-element.148.fan_ref), custom_call_target="tpu_custom_call" | custom-call | tf_op jit(solution)/shard_map/observed/pallas_call | solution.py:647
  55.2 0.0 collective-permute-done.15
  55.3 1.4 %collective-permute-start.16 = (f32[22,128]{1,0:T(8,128)S(1)}, f32[22,128]{1,0:T(8,128)S(1)}, u32[]{:S(2)}, u32[]{:S(2)}) collective-permute-start(f32[22,128]{1,0:T(8,128)S(1)} %add.50), channel_id=1, source_target_pairs={{0,16},{4,20},{8,24},{12,28},{16,0},{20,4},{24,8},{28,12},{1,17},{... | collective-permute-start | bytes 33800 | tf_op jit(solution)/shard_map/ppermute | solution.py:492
  56.7 1.7 %observed.7.rest_3_ = f32[25,320,128]{2,1,0:T(8,128)S(1)} custom-call(bf16[5,1312,128]{2,1,0:T(8,128)(2,1)S(1)} %strips.5.low_ref, bf16[5,1312,128]{2,1,0:T(8,128)(2,1)S(1)} %strips.3.mid_ref, bf16[5,1312,128]{2,1,0:T(8,128)(2,1)S(1)} %strips.4.high_ref, f32[24,128]{1,0:T(8,128)S(1)} %get-tuple-element.147.near_ref, f32[1344,128]{1,0:T(8,128)S(1)} %get-tuple-element.148.fan_ref), custom_call_target="tpu_custom_call" | custom-call | tf_op jit(solution)/shard_map/observed/pallas_call | solution.py:647
  58.4 0.6 collective-permute-done.16
  59.0 12.0 %score.1 = f32[1280,640]{1,0:T(8,128)} custom-call(bf16[5,1312,128]{2,1,0:T(8,128)(2,1)S(1)} %strips.5.low_ref, bf16[5,1312,128]{2,1,0:T(8,128)(2,1)S(1)} %strips.3.mid_ref, bf16[5,1312,128]{2,1,0:T(8,128)(2,1)S(1)} %strips.4.high_ref, f32[22,128]{1,0:T(8,128)S(1)} %add.51.diag_ref, bf16[640,640]{1,0:T(8,128)(2,1)S(1)} %unstrip.1.perm_ref, ...), custom_call_target="tpu_custom_call" | custom-call | tf_op jit(solution)/shard_map/score/pallas_call | solution.py:674
  (13 shorter events, 0.1 us)
Async XLA Ops:
  3.6 5.0 %collective-permute-start = (f32[40,128]{1,0:T(8,128)S(1)}, f32[40,128]{1,0:T(8,128)S(1)}, u32[]{:S(2)}, u32[]{:S(2)}) collective-permute-start(f32[40,128]{1,0:T(8,128)S(1)} %get-tuple-element.81), channel_id=1, source_target_pairs={{0,4},{4,0},{8,12},{12,8},{16,20},{20,16},{24,28},{28,24},{1,5},{5... | collective-permute-start | bytes 61448 | tf_op jit(solution)/shard_map/ppermute | solution.py:492
  4.1 8.4 %collective-permute-start.2 = (f32[16,640]{1,0:T(8,128)S(1)}, f32[16,640]{1,0:T(8,128)S(1)}, u32[]{:S(2)}, u32[]{:S(2)}) collective-permute-start(f32[16,640]{1,0:T(8,128)S(1)} %get-tuple-element.84), channel_id=1, source_target_pairs={{0,1},{1,2},{2,3},{4,5},{5,6},{6,7},{8,9},{9,10},{10,11},{12,13},{... | collective-permute-start | bytes 122888 | tf_op jit(solution)/shard_map/ppermute | solution.py:505
  8.7 3.8 %collective-permute-start.1 = (f32[40,128]{1,0:T(8,128)S(1)}, f32[40,128]{1,0:T(8,128)S(1)}, u32[]{:S(2)}, u32[]{:S(2)}) collective-permute-start(f32[40,128]{1,0:T(8,128)S(1)} %add.39), channel_id=1, source_target_pairs={{0,8},{4,12},{8,0},{12,4},{16,24},{20,28},{24,16},{28,20},{1,9},{5... | collective-permute-start | bytes 61448 | tf_op jit(solution)/shard_map/ppermute | solution.py:492
  10.2 6.2 %collective-permute-start.4 = (f32[16,640]{1,0:T(8,128)S(1)}, f32[16,640]{1,0:T(8,128)S(1)}, u32[]{:S(2)}, u32[]{:S(2)}) collective-permute-start(f32[16,640]{1,0:T(8,128)S(1)} %get-tuple-element.86), channel_id=1, source_target_pairs={{1,0},{2,1},{3,2},{5,4},{6,5},{7,6},{9,8},{10,9},{11,10},{13,12},{... | collective-permute-start | bytes 122888 | tf_op jit(solution)/shard_map/ppermute | solution.py:505
  12.5 3.8 %collective-permute-start.3 = (f32[40,128]{1,0:T(8,128)S(1)}, f32[40,128]{1,0:T(8,128)S(1)}, u32[]{:S(2)}, u32[]{:S(2)}) collective-permute-start(f32[40,128]{1,0:T(8,128)S(1)} %add.40), channel_id=1, source_target_pairs={{0,16},{4,20},{8,24},{12,28},{16,0},{20,4},{24,8},{28,12},{1,17},{... | collective-permute-start | bytes 61448 | tf_op jit(solution)/shard_map/ppermute | solution.py:492
  16.4 3.8 %collective-permute-start.5 = (f32[40,128]{1,0:T(8,128)S(1)}, f32[40,128]{1,0:T(8,128)S(1)}, u32[]{:S(2)}, u32[]{:S(2)}) collective-permute-start(f32[40,128]{1,0:T(8,128)S(1)} %add.41), channel_id=1, source_target_pairs={{0,1},{1,0},{2,3},{3,2},{4,5},{5,4},{6,7},{7,6},{8,9},{9,8},{10,11... | collective-permute-start | bytes 61448 | tf_op jit(solution)/shard_map/ppermute | solution.py:492
  18.4 11.1 %collective-permute-start.8 = (f32[8,1312]{1,0:T(8,128)S(1)}, f32[8,1312]{1,0:T(8,128)S(1)}, u32[]{:S(2)}, u32[]{:S(2)}) collective-permute-start(f32[8,1312]{1,0:T(8,128)S(1)} %get-tuple-element.99), channel_id=1, source_target_pairs={{4,0},{8,4},{12,8},{16,12},{20,16},{24,20},{28,24},{5,1},{9,5},{13... | collective-permute-start | bytes 125960 | tf_op jit(solution)/shard_map/ppermute | solution.py:505
  20.2 4.7 %collective-permute-start.6 = (f32[40,128]{1,0:T(8,128)S(1)}, f32[40,128]{1,0:T(8,128)S(1)}, u32[]{:S(2)}, u32[]{:S(2)}) collective-permute-start(f32[40,128]{1,0:T(8,128)S(1)} %add.42), channel_id=1, source_target_pairs={{0,2},{1,3},{2,0},{3,1},{4,6},{5,7},{6,4},{7,5},{8,10},{9,11},{10,... | collective-permute-start | bytes 61448 | tf_op jit(solution)/shard_map/ppermute | solution.py:492
  26.8 2.6 %collective-permute-start.7 = (f32[40,128]{1,0:T(8,128)S(1)}, f32[40,128]{1,0:T(8,128)S(1)}, u32[]{:S(2)}, u32[]{:S(2)}) collective-permute-start(f32[40,128]{1,0:T(8,128)S(1)} %get-tuple-element.98), channel_id=1, source_target_pairs={{0,4},{4,0},{8,12},{12,8},{16,20},{20,16},{24,28},{28,24},{1,5},{5... | collective-permute-start | bytes 61448 | tf_op jit(solution)/shard_map/ppermute | solution.py:492
  27.0 10.6 %collective-permute-start.11 = (f32[8,1312]{1,0:T(8,128)S(1)}, f32[8,1312]{1,0:T(8,128)S(1)}, u32[]{:S(2)}, u32[]{:S(2)}) collective-permute-start(f32[8,1312]{1,0:T(8,128)S(1)} %get-tuple-element.112), channel_id=1, source_target_pairs={{0,4},{4,8},{8,12},{12,16},{16,20},{20,24},{24,28},{1,5},{5,9},{9,... | collective-permute-start | bytes 125960 | tf_op jit(solution)/shard_map/ppermute | solution.py:505
  29.5 4.1 %collective-permute-start.9 = (f32[40,128]{1,0:T(8,128)S(1)}, f32[40,128]{1,0:T(8,128)S(1)}, u32[]{:S(2)}, u32[]{:S(2)}) collective-permute-start(f32[40,128]{1,0:T(8,128)S(1)} %add.44), channel_id=1, source_target_pairs={{0,8},{4,12},{8,0},{12,4},{16,24},{20,28},{24,16},{28,20},{1,9},{5... | collective-permute-start | bytes 61448 | tf_op jit(solution)/shard_map/ppermute | solution.py:492
  33.5 4.0 %collective-permute-start.10 = (f32[40,128]{1,0:T(8,128)S(1)}, f32[40,128]{1,0:T(8,128)S(1)}, u32[]{:S(2)}, u32[]{:S(2)}) collective-permute-start(f32[40,128]{1,0:T(8,128)S(1)} %add.45), channel_id=1, source_target_pairs={{0,16},{4,20},{8,24},{12,28},{16,0},{20,4},{24,8},{28,12},{1,17},{... | collective-permute-start | bytes 61448 | tf_op jit(solution)/shard_map/ppermute | solution.py:492
  37.6 4.0 %collective-permute-start.12 = (f32[40,128]{1,0:T(8,128)S(1)}, f32[40,128]{1,0:T(8,128)S(1)}, u32[]{:S(2)}, u32[]{:S(2)}) collective-permute-start(f32[40,128]{1,0:T(8,128)S(1)} %add.46), channel_id=1, source_target_pairs={{0,1},{1,0},{2,3},{3,2},{4,5},{5,4},{6,7},{7,6},{8,9},{9,8},{10,11... | collective-permute-start | bytes 61448 | tf_op jit(solution)/shard_map/ppermute | solution.py:492
  41.6 4.7 %collective-permute-start.13 = (f32[40,128]{1,0:T(8,128)S(1)}, f32[40,128]{1,0:T(8,128)S(1)}, u32[]{:S(2)}, u32[]{:S(2)}) collective-permute-start(f32[40,128]{1,0:T(8,128)S(1)} %add.47), channel_id=1, source_target_pairs={{0,2},{1,3},{2,0},{3,1},{4,6},{5,7},{6,4},{7,5},{8,10},{9,11},{10,... | collective-permute-start | bytes 61448 | tf_op jit(solution)/shard_map/ppermute | solution.py:492
  48.6 1.8 %collective-permute-start.14 = (f32[22,128]{1,0:T(8,128)S(1)}, f32[22,128]{1,0:T(8,128)S(1)}, u32[]{:S(2)}, u32[]{:S(2)}) collective-permute-start(f32[22,128]{1,0:T(8,128)S(1)} %get-tuple-element.129), channel_id=1, source_target_pairs={{0,4},{4,0},{8,12},{12,8},{16,20},{20,16},{24,28},{28,24},{1,5},{5... | collective-permute-start | bytes 33800 | tf_op jit(solution)/shard_map/ppermute | solution.py:492
  50.5 4.8 %collective-permute-start.15 = (f32[22,128]{1,0:T(8,128)S(1)}, f32[22,128]{1,0:T(8,128)S(1)}, u32[]{:S(2)}, u32[]{:S(2)}) collective-permute-start(f32[22,128]{1,0:T(8,128)S(1)} %add.49), channel_id=1, source_target_pairs={{0,8},{4,12},{8,0},{12,4},{16,24},{20,28},{24,16},{28,20},{1,9},{5... | collective-permute-start | bytes 33800 | tf_op jit(solution)/shard_map/ppermute | solution.py:492
  55.3 3.8 %collective-permute-start.16 = (f32[22,128]{1,0:T(8,128)S(1)}, f32[22,128]{1,0:T(8,128)S(1)}, u32[]{:S(2)}, u32[]{:S(2)}) collective-permute-start(f32[22,128]{1,0:T(8,128)S(1)} %add.50), channel_id=1, source_target_pairs={{0,16},{4,20},{8,24},{12,28},{16,0},{20,4},{24,8},{28,12},{1,17},{... | collective-permute-start | bytes 33800 | tf_op jit(solution)/shard_map/ppermute | solution.py:492

commit v6 on v5

--- a/solution.py
+++ b/solution.py
@@ -352,15 +352,11 @@
         run(start + steps * step, count % step)
 
 
-def strips_of(stride, low_ref, mid_ref, high_ref):
-    strips = {}
-    for s in range(-5, 0):
-        strips[s] = (low_ref, s + 5)
-    for s in range(stride):
-        strips[s] = (mid_ref, s)
-    for s in range(stride, stride + 5):
-        strips[s] = (high_ref, s - stride)
-    return strips
+STRIPS = ("low", "last", "mid", "high", "final")
+
+
+def strips_of(refs):
+    return dict(enumerate(((ref, k) for ref in refs for k in range(ref.shape[0])), -5))
 
 
 def shift_sums(chunk, stride, step, x, h, u, l, w, t):
@@ -390,9 +386,10 @@
     return donut, lower, six(t), below + at(u, 0) + above
 
 
-def observed_kernel(nd, nb, chunk, step, base, low_ref, mid_ref, high_ref, near_ref, fan_ref, out_ref, x_ref, *refs):
+def observed_kernel(nd, nb, chunk, step, base, *refs):
     stride = nb // LANES
-    strips = strips_of(stride, low_ref, mid_ref, high_ref)
+    strips = strips_of(refs[: len(STRIPS)])
+    near_ref, fan_ref, out_ref, x_ref, *refs = refs[len(STRIPS) :]
 
     def fill(r0, size):
         for s, (ref, k) in strips.items():
@@ -412,13 +409,14 @@
     over(RIM, chunk, step, emit)
 
 
-def score_kernel(nd, nb, chunk, step, low_ref, mid_ref, high_ref, diag_ref, perm_ref, *rest):
+def score_kernel(nd, nb, chunk, step, *rest):
     stride = nb // LANES
     count = nd // chunk
+    strips = strips_of(rest[: len(STRIPS)])
+    diag_ref, perm_ref, *rest = rest[len(STRIPS) :]
     seen_refs, out_hbm = rest[:count], rest[count]
     col_ref, out_ref, sems, x_ref = rest[count + 1 : count + 5]
     refs = rest[count + 5 :]
-    strips = strips_of(stride, low_ref, mid_ref, high_ref)
     tiles = diag_ref.shape[0] // 2
     expected = diag_ref[:tiles, :] / jnp.maximum(diag_ref[tiles:, :], 1.0)
     expected = jnp.where(expected > 0.0, expected, 1.0)
@@ -556,7 +554,7 @@
         1: (("top",), lambda top: dict(below=shifted(top, "offset", -1))),
         3: (("w", "above", "below"), first_side),
     }
-    sums = total(part, ("genome", "offset"), state, tasks, {1: ("above",), 2: ("below",)})
+    sums = total(part, ("offset", "genome"), state, tasks, {1: ("above",), 2: ("below",)})
     w = state["w"]
 
     part, bias = pl.pallas_call(
@@ -590,8 +588,13 @@
             )(*operands)
             return {name: strips}
 
-        side = dict(low="before", mid="above", high="after")[name]
+        side = dict(low="before", last="before", mid="above", high="after", final="after")[name]
         return ("w", "above", "below", side, side), run
+
+    def ends(w, above, below, before, after):
+        made = strip("last", -1, 1)[1](w, above, below, before, before)
+        made.update(strip("final", cols + 4, 1)[1](w, above, below, after, after))
+        return made
 
     def back(_, right):
         matrix = pl.pallas_call(
@@ -606,13 +609,14 @@
     tasks = {
         0: (("keep", "right"), back),
         1: strip("mid", 0, cols),
-        2: strip("high", cols, 5),
-        3: strip("low", -5, 5),
+        2: strip("high", cols, 4),
+        3: strip("low", -5, 4),
+        4: (("w", "above", "below", "before", "after"), ends),
     }
     state["keep"] = keep
-    due = {0: ("perm", "after"), 1: ("mid",), 2: ("high", "before"), 3: ("low",)}
-    sums = total(part, ("genome", "offset"), state, tasks, due)
-    low, high, mid, perm, keep = (state[name] for name in ("low", "high", "mid", "perm", "keep"))
+    due = {0: ("perm", "after"), 1: ("mid",), 2: ("high", "before"), 3: ("low",), 4: ("last", "final")}
+    sums = total(part, ("offset", "genome"), state, tasks, due)
+    mid, perm, keep = (state[name] for name in ("mid", "perm", "keep"))
 
     padded = -(-total_rows // LANES) * LANES
     fan_len = fan_rows(nd)
@@ -647,7 +651,7 @@
                 made[f"seen{c}"] = pl.pallas_call(
                     functools.partial(observed_kernel, nd, nb, chunk, STEP, c * chunk),
                     out_shape=f(5 * cols, chunk, LANES),
-                    in_specs=[VMEM] * 5,
+                    in_specs=[VMEM] * len(operands),
                     out_specs=VMEM,
                     scratch_shapes=scratch,
                     compiler_params=params(20),
@@ -655,7 +659,7 @@
                 )(*operands)
             return made
 
-        return ("low", "mid", "high", "near", "fan"), run
+        return STRIPS + ("near", "fan"), run
 
     rounds = (lax.axis_size("genome") - 1).bit_length()
     turns = {}
@@ -670,7 +674,7 @@
         {k: tuple(f"seen{c}" for c in which) for k, which in turns.items()},
     )
 
-    operands = (low, mid, high, diag, perm) + tuple(state[f"seen{c}"] for c in range(count))
+    operands = tuple(state[name] for name in STRIPS) + (diag, perm) + tuple(state[f"seen{c}"] for c in range(count))
     score = pl.pallas_call(
         functools.partial(score_kernel, nd, nb, chunk, STEP),
         out_shape=f(nd, nb),

time: 71.5 us -> 70.4 us (0.985)
  starting transfers between devices: 28 us -> 23.3 us
  waiting for transfers between devices: 8.88 us -> 12.4 us
    ppermute x4, starting transfers between devices: 9.47 us -> 5.79 us  [shifted(): lax.ppermute(x, axis, pairs if step > 0 else [(j, i) for i, j in pairs])]
    ppermute x4, waiting for transfers between devices: 0.01 us -> 2.86 us  [shifted(): lax.ppermute(x, axis, pairs if step > 0 else [(j, i) for i, j in pairs])]
    ppermute x13, starting transfers between devices: 18.5 us -> 17.5 us  [total(): came = lax.ppermute(x, axis, pairs)]
    ppermute x13, waiting for transfers between devices: 8.87 us -> 9.59 us  [total(): came = lax.ppermute(x, axis, pairs)]
    pallas_call x3 -> x5, Pallas kernels: 6.79 us -> 7.1 us  [run(): pl.pallas_call(functools.partial(strip_kernel, nd, nb, first, count), out...]
  transfers between devices with their start and end apart: 17 -> 17, of which waited for: 7 -> 10; matrix products, arithmetic and copies ran while one was open for 0% -> 0% of each run, Pallas kernels for 22% -> 23%
where the time goes in v6:
time: 70.4 us; the launch traced here: 70.2 us
  Pallas kernels  33.3 us (47%)
  starting transfers between devices  23.3 us (33%)
  waiting for transfers between devices  12.4 us (18%)
  between operations  1.01 us (1%)
    ppermute x13, starting transfers between devices, total(): came = lax.ppermute(x, axis, pairs)  17.5 us
    pallas_call x1, Pallas kernels, on_device(): pl.pallas_call(functools.partial(score_kernel, nd, nb, chunk, STEP), out_...  11.8 us
    ppermute x13, waiting for transfers between devices, total(): came = lax.ppermute(x, axis, pairs)  9.59 us
    pallas_call x5, Pallas kernels, run(): pl.pallas_call(functools.partial(strip_kernel, nd, nb, first, count), out...  7.1 us
    pallas_call x4, Pallas kernels, run(): pl.pallas_call(functools.partial(observed_kernel, nd, nb, chunk, STEP, c...  6.89 us
    ppermute x4, starting transfers between devices, shifted(): lax.ppermute(x, axis, pairs if step > 0 else [(j, i) for i, j in pairs])  5.79 us
    pallas_call x1, Pallas kernels, on_device(): pl.pallas_call(functools.partial(first_kernel, nd, nb), out_shape=(shape(...  2.98 us
    ppermute x4, waiting for transfers between devices, shifted(): lax.ppermute(x, axis, pairs if step > 0 else [(j, i) for i, j in pairs])  2.86 us
  transfers between devices with their start and end apart: 17, of which 10 were waited for; matrix products, arithmetic and copies ran while one was open for 0% of the time, Pallas kernels for 23%

profile of v6, /device:TPU:0, one launch (start us, length us, event | category | flops | bytes accessed | tf_op | source)
XLA Modules:
  0.0 70.2 jit_solution(1689119729991670637)
XLA Ops:
  0.6 3.0 %first_sums.1 = (bf16[1280,640]{1,0:T(8,128)(2,1)S(1)}, f32[40,128]{1,0:T(8,128)S(1)}, f32[40,128]{1,0:T(8,128)S(1)}, f32[16,640]{1,0:T(8,128)S(1)}, f32[16,640]{1,0:T(8,128)S(1)}) custom-call(s32[2]{0:T(128)} %bounds_hbm.1, bf16[1280,640]{1,0:T(8,128)(2,1)} %x_hbm.1, s32[1,128]{1,0:T(1,128)} %bitcast.2), custom_call_target="tpu_custom_call" | custom-call | tf_op jit(solution)/shard_map/first_sums/pallas_call | solution.py:518
  3.6 3.1 %collective-permute-start = (f32[40,128]{1,0:T(8,128)S(1)}, f32[40,128]{1,0:T(8,128)S(1)}, u32[]{:S(2)}, u32[]{:S(2)}) collective-permute-start(f32[40,128]{1,0:T(8,128)S(1)} %get-tuple-element.96), channel_id=1, source_target_pairs={{0,1},{1,0},{2,3},{3,2},{4,5},{5,4},{6,7},{7,6},{8,9},{9,8},{10,11... | collective-permute-start | bytes 61448 | tf_op jit(solution)/shard_map/ppermute | solution.py:490
  6.7 1.9 %collective-permute-start.2 = (f32[16,640]{1,0:T(8,128)S(1)}, f32[16,640]{1,0:T(8,128)S(1)}, u32[]{:S(2)}, u32[]{:S(2)}) collective-permute-start(f32[16,640]{1,0:T(8,128)S(1)} %get-tuple-element.99), channel_id=1, source_target_pairs={{0,1},{1,2},{2,3},{4,5},{5,6},{6,7},{8,9},{9,10},{10,11},{12,13},{... | collective-permute-start | bytes 122888 | tf_op jit(solution)/shard_map/ppermute | solution.py:503
  8.6 0.0 collective-permute-done
  8.7 3.1 %collective-permute-start.1 = (f32[40,128]{1,0:T(8,128)S(1)}, f32[40,128]{1,0:T(8,128)S(1)}, u32[]{:S(2)}, u32[]{:S(2)}) collective-permute-start(f32[40,128]{1,0:T(8,128)S(1)} %add.39), channel_id=1, source_target_pairs={{0,2},{1,3},{2,0},{3,1},{4,6},{5,7},{6,4},{7,5},{8,10},{9,11},{10,... | collective-permute-start | bytes 61448 | tf_op jit(solution)/shard_map/ppermute | solution.py:490
  11.7 1.3 %collective-permute-start.4 = (f32[16,640]{1,0:T(8,128)S(1)}, f32[16,640]{1,0:T(8,128)S(1)}, u32[]{:S(2)}, u32[]{:S(2)}) collective-permute-start(f32[16,640]{1,0:T(8,128)S(1)} %get-tuple-element.101), channel_id=1, source_target_pairs={{1,0},{2,1},{3,2},{5,4},{6,5},{7,6},{9,8},{10,9},{11,10},{13,12},{... | collective-permute-start | bytes 122888 | tf_op jit(solution)/shard_map/ppermute | solution.py:503
  13.0 0.5 collective-permute-done.1
  13.5 0.0 collective-permute-done.2.top_ref.left_ref.right_ref
  13.5 0.1 collective-permute-start.3
  13.6 1.2 %collective-permute-done.3 = f32[40,128]{1,0:T(8,128)S(1)} collective-permute-done((f32[40,128]{1,0:T(8,128)S(1)}, f32[40,128]{1,0:T(8,128)S(1)}, u32[]{:S(2)}, u32[]{:S(2)}) %collective-permute-start.3) | collective-permute-done | bytes 20512 | tf_op jit(solution)/shard_map/ppermute | solution.py:490
  14.8 2.9 %collective-permute-done.4.bottom_ref = f32[16,640]{1,0:T(8,128)S(1)} collective-permute-done((f32[16,640]{1,0:T(8,128)S(1)}, f32[16,640]{1,0:T(8,128)S(1)}, u32[]{:S(2)}, u32[]{:S(2)}) %collective-permute-start.4) | collective-permute-done | bytes 40992 | tf_op jit(solution)/shard_map/ppermute | solution.py:503
  17.6 1.5 %collective-permute-start.5 = (f32[40,128]{1,0:T(8,128)S(1)}, f32[40,128]{1,0:T(8,128)S(1)}, u32[]{:S(2)}, u32[]{:S(2)}) collective-permute-start(f32[40,128]{1,0:T(8,128)S(1)} %add.41), channel_id=1, source_target_pairs={{0,8},{4,12},{8,0},{12,4},{16,24},{20,28},{24,16},{28,20},{1,9},{5... | collective-permute-start | bytes 61448 | tf_op jit(solution)/shard_map/ppermute | solution.py:490
  19.1 0.3 sides.1
  19.4 1.3 %collective-permute-start.8 = (f32[8,1312]{1,0:T(8,128)S(1)}, f32[8,1312]{1,0:T(8,128)S(1)}, u32[]{:S(2)}, u32[]{:S(2)}) collective-permute-start(f32[8,1312]{1,0:T(8,128)S(1)} %get-tuple-element.114), channel_id=1, source_target_pairs={{4,0},{8,4},{12,8},{16,12},{20,16},{24,20},{28,24},{5,1},{9,5},{13... | collective-permute-start | bytes 125960 | tf_op jit(solution)/shard_map/ppermute | solution.py:503
  20.7 0.7 %collective-permute-done.5 = f32[40,128]{1,0:T(8,128)S(1)} collective-permute-done((f32[40,128]{1,0:T(8,128)S(1)}, f32[40,128]{1,0:T(8,128)S(1)}, u32[]{:S(2)}, u32[]{:S(2)}) %collective-permute-start.5) | collective-permute-done | bytes 20512 | tf_op jit(solution)/shard_map/ppermute | solution.py:490
  21.4 1.5 %collective-permute-start.6 = (f32[40,128]{1,0:T(8,128)S(1)}, f32[40,128]{1,0:T(8,128)S(1)}, u32[]{:S(2)}, u32[]{:S(2)}) collective-permute-start(f32[40,128]{1,0:T(8,128)S(1)} %add.42), channel_id=1, source_target_pairs={{0,16},{4,20},{8,24},{12,28},{16,0},{20,4},{24,8},{28,12},{1,17},{... | collective-permute-start | bytes 61448 | tf_op jit(solution)/shard_map/ppermute | solution.py:490
  22.9 2.3 %collective-permute-done.6 = f32[40,128]{1,0:T(8,128)S(1)} collective-permute-done((f32[40,128]{1,0:T(8,128)S(1)}, f32[40,128]{1,0:T(8,128)S(1)}, u32[]{:S(2)}, u32[]{:S(2)}) %collective-permute-start.6) | collective-permute-done | bytes 20512 | tf_op jit(solution)/shard_map/ppermute | solution.py:490
  25.2 1.9 %second_sums.1 = (f32[40,128]{1,0:T(8,128)S(1)}, f32[40,128]{1,0:T(8,128)S(1)}) custom-call(bf16[1280,640]{1,0:T(8,128)(2,1)S(1)} %get-tuple-element.138.w_ref, f32[40,128]{1,0:T(8,128)S(1)} %add.43.sums_ref, f32[40,128]{1,0:T(8,128)S(1)} %get-tuple-element.144.keep_ref), custom_call_target="tpu_custom_call" | custom-call | tf_op jit(solution)/shard_map/second_sums/pallas_call | solution.py:560
  27.1 1.4 %collective-permute-start.7 = (f32[40,128]{1,0:T(8,128)S(1)}, f32[40,128]{1,0:T(8,128)S(1)}, u32[]{:S(2)}, u32[]{:S(2)}) collective-permute-start(f32[40,128]{1,0:T(8,128)S(1)} %get-tuple-element.113), channel_id=1, source_target_pairs={{0,1},{1,0},{2,3},{3,2},{4,5},{5,4},{6,7},{7,6},{8,9},{9,8},{10,11... | collective-permute-start | bytes 61448 | tf_op jit(solution)/shard_map/ppermute | solution.py:490
  28.5 0.2 unstrip.1.rest_6_
  28.6 1.3 %collective-permute-start.11 = (f32[8,1312]{1,0:T(8,128)S(1)}, f32[8,1312]{1,0:T(8,128)S(1)}, u32[]{:S(2)}, u32[]{:S(2)}) collective-permute-start(f32[8,1312]{1,0:T(8,128)S(1)} %get-tuple-element.128), channel_id=1, source_target_pairs={{0,4},{4,8},{8,12},{12,16},{16,20},{20,24},{24,28},{1,5},{5,9},{9,... | collective-permute-start | bytes 125960 | tf_op jit(solution)/shard_map/ppermute | solution.py:503
  29.9 1.0 %collective-permute-done.7 = f32[40,128]{1,0:T(8,128)S(1)} collective-permute-done((f32[40,128]{1,0:T(8,128)S(1)}, f32[40,128]{1,0:T(8,128)S(1)}, u32[]{:S(2)}, u32[]{:S(2)}) %collective-permute-start.7) | collective-permute-done | bytes 20512 | tf_op jit(solution)/shard_map/ppermute | solution.py:490
  30.9 0.0 collective-permute-done.8.left_ref.right_ref
  30.9 0.5 collective-permute-start.9
  31.5 2.0 %strips.5.mid_ref.refs_2_.rest_2_ = bf16[5,1312,128]{2,1,0:T(8,128)(2,1)S(1)} custom-call(bf16[1280,640]{1,0:T(8,128)(2,1)S(1)} %get-tuple-element.138.w_ref, f32[16,640]{1,0:T(8,128)S(1)} %collective-permute-done.2.top_ref.left_ref.right_ref, f32[16,640]{1,0:T(8,128)S(1)} %collective-permute-done.4.bottom_ref, ...), custom_call_target="tpu_custom_call" | custom-call | tf_op jit(solution)/shard_map/strips/pallas_call | solution.py:577
  33.5 2.2 %collective-permute-done.9 = f32[40,128]{1,0:T(8,128)S(1)} collective-permute-done((f32[40,128]{1,0:T(8,128)S(1)}, f32[40,128]{1,0:T(8,128)S(1)}, u32[]{:S(2)}, u32[]{:S(2)}) %collective-permute-start.9) | collective-permute-done | bytes 20512 | tf_op jit(solution)/shard_map/ppermute | solution.py:490
  35.7 0.1 collective-permute-start.10
  35.8 1.8 %strips.6.refs_3_.rest_3_ = bf16[4,1312,128]{2,1,0:T(8,128)(2,1)S(1)} custom-call(bf16[1280,640]{1,0:T(8,128)(2,1)S(1)} %get-tuple-element.138.w_ref, f32[16,640]{1,0:T(8,128)S(1)} %collective-permute-done.2.top_ref.left_ref.right_ref, f32[16,640]{1,0:T(8,128)S(1)} %collective-permute-done.4.bottom_ref, ...), custom_call_target="tpu_custom_call" | custom-call | tf_op jit(solution)/shard_map/strips/pallas_call | solution.py:577
  37.6 0.0 collective-permute-done.10
  37.6 0.0 collective-permute-done.11.left_ref.right_ref
  37.6 1.6 %collective-permute-start.12 = (f32[40,128]{1,0:T(8,128)S(1)}, f32[40,128]{1,0:T(8,128)S(1)}, u32[]{:S(2)}, u32[]{:S(2)}) collective-permute-start(f32[40,128]{1,0:T(8,128)S(1)} %add.46), channel_id=1, source_target_pairs={{0,8},{4,12},{8,0},{12,4},{16,24},{20,28},{24,16},{28,20},{1,9},{5... | collective-permute-start | bytes 61448 | tf_op jit(solution)/shard_map/ppermute | solution.py:490
  39.2 1.8 %strips.7.refs_0_.rest_0_ = bf16[4,1312,128]{2,1,0:T(8,128)(2,1)S(1)} custom-call(bf16[1280,640]{1,0:T(8,128)(2,1)S(1)} %get-tuple-element.138.w_ref, f32[16,640]{1,0:T(8,128)S(1)} %collective-permute-done.2.top_ref.left_ref.right_ref, f32[16,640]{1,0:T(8,128)S(1)} %collective-permute-done.4.bottom_ref, ...), custom_call_target="tpu_custom_call" | custom-call | tf_op jit(solution)/shard_map/strips/pallas_call | solution.py:577
  41.0 0.5 collective-permute-done.12
  41.5 1.5 %collective-permute-start.13 = (f32[40,128]{1,0:T(8,128)S(1)}, f32[40,128]{1,0:T(8,128)S(1)}, u32[]{:S(2)}, u32[]{:S(2)}) collective-permute-start(f32[40,128]{1,0:T(8,128)S(1)} %add.47), channel_id=1, source_target_pairs={{0,16},{4,20},{8,24},{12,28},{16,0},{20,4},{24,8},{28,12},{1,17},{... | collective-permute-start | bytes 61448 | tf_op jit(solution)/shard_map/ppermute | solution.py:490
  43.0 0.8 %strips.8.refs_1_.rest_1_ = bf16[1,1312,128]{2,1,0:T(8,128)(2,1)S(1)} custom-call(bf16[1280,640]{1,0:T(8,128)(2,1)S(1)} %get-tuple-element.138.w_ref, f32[16,640]{1,0:T(8,128)S(1)} %collective-permute-done.2.top_ref.left_ref.right_ref, f32[16,640]{1,0:T(8,128)S(1)} %collective-permute-done.4.bottom_ref, ...), custom_call_target="tpu_custom_call" | custom-call | tf_op jit(solution)/shard_map/strips/pallas_call | solution.py:577
  43.8 0.8 %strips.9.refs_4_.rest_4_ = bf16[1,1312,128]{2,1,0:T(8,128)(2,1)S(1)} custom-call(bf16[1280,640]{1,0:T(8,128)(2,1)S(1)} %get-tuple-element.138.w_ref, f32[16,640]{1,0:T(8,128)S(1)} %collective-permute-done.2.top_ref.left_ref.right_ref, f32[16,640]{1,0:T(8,128)S(1)} %collective-permute-done.4.bottom_ref, ...), custom_call_target="tpu_custom_call" | custom-call | tf_op jit(solution)/shard_map/strips/pallas_call | solution.py:577
  44.6 0.7 %collective-permute-done.13 = f32[40,128]{1,0:T(8,128)S(1)} collective-permute-done((f32[40,128]{1,0:T(8,128)S(1)}, f32[40,128]{1,0:T(8,128)S(1)}, u32[]{:S(2)}, u32[]{:S(2)}) %collective-permute-start.13) | collective-permute-done | bytes 20512 | tf_op jit(solution)/shard_map/ppermute | solution.py:490
  45.3 2.3 %diagonal_sums.1 = (f32[5,128]{1,0:T(8,128)}, f32[1344,128]{1,0:T(8,128)S(1)}, f32[24,128]{1,0:T(8,128)S(1)}, f32[22,128]{1,0:T(8,128)S(1)}) custom-call(bf16[5,1312,128]{2,1,0:T(8,128)(2,1)S(1)} %strips.5.mid_ref.refs_2_.rest_2_, f32[40,128]{1,0:T(8,128)S(1)} %add.48.sums_ref, f32[40,128]{1,0:T(8,128)S(1)} %get-tuple-element.144.keep_ref, ...), custom_call_target="tpu_custom_call" | custom-call | tf_op jit(solution)/shard_map/diagonal_sums/pallas_call | solution.py:626
  47.6 0.1 collective-permute-start.14
  47.7 1.7 %observed.4.rest_7_ = f32[25,320,128]{2,1,0:T(8,128)S(1)} custom-call(bf16[4,1312,128]{2,1,0:T(8,128)(2,1)S(1)} %strips.7.refs_0_.rest_0_, bf16[1,1312,128]{2,1,0:T(8,128)(2,1)S(1)} %strips.8.refs_1_.rest_1_, bf16[5,1312,128]{2,1,0:T(8,128)(2,1)S(1)} %strips.5.mid_ref.refs_2_.rest_2_, bf16[4,1312,128]{2,1,0:T(8,128)(2,1)S(1)} %strips.6.refs_3_.rest_3_, ...), custom_call_target="tpu_custom_call" | custom-call | tf_op jit(solution)/shard_map/observed/pallas_call | solution.py:651
  49.4 1.6 %collective-permute-start.15 = (f32[22,128]{1,0:T(8,128)S(1)}, f32[22,128]{1,0:T(8,128)S(1)}, u32[]{:S(2)}, u32[]{:S(2)}) collective-permute-start(f32[22,128]{1,0:T(8,128)S(1)} %add.49), channel_id=1, source_target_pairs={{0,8},{4,12},{8,0},{12,4},{16,24},{20,28},{24,16},{28,20},{1,9},{5... | collective-permute-start | bytes 33800 | tf_op jit(solution)/shard_map/ppermute | solution.py:490
  51.0 1.7 %observed.6.rest_9_ = f32[25,320,128]{2,1,0:T(8,128)S(1)} custom-call(bf16[4,1312,128]{2,1,0:T(8,128)(2,1)S(1)} %strips.7.refs_0_.rest_0_, bf16[1,1312,128]{2,1,0:T(8,128)(2,1)S(1)} %strips.8.refs_1_.rest_1_, bf16[5,1312,128]{2,1,0:T(8,128)(2,1)S(1)} %strips.5.mid_ref.refs_2_.rest_2_, bf16[4,1312,128]{2,1,0:T(8,128)(2,1)S(1)} %strips.6.refs_3_.rest_3_, ...), custom_call_target="tpu_custom_call" | custom-call | tf_op jit(solution)/shard_map/observed/pallas_call | solution.py:651
  52.7 1.7 %observed.5.rest_8_ = f32[25,320,128]{2,1,0:T(8,128)S(1)} custom-call(bf16[4,1312,128]{2,1,0:T(8,128)(2,1)S(1)} %strips.7.refs_0_.rest_0_, bf16[1,1312,128]{2,1,0:T(8,128)(2,1)S(1)} %strips.8.refs_1_.rest_1_, bf16[5,1312,128]{2,1,0:T(8,128)(2,1)S(1)} %strips.5.mid_ref.refs_2_.rest_2_, bf16[4,1312,128]{2,1,0:T(8,128)(2,1)S(1)} %strips.6.refs_3_.rest_3_, ...), custom_call_target="tpu_custom_call" | custom-call | tf_op jit(solution)/shard_map/observed/pallas_call | solution.py:651
  54.4 0.0 collective-permute-done.15
  54.5 1.4 %collective-permute-start.16 = (f32[22,128]{1,0:T(8,128)S(1)}, f32[22,128]{1,0:T(8,128)S(1)}, u32[]{:S(2)}, u32[]{:S(2)}) collective-permute-start(f32[22,128]{1,0:T(8,128)S(1)} %add.50), channel_id=1, source_target_pairs={{0,16},{4,20},{8,24},{12,28},{16,0},{20,4},{24,8},{28,12},{1,17},{... | collective-permute-start | bytes 33800 | tf_op jit(solution)/shard_map/ppermute | solution.py:490
  55.9 1.7 %observed.7.rest_10_ = f32[25,320,128]{2,1,0:T(8,128)S(1)} custom-call(bf16[4,1312,128]{2,1,0:T(8,128)(2,1)S(1)} %strips.7.refs_0_.rest_0_, bf16[1,1312,128]{2,1,0:T(8,128)(2,1)S(1)} %strips.8.refs_1_.rest_1_, bf16[5,1312,128]{2,1,0:T(8,128)(2,1)S(1)} %strips.5.mid_ref.refs_2_.rest_2_, bf16[4,1312,128]{2,1,0:T(8,128)(2,1)S(1)} %strips.6.refs_3_.rest_3_, ...), custom_call_target="tpu_custom_call" | custom-call | tf_op jit(solution)/shard_map/observed/pallas_call | solution.py:651
  57.6 0.6 collective-permute-done.16
  58.2 11.8 %score.1 = f32[1280,640]{1,0:T(8,128)} custom-call(bf16[4,1312,128]{2,1,0:T(8,128)(2,1)S(1)} %strips.7.refs_0_.rest_0_, bf16[1,1312,128]{2,1,0:T(8,128)(2,1)S(1)} %strips.8.refs_1_.rest_1_, bf16[5,1312,128]{2,1,0:T(8,128)(2,1)S(1)} %strips.5.mid_ref.refs_2_.rest_2_, bf16[4,1312,128]{2,1,0:T(8,128)(2,1)S(1)} %strips.6.refs_3_.rest_3_, ...), custom_call_target="tpu_custom_call" | custom-call | tf_op jit(solution)/shard_map/score/pallas_call | solution.py:678
  (14 shorter events, 0.1 us)
Async XLA Ops:
  3.6 5.0 %collective-permute-start = (f32[40,128]{1,0:T(8,128)S(1)}, f32[40,128]{1,0:T(8,128)S(1)}, u32[]{:S(2)}, u32[]{:S(2)}) collective-permute-start(f32[40,128]{1,0:T(8,128)S(1)} %get-tuple-element.96), channel_id=1, source_target_pairs={{0,1},{1,0},{2,3},{3,2},{4,5},{5,4},{6,7},{7,6},{8,9},{9,8},{10,11... | collective-permute-start | bytes 61448 | tf_op jit(solution)/shard_map/ppermute | solution.py:490
  6.7 6.8 %collective-permute-start.2 = (f32[16,640]{1,0:T(8,128)S(1)}, f32[16,640]{1,0:T(8,128)S(1)}, u32[]{:S(2)}, u32[]{:S(2)}) collective-permute-start(f32[16,640]{1,0:T(8,128)S(1)} %get-tuple-element.99), channel_id=1, source_target_pairs={{0,1},{1,2},{2,3},{4,5},{5,6},{6,7},{8,9},{9,10},{10,11},{12,13},{... | collective-permute-start | bytes 122888 | tf_op jit(solution)/shard_map/ppermute | solution.py:503
  8.7 4.8 %collective-permute-start.1 = (f32[40,128]{1,0:T(8,128)S(1)}, f32[40,128]{1,0:T(8,128)S(1)}, u32[]{:S(2)}, u32[]{:S(2)}) collective-permute-start(f32[40,128]{1,0:T(8,128)S(1)} %add.39), channel_id=1, source_target_pairs={{0,2},{1,3},{2,0},{3,1},{4,6},{5,7},{6,4},{7,5},{8,10},{9,11},{10,... | collective-permute-start | bytes 61448 | tf_op jit(solution)/shard_map/ppermute | solution.py:490
  11.7 5.9 %collective-permute-start.4 = (f32[16,640]{1,0:T(8,128)S(1)}, f32[16,640]{1,0:T(8,128)S(1)}, u32[]{:S(2)}, u32[]{:S(2)}) collective-permute-start(f32[16,640]{1,0:T(8,128)S(1)} %get-tuple-element.101), channel_id=1, source_target_pairs={{1,0},{2,1},{3,2},{5,4},{6,5},{7,6},{9,8},{10,9},{11,10},{13,12},{... | collective-permute-start | bytes 122888 | tf_op jit(solution)/shard_map/ppermute | solution.py:503
  13.5 1.3 %collective-permute-start.3 = (f32[40,128]{1,0:T(8,128)S(1)}, f32[40,128]{1,0:T(8,128)S(1)}, u32[]{:S(2)}, u32[]{:S(2)}) collective-permute-start(f32[40,128]{1,0:T(8,128)S(1)} %add.40), channel_id=1, source_target_pairs={{0,4},{4,0},{8,12},{12,8},{16,20},{20,16},{24,28},{28,24},{1,5},{5... | collective-permute-start | bytes 61448 | tf_op jit(solution)/shard_map/ppermute | solution.py:490
  17.6 3.8 %collective-permute-start.5 = (f32[40,128]{1,0:T(8,128)S(1)}, f32[40,128]{1,0:T(8,128)S(1)}, u32[]{:S(2)}, u32[]{:S(2)}) collective-permute-start(f32[40,128]{1,0:T(8,128)S(1)} %add.41), channel_id=1, source_target_pairs={{0,8},{4,12},{8,0},{12,4},{16,24},{20,28},{24,16},{28,20},{1,9},{5... | collective-permute-start | bytes 61448 | tf_op jit(solution)/shard_map/ppermute | solution.py:490
  19.4 11.5 %collective-permute-start.8 = (f32[8,1312]{1,0:T(8,128)S(1)}, f32[8,1312]{1,0:T(8,128)S(1)}, u32[]{:S(2)}, u32[]{:S(2)}) collective-permute-start(f32[8,1312]{1,0:T(8,128)S(1)} %get-tuple-element.114), channel_id=1, source_target_pairs={{4,0},{8,4},{12,8},{16,12},{20,16},{24,20},{28,24},{5,1},{9,5},{13... | collective-permute-start | bytes 125960 | tf_op jit(solution)/shard_map/ppermute | solution.py:503
  21.4 3.8 %collective-permute-start.6 = (f32[40,128]{1,0:T(8,128)S(1)}, f32[40,128]{1,0:T(8,128)S(1)}, u32[]{:S(2)}, u32[]{:S(2)}) collective-permute-start(f32[40,128]{1,0:T(8,128)S(1)} %add.42), channel_id=1, source_target_pairs={{0,16},{4,20},{8,24},{12,28},{16,0},{20,4},{24,8},{28,12},{1,17},{... | collective-permute-start | bytes 61448 | tf_op jit(solution)/shard_map/ppermute | solution.py:490
  27.1 3.8 %collective-permute-start.7 = (f32[40,128]{1,0:T(8,128)S(1)}, f32[40,128]{1,0:T(8,128)S(1)}, u32[]{:S(2)}, u32[]{:S(2)}) collective-permute-start(f32[40,128]{1,0:T(8,128)S(1)} %get-tuple-element.113), channel_id=1, source_target_pairs={{0,1},{1,0},{2,3},{3,2},{4,5},{5,4},{6,7},{7,6},{8,9},{9,8},{10,11... | collective-permute-start | bytes 61448 | tf_op jit(solution)/shard_map/ppermute | solution.py:490
  28.6 9.0 %collective-permute-start.11 = (f32[8,1312]{1,0:T(8,128)S(1)}, f32[8,1312]{1,0:T(8,128)S(1)}, u32[]{:S(2)}, u32[]{:S(2)}) collective-permute-start(f32[8,1312]{1,0:T(8,128)S(1)} %get-tuple-element.128), channel_id=1, source_target_pairs={{0,4},{4,8},{8,12},{12,16},{16,20},{20,24},{24,28},{1,5},{5,9},{9,... | collective-permute-start | bytes 125960 | tf_op jit(solution)/shard_map/ppermute | solution.py:503
  30.9 4.7 %collective-permute-start.9 = (f32[40,128]{1,0:T(8,128)S(1)}, f32[40,128]{1,0:T(8,128)S(1)}, u32[]{:S(2)}, u32[]{:S(2)}) collective-permute-start(f32[40,128]{1,0:T(8,128)S(1)} %add.44), channel_id=1, source_target_pairs={{0,2},{1,3},{2,0},{3,1},{4,6},{5,7},{6,4},{7,5},{8,10},{9,11},{10,... | collective-permute-start | bytes 61448 | tf_op jit(solution)/shard_map/ppermute | solution.py:490
  35.7 1.9 %collective-permute-start.10 = (f32[40,128]{1,0:T(8,128)S(1)}, f32[40,128]{1,0:T(8,128)S(1)}, u32[]{:S(2)}, u32[]{:S(2)}) collective-permute-start(f32[40,128]{1,0:T(8,128)S(1)} %add.45), channel_id=1, source_target_pairs={{0,4},{4,0},{8,12},{12,8},{16,20},{20,16},{24,28},{28,24},{1,5},{5... | collective-permute-start | bytes 61448 | tf_op jit(solution)/shard_map/ppermute | solution.py:490
  37.6 3.9 %collective-permute-start.12 = (f32[40,128]{1,0:T(8,128)S(1)}, f32[40,128]{1,0:T(8,128)S(1)}, u32[]{:S(2)}, u32[]{:S(2)}) collective-permute-start(f32[40,128]{1,0:T(8,128)S(1)} %add.46), channel_id=1, source_target_pairs={{0,8},{4,12},{8,0},{12,4},{16,24},{20,28},{24,16},{28,20},{1,9},{5... | collective-permute-start | bytes 61448 | tf_op jit(solution)/shard_map/ppermute | solution.py:490
  41.5 3.8 %collective-permute-start.13 = (f32[40,128]{1,0:T(8,128)S(1)}, f32[40,128]{1,0:T(8,128)S(1)}, u32[]{:S(2)}, u32[]{:S(2)}) collective-permute-start(f32[40,128]{1,0:T(8,128)S(1)} %add.47), channel_id=1, source_target_pairs={{0,16},{4,20},{8,24},{12,28},{16,0},{20,4},{24,8},{28,12},{1,17},{... | collective-permute-start | bytes 61448 | tf_op jit(solution)/shard_map/ppermute | solution.py:490
  47.6 1.8 %collective-permute-start.14 = (f32[22,128]{1,0:T(8,128)S(1)}, f32[22,128]{1,0:T(8,128)S(1)}, u32[]{:S(2)}, u32[]{:S(2)}) collective-permute-start(f32[22,128]{1,0:T(8,128)S(1)} %get-tuple-element.153), channel_id=1, source_target_pairs={{0,4},{4,0},{8,12},{12,8},{16,20},{20,16},{24,28},{28,24},{1,5},{5... | collective-permute-start | bytes 33800 | tf_op jit(solution)/shard_map/ppermute | solution.py:490
  49.4 5.0 %collective-permute-start.15 = (f32[22,128]{1,0:T(8,128)S(1)}, f32[22,128]{1,0:T(8,128)S(1)}, u32[]{:S(2)}, u32[]{:S(2)}) collective-permute-start(f32[22,128]{1,0:T(8,128)S(1)} %add.49), channel_id=1, source_target_pairs={{0,8},{4,12},{8,0},{12,4},{16,24},{20,28},{24,16},{28,20},{1,9},{5... | collective-permute-start | bytes 33800 | tf_op jit(solution)/shard_map/ppermute | solution.py:490
  54.5 3.8 %collective-permute-start.16 = (f32[22,128]{1,0:T(8,128)S(1)}, f32[22,128]{1,0:T(8,128)S(1)}, u32[]{:S(2)}, u32[]{:S(2)}) collective-permute-start(f32[22,128]{1,0:T(8,128)S(1)} %add.50), channel_id=1, source_target_pairs={{0,16},{4,20},{8,24},{12,28},{16,0},{20,4},{24,8},{28,12},{1,17},{... | collective-permute-start | bytes 33800 | tf_op jit(solution)/shard_map/ppermute | solution.py:490

commit v7 on v6

--- a/solution.py
+++ b/solution.py
@@ -9,7 +9,7 @@
 from jax.sharding import PartitionSpec as P
 
 RIM = 16
-STEP = 176
+STEP = 88
 SIDE = 8
 LANES = 128
 F32 = jnp.float32
@@ -397,7 +397,7 @@
             near = jnp.broadcast_to(near_ref[8 + s : 9 + s, :], (size, LANES))
             x_ref[s + 5, pl.ds(r0, size), :] = w * near * fan_ref[pl.ds(base + r0 + 8 + s, size), :]
 
-    over(0, chunk + 2 * RIM, step, fill)
+    over(0, chunk + 2 * RIM, 2 * step, fill)
     shift_sums(chunk, stride, step, x_ref, *refs)
 
     def emit(r0, size):
@@ -455,7 +455,7 @@
                 w = ref[k, pl.ds(base + r0, size), :].astype(F32)
                 x_ref[s + 5, pl.ds(r0, size), :] = jnp.where(w > 0.0, e, 0.0)
 
-        over(0, chunk + 2 * RIM, step, fill)
+        over(0, chunk + 2 * RIM, 2 * step, fill)
         shift_sums(chunk, stride, step, x_ref, *refs)
         for c in range(count):
 

time: 70.4 us -> 69.3 us (0.984)
  Pallas kernels: 33.3 us -> 32 us
    pallas_call x4, Pallas kernels: 6.89 us -> 5.85 us  [run(): pl.pallas_call(functools.partial(observed_kernel, nd, nb, chunk, STEP, c...]
  transfers between devices with their start and end apart: 17 -> 17, of which waited for: 10 -> 10; matrix products, arithmetic and copies ran while one was open for 0% -> 0% of each run, Pallas kernels for 23% -> 22%
where the time goes in v7:
time: 69.3 us; the launch traced here: 69.1 us
  Pallas kernels  32 us (46%)
  starting transfers between devices  23.3 us (34%)
  waiting for transfers between devices  12.7 us (18%)
  between operations  1 us (1%)
    ppermute x13, starting transfers between devices, total(): came = lax.ppermute(x, axis, pairs)  17.5 us
    pallas_call x1, Pallas kernels, on_device(): pl.pallas_call(functools.partial(score_kernel, nd, nb, chunk, STEP), out_...  11.5 us
    ppermute x13, waiting for transfers between devices, total(): came = lax.ppermute(x, axis, pairs)  9.85 us
    pallas_call x5, Pallas kernels, run(): pl.pallas_call(functools.partial(strip_kernel, nd, nb, first, count), out...  7.1 us
    pallas_call x4, Pallas kernels, run(): pl.pallas_call(functools.partial(observed_kernel, nd, nb, chunk, STEP, c...  5.85 us
    ppermute x4, starting transfers between devices, shifted(): lax.ppermute(x, axis, pairs if step > 0 else [(j, i) for i, j in pairs])  5.79 us
    pallas_call x1, Pallas kernels, on_device(): pl.pallas_call(functools.partial(first_kernel, nd, nb), out_shape=(shape(...  2.98 us
    ppermute x4, waiting for transfers between devices, shifted(): lax.ppermute(x, axis, pairs if step > 0 else [(j, i) for i, j in pairs])  2.86 us
  transfers between devices with their start and end apart: 17, of which 10 were waited for; matrix products, arithmetic and copies ran while one was open for 0% of the time, Pallas kernels for 22%

profile of v7, /device:TPU:0, one launch (start us, length us, event | category | flops | bytes accessed | tf_op | source)
XLA Modules:
  0.0 69.1 jit_solution(15495541646951499788)
XLA Ops:
  0.6 3.0 %first_sums.1 = (bf16[1280,640]{1,0:T(8,128)(2,1)S(1)}, f32[40,128]{1,0:T(8,128)S(1)}, f32[40,128]{1,0:T(8,128)S(1)}, f32[16,640]{1,0:T(8,128)S(1)}, f32[16,640]{1,0:T(8,128)S(1)}) custom-call(s32[2]{0:T(128)} %bounds_hbm.1, bf16[1280,640]{1,0:T(8,128)(2,1)} %x_hbm.1, s32[1,128]{1,0:T(1,128)} %bitcast.2), custom_call_target="tpu_custom_call" | custom-call | tf_op jit(solution)/shard_map/first_sums/pallas_call | solution.py:518
  3.6 3.1 %collective-permute-start = (f32[40,128]{1,0:T(8,128)S(1)}, f32[40,128]{1,0:T(8,128)S(1)}, u32[]{:S(2)}, u32[]{:S(2)}) collective-permute-start(f32[40,128]{1,0:T(8,128)S(1)} %get-tuple-element.96), channel_id=1, source_target_pairs={{0,1},{1,0},{2,3},{3,2},{4,5},{5,4},{6,7},{7,6},{8,9},{9,8},{10,11... | collective-permute-start | bytes 61448 | tf_op jit(solution)/shard_map/ppermute | solution.py:490
  6.7 1.9 %collective-permute-start.2 = (f32[16,640]{1,0:T(8,128)S(1)}, f32[16,640]{1,0:T(8,128)S(1)}, u32[]{:S(2)}, u32[]{:S(2)}) collective-permute-start(f32[16,640]{1,0:T(8,128)S(1)} %get-tuple-element.99), channel_id=1, source_target_pairs={{0,1},{1,2},{2,3},{4,5},{5,6},{6,7},{8,9},{9,10},{10,11},{12,13},{... | collective-permute-start | bytes 122888 | tf_op jit(solution)/shard_map/ppermute | solution.py:503
  8.6 0.0 collective-permute-done
  8.7 3.1 %collective-permute-start.1 = (f32[40,128]{1,0:T(8,128)S(1)}, f32[40,128]{1,0:T(8,128)S(1)}, u32[]{:S(2)}, u32[]{:S(2)}) collective-permute-start(f32[40,128]{1,0:T(8,128)S(1)} %add.39), channel_id=1, source_target_pairs={{0,2},{1,3},{2,0},{3,1},{4,6},{5,7},{6,4},{7,5},{8,10},{9,11},{10,... | collective-permute-start | bytes 61448 | tf_op jit(solution)/shard_map/ppermute | solution.py:490
  11.7 1.3 %collective-permute-start.4 = (f32[16,640]{1,0:T(8,128)S(1)}, f32[16,640]{1,0:T(8,128)S(1)}, u32[]{:S(2)}, u32[]{:S(2)}) collective-permute-start(f32[16,640]{1,0:T(8,128)S(1)} %get-tuple-element.101), channel_id=1, source_target_pairs={{1,0},{2,1},{3,2},{5,4},{6,5},{7,6},{9,8},{10,9},{11,10},{13,12},{... | collective-permute-start | bytes 122888 | tf_op jit(solution)/shard_map/ppermute | solution.py:503
  13.0 0.5 collective-permute-done.1
  13.5 0.0 collective-permute-done.2.top_ref.left_ref.right_ref
  13.5 0.1 collective-permute-start.3
  13.6 1.2 %collective-permute-done.3 = f32[40,128]{1,0:T(8,128)S(1)} collective-permute-done((f32[40,128]{1,0:T(8,128)S(1)}, f32[40,128]{1,0:T(8,128)S(1)}, u32[]{:S(2)}, u32[]{:S(2)}) %collective-permute-start.3) | collective-permute-done | bytes 20512 | tf_op jit(solution)/shard_map/ppermute | solution.py:490
  14.8 2.9 %collective-permute-done.4.bottom_ref = f32[16,640]{1,0:T(8,128)S(1)} collective-permute-done((f32[16,640]{1,0:T(8,128)S(1)}, f32[16,640]{1,0:T(8,128)S(1)}, u32[]{:S(2)}, u32[]{:S(2)}) %collective-permute-start.4) | collective-permute-done | bytes 40992 | tf_op jit(solution)/shard_map/ppermute | solution.py:503
  17.6 1.5 %collective-permute-start.5 = (f32[40,128]{1,0:T(8,128)S(1)}, f32[40,128]{1,0:T(8,128)S(1)}, u32[]{:S(2)}, u32[]{:S(2)}) collective-permute-start(f32[40,128]{1,0:T(8,128)S(1)} %add.41), channel_id=1, source_target_pairs={{0,8},{4,12},{8,0},{12,4},{16,24},{20,28},{24,16},{28,20},{1,9},{5... | collective-permute-start | bytes 61448 | tf_op jit(solution)/shard_map/ppermute | solution.py:490
  19.1 0.3 sides.1
  19.4 1.3 %collective-permute-start.8 = (f32[8,1312]{1,0:T(8,128)S(1)}, f32[8,1312]{1,0:T(8,128)S(1)}, u32[]{:S(2)}, u32[]{:S(2)}) collective-permute-start(f32[8,1312]{1,0:T(8,128)S(1)} %get-tuple-element.114), channel_id=1, source_target_pairs={{4,0},{8,4},{12,8},{16,12},{20,16},{24,20},{28,24},{5,1},{9,5},{13... | collective-permute-start | bytes 125960 | tf_op jit(solution)/shard_map/ppermute | solution.py:503
  20.7 0.7 %collective-permute-done.5 = f32[40,128]{1,0:T(8,128)S(1)} collective-permute-done((f32[40,128]{1,0:T(8,128)S(1)}, f32[40,128]{1,0:T(8,128)S(1)}, u32[]{:S(2)}, u32[]{:S(2)}) %collective-permute-start.5) | collective-permute-done | bytes 20512 | tf_op jit(solution)/shard_map/ppermute | solution.py:490
  21.4 1.5 %collective-permute-start.6 = (f32[40,128]{1,0:T(8,128)S(1)}, f32[40,128]{1,0:T(8,128)S(1)}, u32[]{:S(2)}, u32[]{:S(2)}) collective-permute-start(f32[40,128]{1,0:T(8,128)S(1)} %add.42), channel_id=1, source_target_pairs={{0,16},{4,20},{8,24},{12,28},{16,0},{20,4},{24,8},{28,12},{1,17},{... | collective-permute-start | bytes 61448 | tf_op jit(solution)/shard_map/ppermute | solution.py:490
  22.9 2.3 %collective-permute-done.6 = f32[40,128]{1,0:T(8,128)S(1)} collective-permute-done((f32[40,128]{1,0:T(8,128)S(1)}, f32[40,128]{1,0:T(8,128)S(1)}, u32[]{:S(2)}, u32[]{:S(2)}) %collective-permute-start.6) | collective-permute-done | bytes 20512 | tf_op jit(solution)/shard_map/ppermute | solution.py:490
  25.2 1.9 %second_sums.1 = (f32[40,128]{1,0:T(8,128)S(1)}, f32[40,128]{1,0:T(8,128)S(1)}) custom-call(bf16[1280,640]{1,0:T(8,128)(2,1)S(1)} %get-tuple-element.138.w_ref, f32[40,128]{1,0:T(8,128)S(1)} %add.43.sums_ref, f32[40,128]{1,0:T(8,128)S(1)} %get-tuple-element.144.keep_ref), custom_call_target="tpu_custom_call" | custom-call | tf_op jit(solution)/shard_map/second_sums/pallas_call | solution.py:560
  27.1 1.4 %collective-permute-start.7 = (f32[40,128]{1,0:T(8,128)S(1)}, f32[40,128]{1,0:T(8,128)S(1)}, u32[]{:S(2)}, u32[]{:S(2)}) collective-permute-start(f32[40,128]{1,0:T(8,128)S(1)} %get-tuple-element.113), channel_id=1, source_target_pairs={{0,1},{1,0},{2,3},{3,2},{4,5},{5,4},{6,7},{7,6},{8,9},{9,8},{10,11... | collective-permute-start | bytes 61448 | tf_op jit(solution)/shard_map/ppermute | solution.py:490
  28.5 0.2 unstrip.1.rest_6_
  28.6 1.3 %collective-permute-start.11 = (f32[8,1312]{1,0:T(8,128)S(1)}, f32[8,1312]{1,0:T(8,128)S(1)}, u32[]{:S(2)}, u32[]{:S(2)}) collective-permute-start(f32[8,1312]{1,0:T(8,128)S(1)} %get-tuple-element.128), channel_id=1, source_target_pairs={{0,4},{4,8},{8,12},{12,16},{16,20},{20,24},{24,28},{1,5},{5,9},{9,... | collective-permute-start | bytes 125960 | tf_op jit(solution)/shard_map/ppermute | solution.py:503
  29.9 1.0 %collective-permute-done.7 = f32[40,128]{1,0:T(8,128)S(1)} collective-permute-done((f32[40,128]{1,0:T(8,128)S(1)}, f32[40,128]{1,0:T(8,128)S(1)}, u32[]{:S(2)}, u32[]{:S(2)}) %collective-permute-start.7) | collective-permute-done | bytes 20512 | tf_op jit(solution)/shard_map/ppermute | solution.py:490
  30.9 0.0 collective-permute-done.8.left_ref.right_ref
  30.9 0.5 collective-permute-start.9
  31.5 2.0 %strips.5.mid_ref.refs_2_.rest_2_ = bf16[5,1312,128]{2,1,0:T(8,128)(2,1)S(1)} custom-call(bf16[1280,640]{1,0:T(8,128)(2,1)S(1)} %get-tuple-element.138.w_ref, f32[16,640]{1,0:T(8,128)S(1)} %collective-permute-done.2.top_ref.left_ref.right_ref, f32[16,640]{1,0:T(8,128)S(1)} %collective-permute-done.4.bottom_ref, ...), custom_call_target="tpu_custom_call" | custom-call | tf_op jit(solution)/shard_map/strips/pallas_call | solution.py:577
  33.5 2.2 %collective-permute-done.9 = f32[40,128]{1,0:T(8,128)S(1)} collective-permute-done((f32[40,128]{1,0:T(8,128)S(1)}, f32[40,128]{1,0:T(8,128)S(1)}, u32[]{:S(2)}, u32[]{:S(2)}) %collective-permute-start.9) | collective-permute-done | bytes 20512 | tf_op jit(solution)/shard_map/ppermute | solution.py:490
  35.7 0.1 collective-permute-start.10
  35.8 1.8 %strips.6.refs_3_.rest_3_ = bf16[4,1312,128]{2,1,0:T(8,128)(2,1)S(1)} custom-call(bf16[1280,640]{1,0:T(8,128)(2,1)S(1)} %get-tuple-element.138.w_ref, f32[16,640]{1,0:T(8,128)S(1)} %collective-permute-done.2.top_ref.left_ref.right_ref, f32[16,640]{1,0:T(8,128)S(1)} %collective-permute-done.4.bottom_ref, ...), custom_call_target="tpu_custom_call" | custom-call | tf_op jit(solution)/shard_map/strips/pallas_call | solution.py:577
  37.6 0.0 collective-permute-done.10
  37.6 0.0 collective-permute-done.11.left_ref.right_ref
  37.6 1.6 %collective-permute-start.12 = (f32[40,128]{1,0:T(8,128)S(1)}, f32[40,128]{1,0:T(8,128)S(1)}, u32[]{:S(2)}, u32[]{:S(2)}) collective-permute-start(f32[40,128]{1,0:T(8,128)S(1)} %add.46), channel_id=1, source_target_pairs={{0,8},{4,12},{8,0},{12,4},{16,24},{20,28},{24,16},{28,20},{1,9},{5... | collective-permute-start | bytes 61448 | tf_op jit(solution)/shard_map/ppermute | solution.py:490
  39.2 1.8 %strips.7.refs_0_.rest_0_ = bf16[4,1312,128]{2,1,0:T(8,128)(2,1)S(1)} custom-call(bf16[1280,640]{1,0:T(8,128)(2,1)S(1)} %get-tuple-element.138.w_ref, f32[16,640]{1,0:T(8,128)S(1)} %collective-permute-done.2.top_ref.left_ref.right_ref, f32[16,640]{1,0:T(8,128)S(1)} %collective-permute-done.4.bottom_ref, ...), custom_call_target="tpu_custom_call" | custom-call | tf_op jit(solution)/shard_map/strips/pallas_call | solution.py:577
  41.0 0.5 collective-permute-done.12
  41.5 1.5 %collective-permute-start.13 = (f32[40,128]{1,0:T(8,128)S(1)}, f32[40,128]{1,0:T(8,128)S(1)}, u32[]{:S(2)}, u32[]{:S(2)}) collective-permute-start(f32[40,128]{1,0:T(8,128)S(1)} %add.47), channel_id=1, source_target_pairs={{0,16},{4,20},{8,24},{12,28},{16,0},{20,4},{24,8},{28,12},{1,17},{... | collective-permute-start | bytes 61448 | tf_op jit(solution)/shard_map/ppermute | solution.py:490
  43.0 0.8 %strips.8.refs_1_.rest_1_ = bf16[1,1312,128]{2,1,0:T(8,128)(2,1)S(1)} custom-call(bf16[1280,640]{1,0:T(8,128)(2,1)S(1)} %get-tuple-element.138.w_ref, f32[16,640]{1,0:T(8,128)S(1)} %collective-permute-done.2.top_ref.left_ref.right_ref, f32[16,640]{1,0:T(8,128)S(1)} %collective-permute-done.4.bottom_ref, ...), custom_call_target="tpu_custom_call" | custom-call | tf_op jit(solution)/shard_map/strips/pallas_call | solution.py:577
  43.8 0.8 %strips.9.refs_4_.rest_4_ = bf16[1,1312,128]{2,1,0:T(8,128)(2,1)S(1)} custom-call(bf16[1280,640]{1,0:T(8,128)(2,1)S(1)} %get-tuple-element.138.w_ref, f32[16,640]{1,0:T(8,128)S(1)} %collective-permute-done.2.top_ref.left_ref.right_ref, f32[16,640]{1,0:T(8,128)S(1)} %collective-permute-done.4.bottom_ref, ...), custom_call_target="tpu_custom_call" | custom-call | tf_op jit(solution)/shard_map/strips/pallas_call | solution.py:577
  44.6 0.7 %collective-permute-done.13 = f32[40,128]{1,0:T(8,128)S(1)} collective-permute-done((f32[40,128]{1,0:T(8,128)S(1)}, f32[40,128]{1,0:T(8,128)S(1)}, u32[]{:S(2)}, u32[]{:S(2)}) %collective-permute-start.13) | collective-permute-done | bytes 20512 | tf_op jit(solution)/shard_map/ppermute | solution.py:490
  45.3 2.3 %diagonal_sums.1 = (f32[5,128]{1,0:T(8,128)}, f32[1344,128]{1,0:T(8,128)S(1)}, f32[24,128]{1,0:T(8,128)S(1)}, f32[22,128]{1,0:T(8,128)S(1)}) custom-call(bf16[5,1312,128]{2,1,0:T(8,128)(2,1)S(1)} %strips.5.mid_ref.refs_2_.rest_2_, f32[40,128]{1,0:T(8,128)S(1)} %add.48.sums_ref, f32[40,128]{1,0:T(8,128)S(1)} %get-tuple-element.144.keep_ref, ...), custom_call_target="tpu_custom_call" | custom-call | tf_op jit(solution)/shard_map/diagonal_sums/pallas_call | solution.py:626
  47.6 0.1 collective-permute-start.14
  47.7 1.5 %observed.4.rest_7_ = f32[25,320,128]{2,1,0:T(8,128)S(1)} custom-call(bf16[4,1312,128]{2,1,0:T(8,128)(2,1)S(1)} %strips.7.refs_0_.rest_0_, bf16[1,1312,128]{2,1,0:T(8,128)(2,1)S(1)} %strips.8.refs_1_.rest_1_, bf16[5,1312,128]{2,1,0:T(8,128)(2,1)S(1)} %strips.5.mid_ref.refs_2_.rest_2_, bf16[4,1312,128]{2,1,0:T(8,128)(2,1)S(1)} %strips.6.refs_3_.rest_3_, ...), custom_call_target="tpu_custom_call" | custom-call | tf_op jit(solution)/shard_map/observed/pallas_call | solution.py:651
  49.2 1.6 %collective-permute-start.15 = (f32[22,128]{1,0:T(8,128)S(1)}, f32[22,128]{1,0:T(8,128)S(1)}, u32[]{:S(2)}, u32[]{:S(2)}) collective-permute-start(f32[22,128]{1,0:T(8,128)S(1)} %add.49), channel_id=1, source_target_pairs={{0,8},{4,12},{8,0},{12,4},{16,24},{20,28},{24,16},{28,20},{1,9},{5... | collective-permute-start | bytes 33800 | tf_op jit(solution)/shard_map/ppermute | solution.py:490
  50.7 1.5 %observed.6.rest_9_ = f32[25,320,128]{2,1,0:T(8,128)S(1)} custom-call(bf16[4,1312,128]{2,1,0:T(8,128)(2,1)S(1)} %strips.7.refs_0_.rest_0_, bf16[1,1312,128]{2,1,0:T(8,128)(2,1)S(1)} %strips.8.refs_1_.rest_1_, bf16[5,1312,128]{2,1,0:T(8,128)(2,1)S(1)} %strips.5.mid_ref.refs_2_.rest_2_, bf16[4,1312,128]{2,1,0:T(8,128)(2,1)S(1)} %strips.6.refs_3_.rest_3_, ...), custom_call_target="tpu_custom_call" | custom-call | tf_op jit(solution)/shard_map/observed/pallas_call | solution.py:651
  52.2 1.5 %observed.5.rest_8_ = f32[25,320,128]{2,1,0:T(8,128)S(1)} custom-call(bf16[4,1312,128]{2,1,0:T(8,128)(2,1)S(1)} %strips.7.refs_0_.rest_0_, bf16[1,1312,128]{2,1,0:T(8,128)(2,1)S(1)} %strips.8.refs_1_.rest_1_, bf16[5,1312,128]{2,1,0:T(8,128)(2,1)S(1)} %strips.5.mid_ref.refs_2_.rest_2_, bf16[4,1312,128]{2,1,0:T(8,128)(2,1)S(1)} %strips.6.refs_3_.rest_3_, ...), custom_call_target="tpu_custom_call" | custom-call | tf_op jit(solution)/shard_map/observed/pallas_call | solution.py:651
  53.7 0.0 collective-permute-done.15
  53.7 1.4 %collective-permute-start.16 = (f32[22,128]{1,0:T(8,128)S(1)}, f32[22,128]{1,0:T(8,128)S(1)}, u32[]{:S(2)}, u32[]{:S(2)}) collective-permute-start(f32[22,128]{1,0:T(8,128)S(1)} %add.50), channel_id=1, source_target_pairs={{0,16},{4,20},{8,24},{12,28},{16,0},{20,4},{24,8},{28,12},{1,17},{... | collective-permute-start | bytes 33800 | tf_op jit(solution)/shard_map/ppermute | solution.py:490
  55.1 1.5 %observed.7.rest_10_ = f32[25,320,128]{2,1,0:T(8,128)S(1)} custom-call(bf16[4,1312,128]{2,1,0:T(8,128)(2,1)S(1)} %strips.7.refs_0_.rest_0_, bf16[1,1312,128]{2,1,0:T(8,128)(2,1)S(1)} %strips.8.refs_1_.rest_1_, bf16[5,1312,128]{2,1,0:T(8,128)(2,1)S(1)} %strips.5.mid_ref.refs_2_.rest_2_, bf16[4,1312,128]{2,1,0:T(8,128)(2,1)S(1)} %strips.6.refs_3_.rest_3_, ...), custom_call_target="tpu_custom_call" | custom-call | tf_op jit(solution)/shard_map/observed/pallas_call | solution.py:651
  56.6 0.8 %collective-permute-done.16 = f32[22,128]{1,0:T(8,128)S(1)} collective-permute-done((f32[22,128]{1,0:T(8,128)S(1)}, f32[22,128]{1,0:T(8,128)S(1)}, u32[]{:S(2)}, u32[]{:S(2)}) %collective-permute-start.16) | collective-permute-done | bytes 11296 | tf_op jit(solution)/shard_map/ppermute | solution.py:490
  57.5 11.5 %score.1 = f32[1280,640]{1,0:T(8,128)} custom-call(bf16[4,1312,128]{2,1,0:T(8,128)(2,1)S(1)} %strips.7.refs_0_.rest_0_, bf16[1,1312,128]{2,1,0:T(8,128)(2,1)S(1)} %strips.8.refs_1_.rest_1_, bf16[5,1312,128]{2,1,0:T(8,128)(2,1)S(1)} %strips.5.mid_ref.refs_2_.rest_2_, bf16[4,1312,128]{2,1,0:T(8,128)(2,1)S(1)} %strips.6.refs_3_.rest_3_, ...), custom_call_target="tpu_custom_call" | custom-call | tf_op jit(solution)/shard_map/score/pallas_call | solution.py:678
  (14 shorter events, 0.1 us)
Async XLA Ops:
  3.6 5.0 %collective-permute-start = (f32[40,128]{1,0:T(8,128)S(1)}, f32[40,128]{1,0:T(8,128)S(1)}, u32[]{:S(2)}, u32[]{:S(2)}) collective-permute-start(f32[40,128]{1,0:T(8,128)S(1)} %get-tuple-element.96), channel_id=1, source_target_pairs={{0,1},{1,0},{2,3},{3,2},{4,5},{5,4},{6,7},{7,6},{8,9},{9,8},{10,11... | collective-permute-start | bytes 61448 | tf_op jit(solution)/shard_map/ppermute | solution.py:490
  6.7 6.8 %collective-permute-start.2 = (f32[16,640]{1,0:T(8,128)S(1)}, f32[16,640]{1,0:T(8,128)S(1)}, u32[]{:S(2)}, u32[]{:S(2)}) collective-permute-start(f32[16,640]{1,0:T(8,128)S(1)} %get-tuple-element.99), channel_id=1, source_target_pairs={{0,1},{1,2},{2,3},{4,5},{5,6},{6,7},{8,9},{9,10},{10,11},{12,13},{... | collective-permute-start | bytes 122888 | tf_op jit(solution)/shard_map/ppermute | solution.py:503
  8.7 4.8 %collective-permute-start.1 = (f32[40,128]{1,0:T(8,128)S(1)}, f32[40,128]{1,0:T(8,128)S(1)}, u32[]{:S(2)}, u32[]{:S(2)}) collective-permute-start(f32[40,128]{1,0:T(8,128)S(1)} %add.39), channel_id=1, source_target_pairs={{0,2},{1,3},{2,0},{3,1},{4,6},{5,7},{6,4},{7,5},{8,10},{9,11},{10,... | collective-permute-start | bytes 61448 | tf_op jit(solution)/shard_map/ppermute | solution.py:490
  11.7 5.9 %collective-permute-start.4 = (f32[16,640]{1,0:T(8,128)S(1)}, f32[16,640]{1,0:T(8,128)S(1)}, u32[]{:S(2)}, u32[]{:S(2)}) collective-permute-start(f32[16,640]{1,0:T(8,128)S(1)} %get-tuple-element.101), channel_id=1, source_target_pairs={{1,0},{2,1},{3,2},{5,4},{6,5},{7,6},{9,8},{10,9},{11,10},{13,12},{... | collective-permute-start | bytes 122888 | tf_op jit(solution)/shard_map/ppermute | solution.py:503
  13.5 1.3 %collective-permute-start.3 = (f32[40,128]{1,0:T(8,128)S(1)}, f32[40,128]{1,0:T(8,128)S(1)}, u32[]{:S(2)}, u32[]{:S(2)}) collective-permute-start(f32[40,128]{1,0:T(8,128)S(1)} %add.40), channel_id=1, source_target_pairs={{0,4},{4,0},{8,12},{12,8},{16,20},{20,16},{24,28},{28,24},{1,5},{5... | collective-permute-start | bytes 61448 | tf_op jit(solution)/shard_map/ppermute | solution.py:490
  17.6 3.8 %collective-permute-start.5 = (f32[40,128]{1,0:T(8,128)S(1)}, f32[40,128]{1,0:T(8,128)S(1)}, u32[]{:S(2)}, u32[]{:S(2)}) collective-permute-start(f32[40,128]{1,0:T(8,128)S(1)} %add.41), channel_id=1, source_target_pairs={{0,8},{4,12},{8,0},{12,4},{16,24},{20,28},{24,16},{28,20},{1,9},{5... | collective-permute-start | bytes 61448 | tf_op jit(solution)/shard_map/ppermute | solution.py:490
  19.4 11.5 %collective-permute-start.8 = (f32[8,1312]{1,0:T(8,128)S(1)}, f32[8,1312]{1,0:T(8,128)S(1)}, u32[]{:S(2)}, u32[]{:S(2)}) collective-permute-start(f32[8,1312]{1,0:T(8,128)S(1)} %get-tuple-element.114), channel_id=1, source_target_pairs={{4,0},{8,4},{12,8},{16,12},{20,16},{24,20},{28,24},{5,1},{9,5},{13... | collective-permute-start | bytes 125960 | tf_op jit(solution)/shard_map/ppermute | solution.py:503
  21.4 3.8 %collective-permute-start.6 = (f32[40,128]{1,0:T(8,128)S(1)}, f32[40,128]{1,0:T(8,128)S(1)}, u32[]{:S(2)}, u32[]{:S(2)}) collective-permute-start(f32[40,128]{1,0:T(8,128)S(1)} %add.42), channel_id=1, source_target_pairs={{0,16},{4,20},{8,24},{12,28},{16,0},{20,4},{24,8},{28,12},{1,17},{... | collective-permute-start | bytes 61448 | tf_op jit(solution)/shard_map/ppermute | solution.py:490
  27.1 3.8 %collective-permute-start.7 = (f32[40,128]{1,0:T(8,128)S(1)}, f32[40,128]{1,0:T(8,128)S(1)}, u32[]{:S(2)}, u32[]{:S(2)}) collective-permute-start(f32[40,128]{1,0:T(8,128)S(1)} %get-tuple-element.113), channel_id=1, source_target_pairs={{0,1},{1,0},{2,3},{3,2},{4,5},{5,4},{6,7},{7,6},{8,9},{9,8},{10,11... | collective-permute-start | bytes 61448 | tf_op jit(solution)/shard_map/ppermute | solution.py:490
  28.6 9.0 %collective-permute-start.11 = (f32[8,1312]{1,0:T(8,128)S(1)}, f32[8,1312]{1,0:T(8,128)S(1)}, u32[]{:S(2)}, u32[]{:S(2)}) collective-permute-start(f32[8,1312]{1,0:T(8,128)S(1)} %get-tuple-element.128), channel_id=1, source_target_pairs={{0,4},{4,8},{8,12},{12,16},{16,20},{20,24},{24,28},{1,5},{5,9},{9,... | collective-permute-start | bytes 125960 | tf_op jit(solution)/shard_map/ppermute | solution.py:503
  30.9 4.7 %collective-permute-start.9 = (f32[40,128]{1,0:T(8,128)S(1)}, f32[40,128]{1,0:T(8,128)S(1)}, u32[]{:S(2)}, u32[]{:S(2)}) collective-permute-start(f32[40,128]{1,0:T(8,128)S(1)} %add.44), channel_id=1, source_target_pairs={{0,2},{1,3},{2,0},{3,1},{4,6},{5,7},{6,4},{7,5},{8,10},{9,11},{10,... | collective-permute-start | bytes 61448 | tf_op jit(solution)/shard_map/ppermute | solution.py:490
  35.7 1.9 %collective-permute-start.10 = (f32[40,128]{1,0:T(8,128)S(1)}, f32[40,128]{1,0:T(8,128)S(1)}, u32[]{:S(2)}, u32[]{:S(2)}) collective-permute-start(f32[40,128]{1,0:T(8,128)S(1)} %add.45), channel_id=1, source_target_pairs={{0,4},{4,0},{8,12},{12,8},{16,20},{20,16},{24,28},{28,24},{1,5},{5... | collective-permute-start | bytes 61448 | tf_op jit(solution)/shard_map/ppermute | solution.py:490
  37.6 3.9 %collective-permute-start.12 = (f32[40,128]{1,0:T(8,128)S(1)}, f32[40,128]{1,0:T(8,128)S(1)}, u32[]{:S(2)}, u32[]{:S(2)}) collective-permute-start(f32[40,128]{1,0:T(8,128)S(1)} %add.46), channel_id=1, source_target_pairs={{0,8},{4,12},{8,0},{12,4},{16,24},{20,28},{24,16},{28,20},{1,9},{5... | collective-permute-start | bytes 61448 | tf_op jit(solution)/shard_map/ppermute | solution.py:490
  41.5 3.8 %collective-permute-start.13 = (f32[40,128]{1,0:T(8,128)S(1)}, f32[40,128]{1,0:T(8,128)S(1)}, u32[]{:S(2)}, u32[]{:S(2)}) collective-permute-start(f32[40,128]{1,0:T(8,128)S(1)} %add.47), channel_id=1, source_target_pairs={{0,16},{4,20},{8,24},{12,28},{16,0},{20,4},{24,8},{28,12},{1,17},{... | collective-permute-start | bytes 61448 | tf_op jit(solution)/shard_map/ppermute | solution.py:490
  47.6 1.6 %collective-permute-start.14 = (f32[22,128]{1,0:T(8,128)S(1)}, f32[22,128]{1,0:T(8,128)S(1)}, u32[]{:S(2)}, u32[]{:S(2)}) collective-permute-start(f32[22,128]{1,0:T(8,128)S(1)} %get-tuple-element.153), channel_id=1, source_target_pairs={{0,4},{4,0},{8,12},{12,8},{16,20},{20,16},{24,28},{28,24},{1,5},{5... | collective-permute-start | bytes 33800 | tf_op jit(solution)/shard_map/ppermute | solution.py:490
  49.2 4.5 %collective-permute-start.15 = (f32[22,128]{1,0:T(8,128)S(1)}, f32[22,128]{1,0:T(8,128)S(1)}, u32[]{:S(2)}, u32[]{:S(2)}) collective-permute-start(f32[22,128]{1,0:T(8,128)S(1)} %add.49), channel_id=1, source_target_pairs={{0,8},{4,12},{8,0},{12,4},{16,24},{20,28},{24,16},{28,20},{1,9},{5... | collective-permute-start | bytes 33800 | tf_op jit(solution)/shard_map/ppermute | solution.py:490
  53.7 3.8 %collective-permute-start.16 = (f32[22,128]{1,0:T(8,128)S(1)}, f32[22,128]{1,0:T(8,128)S(1)}, u32[]{:S(2)}, u32[]{:S(2)}) collective-permute-start(f32[22,128]{1,0:T(8,128)S(1)} %add.50), channel_id=1, source_target_pairs={{0,16},{4,20},{8,24},{12,28},{16,0},{20,4},{24,8},{28,12},{1,17},{... | collective-permute-start | bytes 33800 | tf_op jit(solution)/shard_map/ppermute | solution.py:490

commit v8 on v7

--- a/solution.py
+++ b/solution.py
@@ -9,7 +9,7 @@
 from jax.sharding import PartitionSpec as P
 
 RIM = 16
-STEP = 88
+STEP = 64
 SIDE = 8
 LANES = 128
 F32 = jnp.float32

time: 69.3 us -> 69.6 us (level)
  no operation moved by 1% of the time
where the time goes in v8:
time: 69.6 us; the launch traced here: 69.4 us
  Pallas kernels  32.3 us (46%)
  starting transfers between devices  23.3 us (33%)
  waiting for transfers between devices  12.7 us (18%)
  between operations  1.01 us (1%)
    ppermute x13, starting transfers between devices, total(): came = lax.ppermute(x, axis, pairs)  17.5 us
    pallas_call x1, Pallas kernels, on_device(): pl.pallas_call(functools.partial(score_kernel, nd, nb, chunk, STEP), out_...  11.6 us
    ppermute x13, waiting for transfers between devices, total(): came = lax.ppermute(x, axis, pairs)  9.8 us
    pallas_call x5, Pallas kernels, run(): pl.pallas_call(functools.partial(strip_kernel, nd, nb, first, count), out...  7.1 us
    pallas_call x4, Pallas kernels, run(): pl.pallas_call(functools.partial(observed_kernel, nd, nb, chunk, STEP, c...  6.06 us
    ppermute x4, starting transfers between devices, shifted(): lax.ppermute(x, axis, pairs if step > 0 else [(j, i) for i, j in pairs])  5.79 us
    pallas_call x1, Pallas kernels, on_device(): pl.pallas_call(functools.partial(first_kernel, nd, nb), out_shape=(shape(...  2.98 us
    ppermute x4, waiting for transfers between devices, shifted(): lax.ppermute(x, axis, pairs if step > 0 else [(j, i) for i, j in pairs])  2.86 us
  transfers between devices with their start and end apart: 17, of which 10 were waited for; matrix products, arithmetic and copies ran while one was open for 0% of the time, Pallas kernels for 22%

profile of v8, /device:TPU:0, one launch (start us, length us, event | category | flops | bytes accessed | tf_op | source)
XLA Modules:
  0.0 69.4 jit_solution(13158830653866492799)
XLA Ops:
  0.6 3.0 %first_sums.1 = (bf16[1280,640]{1,0:T(8,128)(2,1)S(1)}, f32[40,128]{1,0:T(8,128)S(1)}, f32[40,128]{1,0:T(8,128)S(1)}, f32[16,640]{1,0:T(8,128)S(1)}, f32[16,640]{1,0:T(8,128)S(1)}) custom-call(s32[2]{0:T(128)} %bounds_hbm.1, bf16[1280,640]{1,0:T(8,128)(2,1)} %x_hbm.1, s32[1,128]{1,0:T(1,128)} %bitcast.2), custom_call_target="tpu_custom_call" | custom-call | tf_op jit(solution)/shard_map/first_sums/pallas_call | solution.py:518
  3.6 3.1 %collective-permute-start = (f32[40,128]{1,0:T(8,128)S(1)}, f32[40,128]{1,0:T(8,128)S(1)}, u32[]{:S(2)}, u32[]{:S(2)}) collective-permute-start(f32[40,128]{1,0:T(8,128)S(1)} %get-tuple-element.96), channel_id=1, source_target_pairs={{0,1},{1,0},{2,3},{3,2},{4,5},{5,4},{6,7},{7,6},{8,9},{9,8},{10,11... | collective-permute-start | bytes 61448 | tf_op jit(solution)/shard_map/ppermute | solution.py:490
  6.7 1.9 %collective-permute-start.2 = (f32[16,640]{1,0:T(8,128)S(1)}, f32[16,640]{1,0:T(8,128)S(1)}, u32[]{:S(2)}, u32[]{:S(2)}) collective-permute-start(f32[16,640]{1,0:T(8,128)S(1)} %get-tuple-element.99), channel_id=1, source_target_pairs={{0,1},{1,2},{2,3},{4,5},{5,6},{6,7},{8,9},{9,10},{10,11},{12,13},{... | collective-permute-start | bytes 122888 | tf_op jit(solution)/shard_map/ppermute | solution.py:503
  8.6 0.0 collective-permute-done
  8.7 3.1 %collective-permute-start.1 = (f32[40,128]{1,0:T(8,128)S(1)}, f32[40,128]{1,0:T(8,128)S(1)}, u32[]{:S(2)}, u32[]{:S(2)}) collective-permute-start(f32[40,128]{1,0:T(8,128)S(1)} %add.39), channel_id=1, source_target_pairs={{0,2},{1,3},{2,0},{3,1},{4,6},{5,7},{6,4},{7,5},{8,10},{9,11},{10,... | collective-permute-start | bytes 61448 | tf_op jit(solution)/shard_map/ppermute | solution.py:490
  11.7 1.3 %collective-permute-start.4 = (f32[16,640]{1,0:T(8,128)S(1)}, f32[16,640]{1,0:T(8,128)S(1)}, u32[]{:S(2)}, u32[]{:S(2)}) collective-permute-start(f32[16,640]{1,0:T(8,128)S(1)} %get-tuple-element.101), channel_id=1, source_target_pairs={{1,0},{2,1},{3,2},{5,4},{6,5},{7,6},{9,8},{10,9},{11,10},{13,12},{... | collective-permute-start | bytes 122888 | tf_op jit(solution)/shard_map/ppermute | solution.py:503
  13.0 0.5 collective-permute-done.1
  13.5 0.0 collective-permute-done.2.top_ref.left_ref.right_ref
  13.5 0.1 collective-permute-start.3
  13.6 1.2 %collective-permute-done.3 = f32[40,128]{1,0:T(8,128)S(1)} collective-permute-done((f32[40,128]{1,0:T(8,128)S(1)}, f32[40,128]{1,0:T(8,128)S(1)}, u32[]{:S(2)}, u32[]{:S(2)}) %collective-permute-start.3) | collective-permute-done | bytes 20512 | tf_op jit(solution)/shard_map/ppermute | solution.py:490
  14.8 2.9 %collective-permute-done.4.bottom_ref = f32[16,640]{1,0:T(8,128)S(1)} collective-permute-done((f32[16,640]{1,0:T(8,128)S(1)}, f32[16,640]{1,0:T(8,128)S(1)}, u32[]{:S(2)}, u32[]{:S(2)}) %collective-permute-start.4) | collective-permute-done | bytes 40992 | tf_op jit(solution)/shard_map/ppermute | solution.py:503
  17.6 1.5 %collective-permute-start.5 = (f32[40,128]{1,0:T(8,128)S(1)}, f32[40,128]{1,0:T(8,128)S(1)}, u32[]{:S(2)}, u32[]{:S(2)}) collective-permute-start(f32[40,128]{1,0:T(8,128)S(1)} %add.41), channel_id=1, source_target_pairs={{0,8},{4,12},{8,0},{12,4},{16,24},{20,28},{24,16},{28,20},{1,9},{5... | collective-permute-start | bytes 61448 | tf_op jit(solution)/shard_map/ppermute | solution.py:490
  19.1 0.3 sides.1
  19.4 1.3 %collective-permute-start.8 = (f32[8,1312]{1,0:T(8,128)S(1)}, f32[8,1312]{1,0:T(8,128)S(1)}, u32[]{:S(2)}, u32[]{:S(2)}) collective-permute-start(f32[8,1312]{1,0:T(8,128)S(1)} %get-tuple-element.114), channel_id=1, source_target_pairs={{4,0},{8,4},{12,8},{16,12},{20,16},{24,20},{28,24},{5,1},{9,5},{13... | collective-permute-start | bytes 125960 | tf_op jit(solution)/shard_map/ppermute | solution.py:503
  20.7 0.7 %collective-permute-done.5 = f32[40,128]{1,0:T(8,128)S(1)} collective-permute-done((f32[40,128]{1,0:T(8,128)S(1)}, f32[40,128]{1,0:T(8,128)S(1)}, u32[]{:S(2)}, u32[]{:S(2)}) %collective-permute-start.5) | collective-permute-done | bytes 20512 | tf_op jit(solution)/shard_map/ppermute | solution.py:490
  21.4 1.5 %collective-permute-start.6 = (f32[40,128]{1,0:T(8,128)S(1)}, f32[40,128]{1,0:T(8,128)S(1)}, u32[]{:S(2)}, u32[]{:S(2)}) collective-permute-start(f32[40,128]{1,0:T(8,128)S(1)} %add.42), channel_id=1, source_target_pairs={{0,16},{4,20},{8,24},{12,28},{16,0},{20,4},{24,8},{28,12},{1,17},{... | collective-permute-start | bytes 61448 | tf_op jit(solution)/shard_map/ppermute | solution.py:490
  22.9 2.3 %collective-permute-done.6 = f32[40,128]{1,0:T(8,128)S(1)} collective-permute-done((f32[40,128]{1,0:T(8,128)S(1)}, f32[40,128]{1,0:T(8,128)S(1)}, u32[]{:S(2)}, u32[]{:S(2)}) %collective-permute-start.6) | collective-permute-done | bytes 20512 | tf_op jit(solution)/shard_map/ppermute | solution.py:490
  25.2 1.9 %second_sums.1 = (f32[40,128]{1,0:T(8,128)S(1)}, f32[40,128]{1,0:T(8,128)S(1)}) custom-call(bf16[1280,640]{1,0:T(8,128)(2,1)S(1)} %get-tuple-element.138.w_ref, f32[40,128]{1,0:T(8,128)S(1)} %add.43.sums_ref, f32[40,128]{1,0:T(8,128)S(1)} %get-tuple-element.144.keep_ref), custom_call_target="tpu_custom_call" | custom-call | tf_op jit(solution)/shard_map/second_sums/pallas_call | solution.py:560
  27.1 1.4 %collective-permute-start.7 = (f32[40,128]{1,0:T(8,128)S(1)}, f32[40,128]{1,0:T(8,128)S(1)}, u32[]{:S(2)}, u32[]{:S(2)}) collective-permute-start(f32[40,128]{1,0:T(8,128)S(1)} %get-tuple-element.113), channel_id=1, source_target_pairs={{0,1},{1,0},{2,3},{3,2},{4,5},{5,4},{6,7},{7,6},{8,9},{9,8},{10,11... | collective-permute-start | bytes 61448 | tf_op jit(solution)/shard_map/ppermute | solution.py:490
  28.5 0.2 unstrip.1.rest_6_
  28.6 1.3 %collective-permute-start.11 = (f32[8,1312]{1,0:T(8,128)S(1)}, f32[8,1312]{1,0:T(8,128)S(1)}, u32[]{:S(2)}, u32[]{:S(2)}) collective-permute-start(f32[8,1312]{1,0:T(8,128)S(1)} %get-tuple-element.128), channel_id=1, source_target_pairs={{0,4},{4,8},{8,12},{12,16},{16,20},{20,24},{24,28},{1,5},{5,9},{9,... | collective-permute-start | bytes 125960 | tf_op jit(solution)/shard_map/ppermute | solution.py:503
  29.9 1.0 %collective-permute-done.7 = f32[40,128]{1,0:T(8,128)S(1)} collective-permute-done((f32[40,128]{1,0:T(8,128)S(1)}, f32[40,128]{1,0:T(8,128)S(1)}, u32[]{:S(2)}, u32[]{:S(2)}) %collective-permute-start.7) | collective-permute-done | bytes 20512 | tf_op jit(solution)/shard_map/ppermute | solution.py:490
  30.9 0.0 collective-permute-done.8.left_ref.right_ref
  30.9 0.5 collective-permute-start.9
  31.5 2.0 %strips.5.mid_ref.refs_2_.rest_2_ = bf16[5,1312,128]{2,1,0:T(8,128)(2,1)S(1)} custom-call(bf16[1280,640]{1,0:T(8,128)(2,1)S(1)} %get-tuple-element.138.w_ref, f32[16,640]{1,0:T(8,128)S(1)} %collective-permute-done.2.top_ref.left_ref.right_ref, f32[16,640]{1,0:T(8,128)S(1)} %collective-permute-done.4.bottom_ref, ...), custom_call_target="tpu_custom_call" | custom-call | tf_op jit(solution)/shard_map/strips/pallas_call | solution.py:577
  33.5 2.2 %collective-permute-done.9 = f32[40,128]{1,0:T(8,128)S(1)} collective-permute-done((f32[40,128]{1,0:T(8,128)S(1)}, f32[40,128]{1,0:T(8,128)S(1)}, u32[]{:S(2)}, u32[]{:S(2)}) %collective-permute-start.9) | collective-permute-done | bytes 20512 | tf_op jit(solution)/shard_map/ppermute | solution.py:490
  35.7 0.1 collective-permute-start.10
  35.8 1.8 %strips.6.refs_3_.rest_3_ = bf16[4,1312,128]{2,1,0:T(8,128)(2,1)S(1)} custom-call(bf16[1280,640]{1,0:T(8,128)(2,1)S(1)} %get-tuple-element.138.w_ref, f32[16,640]{1,0:T(8,128)S(1)} %collective-permute-done.2.top_ref.left_ref.right_ref, f32[16,640]{1,0:T(8,128)S(1)} %collective-permute-done.4.bottom_ref, ...), custom_call_target="tpu_custom_call" | custom-call | tf_op jit(solution)/shard_map/strips/pallas_call | solution.py:577
  37.6 0.0 collective-permute-done.10
  37.6 0.0 collective-permute-done.11.left_ref.right_ref
  37.6 1.6 %collective-permute-start.12 = (f32[40,128]{1,0:T(8,128)S(1)}, f32[40,128]{1,0:T(8,128)S(1)}, u32[]{:S(2)}, u32[]{:S(2)}) collective-permute-start(f32[40,128]{1,0:T(8,128)S(1)} %add.46), channel_id=1, source_target_pairs={{0,8},{4,12},{8,0},{12,4},{16,24},{20,28},{24,16},{28,20},{1,9},{5... | collective-permute-start | bytes 61448 | tf_op jit(solution)/shard_map/ppermute | solution.py:490
  39.2 1.8 %strips.7.refs_0_.rest_0_ = bf16[4,1312,128]{2,1,0:T(8,128)(2,1)S(1)} custom-call(bf16[1280,640]{1,0:T(8,128)(2,1)S(1)} %get-tuple-element.138.w_ref, f32[16,640]{1,0:T(8,128)S(1)} %collective-permute-done.2.top_ref.left_ref.right_ref, f32[16,640]{1,0:T(8,128)S(1)} %collective-permute-done.4.bottom_ref, ...), custom_call_target="tpu_custom_call" | custom-call | tf_op jit(solution)/shard_map/strips/pallas_call | solution.py:577
  41.0 0.5 collective-permute-done.12
  41.5 1.5 %collective-permute-start.13 = (f32[40,128]{1,0:T(8,128)S(1)}, f32[40,128]{1,0:T(8,128)S(1)}, u32[]{:S(2)}, u32[]{:S(2)}) collective-permute-start(f32[40,128]{1,0:T(8,128)S(1)} %add.47), channel_id=1, source_target_pairs={{0,16},{4,20},{8,24},{12,28},{16,0},{20,4},{24,8},{28,12},{1,17},{... | collective-permute-start | bytes 61448 | tf_op jit(solution)/shard_map/ppermute | solution.py:490
  43.0 0.8 %strips.8.refs_1_.rest_1_ = bf16[1,1312,128]{2,1,0:T(8,128)(2,1)S(1)} custom-call(bf16[1280,640]{1,0:T(8,128)(2,1)S(1)} %get-tuple-element.138.w_ref, f32[16,640]{1,0:T(8,128)S(1)} %collective-permute-done.2.top_ref.left_ref.right_ref, f32[16,640]{1,0:T(8,128)S(1)} %collective-permute-done.4.bottom_ref, ...), custom_call_target="tpu_custom_call" | custom-call | tf_op jit(solution)/shard_map/strips/pallas_call | solution.py:577
  43.8 0.8 %strips.9.refs_4_.rest_4_ = bf16[1,1312,128]{2,1,0:T(8,128)(2,1)S(1)} custom-call(bf16[1280,640]{1,0:T(8,128)(2,1)S(1)} %get-tuple-element.138.w_ref, f32[16,640]{1,0:T(8,128)S(1)} %collective-permute-done.2.top_ref.left_ref.right_ref, f32[16,640]{1,0:T(8,128)S(1)} %collective-permute-done.4.bottom_ref, ...), custom_call_target="tpu_custom_call" | custom-call | tf_op jit(solution)/shard_map/strips/pallas_call | solution.py:577
  44.6 0.7 %collective-permute-done.13 = f32[40,128]{1,0:T(8,128)S(1)} collective-permute-done((f32[40,128]{1,0:T(8,128)S(1)}, f32[40,128]{1,0:T(8,128)S(1)}, u32[]{:S(2)}, u32[]{:S(2)}) %collective-permute-start.13) | collective-permute-done | bytes 20512 | tf_op jit(solution)/shard_map/ppermute | solution.py:490
  45.3 2.3 %diagonal_sums.1 = (f32[5,128]{1,0:T(8,128)}, f32[1344,128]{1,0:T(8,128)S(1)}, f32[24,128]{1,0:T(8,128)S(1)}, f32[22,128]{1,0:T(8,128)S(1)}) custom-call(bf16[5,1312,128]{2,1,0:T(8,128)(2,1)S(1)} %strips.5.mid_ref.refs_2_.rest_2_, f32[40,128]{1,0:T(8,128)S(1)} %add.48.sums_ref, f32[40,128]{1,0:T(8,128)S(1)} %get-tuple-element.144.keep_ref, ...), custom_call_target="tpu_custom_call" | custom-call | tf_op jit(solution)/shard_map/diagonal_sums/pallas_call | solution.py:626
  47.6 0.1 collective-permute-start.14
  47.7 1.5 %observed.4.rest_7_ = f32[25,320,128]{2,1,0:T(8,128)S(1)} custom-call(bf16[4,1312,128]{2,1,0:T(8,128)(2,1)S(1)} %strips.7.refs_0_.rest_0_, bf16[1,1312,128]{2,1,0:T(8,128)(2,1)S(1)} %strips.8.refs_1_.rest_1_, bf16[5,1312,128]{2,1,0:T(8,128)(2,1)S(1)} %strips.5.mid_ref.refs_2_.rest_2_, bf16[4,1312,128]{2,1,0:T(8,128)(2,1)S(1)} %strips.6.refs_3_.rest_3_, ...), custom_call_target="tpu_custom_call" | custom-call | tf_op jit(solution)/shard_map/observed/pallas_call | solution.py:651
  49.2 1.6 %collective-permute-start.15 = (f32[22,128]{1,0:T(8,128)S(1)}, f32[22,128]{1,0:T(8,128)S(1)}, u32[]{:S(2)}, u32[]{:S(2)}) collective-permute-start(f32[22,128]{1,0:T(8,128)S(1)} %add.49), channel_id=1, source_target_pairs={{0,8},{4,12},{8,0},{12,4},{16,24},{20,28},{24,16},{28,20},{1,9},{5... | collective-permute-start | bytes 33800 | tf_op jit(solution)/shard_map/ppermute | solution.py:490
  50.8 1.5 %observed.6.rest_9_ = f32[25,320,128]{2,1,0:T(8,128)S(1)} custom-call(bf16[4,1312,128]{2,1,0:T(8,128)(2,1)S(1)} %strips.7.refs_0_.rest_0_, bf16[1,1312,128]{2,1,0:T(8,128)(2,1)S(1)} %strips.8.refs_1_.rest_1_, bf16[5,1312,128]{2,1,0:T(8,128)(2,1)S(1)} %strips.5.mid_ref.refs_2_.rest_2_, bf16[4,1312,128]{2,1,0:T(8,128)(2,1)S(1)} %strips.6.refs_3_.rest_3_, ...), custom_call_target="tpu_custom_call" | custom-call | tf_op jit(solution)/shard_map/observed/pallas_call | solution.py:651
  52.3 1.5 %observed.5.rest_8_ = f32[25,320,128]{2,1,0:T(8,128)S(1)} custom-call(bf16[4,1312,128]{2,1,0:T(8,128)(2,1)S(1)} %strips.7.refs_0_.rest_0_, bf16[1,1312,128]{2,1,0:T(8,128)(2,1)S(1)} %strips.8.refs_1_.rest_1_, bf16[5,1312,128]{2,1,0:T(8,128)(2,1)S(1)} %strips.5.mid_ref.refs_2_.rest_2_, bf16[4,1312,128]{2,1,0:T(8,128)(2,1)S(1)} %strips.6.refs_3_.rest_3_, ...), custom_call_target="tpu_custom_call" | custom-call | tf_op jit(solution)/shard_map/observed/pallas_call | solution.py:651
  53.8 0.0 collective-permute-done.15
  53.8 1.4 %collective-permute-start.16 = (f32[22,128]{1,0:T(8,128)S(1)}, f32[22,128]{1,0:T(8,128)S(1)}, u32[]{:S(2)}, u32[]{:S(2)}) collective-permute-start(f32[22,128]{1,0:T(8,128)S(1)} %add.50), channel_id=1, source_target_pairs={{0,16},{4,20},{8,24},{12,28},{16,0},{20,4},{24,8},{28,12},{1,17},{... | collective-permute-start | bytes 33800 | tf_op jit(solution)/shard_map/ppermute | solution.py:490
  55.3 1.5 %observed.7.rest_10_ = f32[25,320,128]{2,1,0:T(8,128)S(1)} custom-call(bf16[4,1312,128]{2,1,0:T(8,128)(2,1)S(1)} %strips.7.refs_0_.rest_0_, bf16[1,1312,128]{2,1,0:T(8,128)(2,1)S(1)} %strips.8.refs_1_.rest_1_, bf16[5,1312,128]{2,1,0:T(8,128)(2,1)S(1)} %strips.5.mid_ref.refs_2_.rest_2_, bf16[4,1312,128]{2,1,0:T(8,128)(2,1)S(1)} %strips.6.refs_3_.rest_3_, ...), custom_call_target="tpu_custom_call" | custom-call | tf_op jit(solution)/shard_map/observed/pallas_call | solution.py:651
  56.8 0.8 %collective-permute-done.16 = f32[22,128]{1,0:T(8,128)S(1)} collective-permute-done((f32[22,128]{1,0:T(8,128)S(1)}, f32[22,128]{1,0:T(8,128)S(1)}, u32[]{:S(2)}, u32[]{:S(2)}) %collective-permute-start.16) | collective-permute-done | bytes 11296 | tf_op jit(solution)/shard_map/ppermute | solution.py:490
  57.6 11.6 %score.1 = f32[1280,640]{1,0:T(8,128)} custom-call(bf16[4,1312,128]{2,1,0:T(8,128)(2,1)S(1)} %strips.7.refs_0_.rest_0_, bf16[1,1312,128]{2,1,0:T(8,128)(2,1)S(1)} %strips.8.refs_1_.rest_1_, bf16[5,1312,128]{2,1,0:T(8,128)(2,1)S(1)} %strips.5.mid_ref.refs_2_.rest_2_, bf16[4,1312,128]{2,1,0:T(8,128)(2,1)S(1)} %strips.6.refs_3_.rest_3_, ...), custom_call_target="tpu_custom_call" | custom-call | tf_op jit(solution)/shard_map/score/pallas_call | solution.py:678
  (14 shorter events, 0.1 us)
Async XLA Ops:
  3.6 5.0 %collective-permute-start = (f32[40,128]{1,0:T(8,128)S(1)}, f32[40,128]{1,0:T(8,128)S(1)}, u32[]{:S(2)}, u32[]{:S(2)}) collective-permute-start(f32[40,128]{1,0:T(8,128)S(1)} %get-tuple-element.96), channel_id=1, source_target_pairs={{0,1},{1,0},{2,3},{3,2},{4,5},{5,4},{6,7},{7,6},{8,9},{9,8},{10,11... | collective-permute-start | bytes 61448 | tf_op jit(solution)/shard_map/ppermute | solution.py:490
  6.7 6.8 %collective-permute-start.2 = (f32[16,640]{1,0:T(8,128)S(1)}, f32[16,640]{1,0:T(8,128)S(1)}, u32[]{:S(2)}, u32[]{:S(2)}) collective-permute-start(f32[16,640]{1,0:T(8,128)S(1)} %get-tuple-element.99), channel_id=1, source_target_pairs={{0,1},{1,2},{2,3},{4,5},{5,6},{6,7},{8,9},{9,10},{10,11},{12,13},{... | collective-permute-start | bytes 122888 | tf_op jit(solution)/shard_map/ppermute | solution.py:503
  8.7 4.8 %collective-permute-start.1 = (f32[40,128]{1,0:T(8,128)S(1)}, f32[40,128]{1,0:T(8,128)S(1)}, u32[]{:S(2)}, u32[]{:S(2)}) collective-permute-start(f32[40,128]{1,0:T(8,128)S(1)} %add.39), channel_id=1, source_target_pairs={{0,2},{1,3},{2,0},{3,1},{4,6},{5,7},{6,4},{7,5},{8,10},{9,11},{10,... | collective-permute-start | bytes 61448 | tf_op jit(solution)/shard_map/ppermute | solution.py:490
  11.7 5.9 %collective-permute-start.4 = (f32[16,640]{1,0:T(8,128)S(1)}, f32[16,640]{1,0:T(8,128)S(1)}, u32[]{:S(2)}, u32[]{:S(2)}) collective-permute-start(f32[16,640]{1,0:T(8,128)S(1)} %get-tuple-element.101), channel_id=1, source_target_pairs={{1,0},{2,1},{3,2},{5,4},{6,5},{7,6},{9,8},{10,9},{11,10},{13,12},{... | collective-permute-start | bytes 122888 | tf_op jit(solution)/shard_map/ppermute | solution.py:503
  13.5 1.3 %collective-permute-start.3 = (f32[40,128]{1,0:T(8,128)S(1)}, f32[40,128]{1,0:T(8,128)S(1)}, u32[]{:S(2)}, u32[]{:S(2)}) collective-permute-start(f32[40,128]{1,0:T(8,128)S(1)} %add.40), channel_id=1, source_target_pairs={{0,4},{4,0},{8,12},{12,8},{16,20},{20,16},{24,28},{28,24},{1,5},{5... | collective-permute-start | bytes 61448 | tf_op jit(solution)/shard_map/ppermute | solution.py:490
  17.6 3.8 %collective-permute-start.5 = (f32[40,128]{1,0:T(8,128)S(1)}, f32[40,128]{1,0:T(8,128)S(1)}, u32[]{:S(2)}, u32[]{:S(2)}) collective-permute-start(f32[40,128]{1,0:T(8,128)S(1)} %add.41), channel_id=1, source_target_pairs={{0,8},{4,12},{8,0},{12,4},{16,24},{20,28},{24,16},{28,20},{1,9},{5... | collective-permute-start | bytes 61448 | tf_op jit(solution)/shard_map/ppermute | solution.py:490
  19.4 11.5 %collective-permute-start.8 = (f32[8,1312]{1,0:T(8,128)S(1)}, f32[8,1312]{1,0:T(8,128)S(1)}, u32[]{:S(2)}, u32[]{:S(2)}) collective-permute-start(f32[8,1312]{1,0:T(8,128)S(1)} %get-tuple-element.114), channel_id=1, source_target_pairs={{4,0},{8,4},{12,8},{16,12},{20,16},{24,20},{28,24},{5,1},{9,5},{13... | collective-permute-start | bytes 125960 | tf_op jit(solution)/shard_map/ppermute | solution.py:503
  21.4 3.8 %collective-permute-start.6 = (f32[40,128]{1,0:T(8,128)S(1)}, f32[40,128]{1,0:T(8,128)S(1)}, u32[]{:S(2)}, u32[]{:S(2)}) collective-permute-start(f32[40,128]{1,0:T(8,128)S(1)} %add.42), channel_id=1, source_target_pairs={{0,16},{4,20},{8,24},{12,28},{16,0},{20,4},{24,8},{28,12},{1,17},{... | collective-permute-start | bytes 61448 | tf_op jit(solution)/shard_map/ppermute | solution.py:490
  27.1 3.8 %collective-permute-start.7 = (f32[40,128]{1,0:T(8,128)S(1)}, f32[40,128]{1,0:T(8,128)S(1)}, u32[]{:S(2)}, u32[]{:S(2)}) collective-permute-start(f32[40,128]{1,0:T(8,128)S(1)} %get-tuple-element.113), channel_id=1, source_target_pairs={{0,1},{1,0},{2,3},{3,2},{4,5},{5,4},{6,7},{7,6},{8,9},{9,8},{10,11... | collective-permute-start | bytes 61448 | tf_op jit(solution)/shard_map/ppermute | solution.py:490
  28.6 9.0 %collective-permute-start.11 = (f32[8,1312]{1,0:T(8,128)S(1)}, f32[8,1312]{1,0:T(8,128)S(1)}, u32[]{:S(2)}, u32[]{:S(2)}) collective-permute-start(f32[8,1312]{1,0:T(8,128)S(1)} %get-tuple-element.128), channel_id=1, source_target_pairs={{0,4},{4,8},{8,12},{12,16},{16,20},{20,24},{24,28},{1,5},{5,9},{9,... | collective-permute-start | bytes 125960 | tf_op jit(solution)/shard_map/ppermute | solution.py:503
  30.9 4.7 %collective-permute-start.9 = (f32[40,128]{1,0:T(8,128)S(1)}, f32[40,128]{1,0:T(8,128)S(1)}, u32[]{:S(2)}, u32[]{:S(2)}) collective-permute-start(f32[40,128]{1,0:T(8,128)S(1)} %add.44), channel_id=1, source_target_pairs={{0,2},{1,3},{2,0},{3,1},{4,6},{5,7},{6,4},{7,5},{8,10},{9,11},{10,... | collective-permute-start | bytes 61448 | tf_op jit(solution)/shard_map/ppermute | solution.py:490
  35.7 1.9 %collective-permute-start.10 = (f32[40,128]{1,0:T(8,128)S(1)}, f32[40,128]{1,0:T(8,128)S(1)}, u32[]{:S(2)}, u32[]{:S(2)}) collective-permute-start(f32[40,128]{1,0:T(8,128)S(1)} %add.45), channel_id=1, source_target_pairs={{0,4},{4,0},{8,12},{12,8},{16,20},{20,16},{24,28},{28,24},{1,5},{5... | collective-permute-start | bytes 61448 | tf_op jit(solution)/shard_map/ppermute | solution.py:490
  37.6 3.9 %collective-permute-start.12 = (f32[40,128]{1,0:T(8,128)S(1)}, f32[40,128]{1,0:T(8,128)S(1)}, u32[]{:S(2)}, u32[]{:S(2)}) collective-permute-start(f32[40,128]{1,0:T(8,128)S(1)} %add.46), channel_id=1, source_target_pairs={{0,8},{4,12},{8,0},{12,4},{16,24},{20,28},{24,16},{28,20},{1,9},{5... | collective-permute-start | bytes 61448 | tf_op jit(solution)/shard_map/ppermute | solution.py:490
  41.5 3.8 %collective-permute-start.13 = (f32[40,128]{1,0:T(8,128)S(1)}, f32[40,128]{1,0:T(8,128)S(1)}, u32[]{:S(2)}, u32[]{:S(2)}) collective-permute-start(f32[40,128]{1,0:T(8,128)S(1)} %add.47), channel_id=1, source_target_pairs={{0,16},{4,20},{8,24},{12,28},{16,0},{20,4},{24,8},{28,12},{1,17},{... | collective-permute-start | bytes 61448 | tf_op jit(solution)/shard_map/ppermute | solution.py:490
  47.6 1.6 %collective-permute-start.14 = (f32[22,128]{1,0:T(8,128)S(1)}, f32[22,128]{1,0:T(8,128)S(1)}, u32[]{:S(2)}, u32[]{:S(2)}) collective-permute-start(f32[22,128]{1,0:T(8,128)S(1)} %get-tuple-element.153), channel_id=1, source_target_pairs={{0,4},{4,0},{8,12},{12,8},{16,20},{20,16},{24,28},{28,24},{1,5},{5... | collective-permute-start | bytes 33800 | tf_op jit(solution)/shard_map/ppermute | solution.py:490
  49.2 4.6 %collective-permute-start.15 = (f32[22,128]{1,0:T(8,128)S(1)}, f32[22,128]{1,0:T(8,128)S(1)}, u32[]{:S(2)}, u32[]{:S(2)}) collective-permute-start(f32[22,128]{1,0:T(8,128)S(1)} %add.49), channel_id=1, source_target_pairs={{0,8},{4,12},{8,0},{12,4},{16,24},{20,28},{24,16},{28,20},{1,9},{5... | collective-permute-start | bytes 33800 | tf_op jit(solution)/shard_map/ppermute | solution.py:490
  53.8 3.8 %collective-permute-start.16 = (f32[22,128]{1,0:T(8,128)S(1)}, f32[22,128]{1,0:T(8,128)S(1)}, u32[]{:S(2)}, u32[]{:S(2)}) collective-permute-start(f32[22,128]{1,0:T(8,128)S(1)} %add.50), channel_id=1, source_target_pairs={{0,16},{4,20},{8,24},{12,28},{16,0},{20,4},{24,8},{28,12},{1,17},{... | collective-permute-start | bytes 33800 | tf_op jit(solution)/shard_map/ppermute | solution.py:490
